TPU v7x, 32 devices: a whole 2x2x4 slice. The times are simulated.
32 devices in a mesh: grp: 2 (over y), dev: 8 (over z, x), layer: 2 (over core).
Axes of the slice: x: 2, y: 2, z: 4, core: 2. Of those that a mesh axis runs over, the one named last changes fastest.
Arguments:
- cols: int32 [64, 8], P('grp'), parts along dimension 0, may hold values from 0 to 32, as said below
- tiles: bfloat16 [64, 8, 128, 128], P(('grp', 'dev')), parts along dimension 0, may hold values from -0.16 to 0.5, as said below
Outputs:
- purified: bfloat16 [64, 8, 128, 128], P(('grp', 'dev')), parts along dimension 0
There are 2 independent parts, one for each index of `grp`. A program takes and returns all parts, laid end to end along the dimension named above; each array names one. Nothing has to cross between parts.
Inputs may be any that keep to these rules, and one draw needn't show every extreme that they name: `cols`: in block row i slot 0 holds i itself; the filled slots hold distinct block columns c with (c - i) mod 32 or (i - c) mod 32 at most 4; empty slots hold 32 and come after the filled ones; a row holds 5 to 8 filled slots, and some rows are full. `tiles`: blocks in empty slots are zero.
All inputs are finite; a program needn't handle non-finite values.
Results may differ from a plain program's by a relative error of at most 0.0086.
Values may be sent and summed in bfloat16 or wider, within the bound.
No kernel may reach another device: no remote copies, remote signals or barrier semaphores. Data moves between devices by JAX's collectives and lax.ppermute only.
A program may use at most 64 MiB of HBM per device.

v0:
```python
import jax
import jax.numpy as jnp
from jax import lax
from jax.sharding import PartitionSpec as P

ITERS = 2


def with_halo(block, sides, width):
    for axis, dim in sides:
        count = lax.axis_size(axis)
        forward = [(i, i + 1) for i in range(count - 1)]
        forward.append((count - 1, 0))
        backward = [(target, source) for source, target in forward]
        low = lax.ppermute(
            lax.slice_in_dim(block, block.shape[dim] - width, None, axis=dim), axis, forward
        )
        high = lax.ppermute(lax.slice_in_dim(block, 0, width, axis=dim), axis, backward)
        block = jnp.concatenate([low, block, high], axis=dim)
    return block


def swapped(value, axis, bit):
    return lax.ppermute(value, axis, [(i, i ^ 1 << bit) for i in range(lax.axis_size(axis))])


def per_device(cols, tiles):
    row_count = tiles.shape[0]
    slot_count = tiles.shape[1]
    band_half = slot_count // 2
    half_count = slot_count // 2
    total_rows = cols.shape[0]
    first_row = lax.axis_index("dev") * row_count
    ext_ids = (
        first_row - band_half + jnp.arange(row_count + 2 * band_half, dtype=jnp.int32)
    ) % total_rows
    ext_cols = jnp.take(cols, ext_ids, axis=0)
    own_cols = lax.dynamic_slice_in_dim(cols, first_row, row_count, 0)
    own_ids = first_row + jnp.arange(row_count, dtype=jnp.int32)
    offsets = jnp.clip((own_cols - own_ids[:, None] + band_half) % total_rows, 0, 2 * band_half)
    ext_index = jnp.arange(row_count, dtype=jnp.int32)[:, None] + offsets
    partner_cols = jnp.take(ext_cols, ext_index, axis=0)
    targets = own_cols < total_rows
    matches = (
        (partner_cols[:, :, None, :] == own_cols[:, None, :, None]) & targets[:, None, :, None]
    ).astype(jnp.bfloat16)
    layer_index = lax.axis_index("layer")
    counter = jnp.arange(half_count, dtype=jnp.int32)
    chosen = counter + layer_index * half_count
    current = tiles
    for iteration in range(ITERS):
        extended = with_halo(current, (("dev", 0),), band_half)

        def contract(left, picked, aligned):
            return jnp.einsum(
                "rmab,rmnbc->rnac",
                jnp.take(left, picked, axis=1),
                aligned,
                preferred_element_type=jnp.float32,
            )

        fetched = jnp.take(extended, jnp.take(ext_index, chosen, axis=1), axis=0)
        match = jnp.take(matches, chosen, axis=1)
        aligned = jnp.einsum(
            "rmnq,rmqab->rmnab", match, fetched, preferred_element_type=jnp.float32
        ).astype(jnp.bfloat16)
        square_part = contract(current, chosen, aligned)
        square_full = square_part + swapped(square_part, "layer", 0)
        square = square_full.astype(jnp.bfloat16)
        cube_part = contract(square, chosen, aligned)
        cube_term = cube_part + swapped(cube_part, "layer", 0)
        current = (3.0 * square.astype(jnp.float32) - 2.0 * cube_term).astype(jnp.bfloat16)
    return current


def solution(mesh):
    placed = (P("grp", None), P(("grp", "dev"), None, None, None))
    return jax.shard_map(
        per_device,
        mesh=mesh,
        in_specs=placed,
        out_specs=P(("grp", "dev"), None, None, None),
        check_vma=False,
    )
```

profile of v0, /device:TPU:0, one launch (start us, length us, event | category | flops | bytes accessed | tf_op | source)
XLA Modules:
  0.0 178.9 jit_solution(588229906052503185)
XLA Ops:
  0.0 6.0 %collective-permute-start.1 = (bf16[4,8,128,128]{3,2,1,0:T(8,128)(2,1)}, bf16[4,8,128,128]{3,2,1,0:T(8,128)(2,1)S(1)}, u32[]{:S(2)}, u32[]{:S(2)}) collective-permute-start(bf16[4,8,128,128]{3,2,1,0:T(8,128)(2,1)} %param.11), channel_id=1, source_target_pairs={{2,0},{4,2},{6,4},{8,6},{10,8},{12,10},{14,12},{0,14},{3,1},{5,3},... | collective-permute-start | bytes 3145736 | tf_op jit(solution)/shard_map/ppermute | solution.py:18
  6.1 0.8 broadcast_compare_fusion
  6.9 0.6 gather_fusion.3
  7.5 0.1 copy.26
  7.6 0.8 copy.24
  8.3 2.7 %gather_fusion.5 = bf16[4,4,128,128]{3,2,1,0:T(8,128)(2,1)} fusion(bf16[4,8,128,128]{3,2,1,0:T(8,128)(2,1)} %param.11, s32[1024]{0:T(1024)S(1)} %pad_clamp_fusion.1), kind=kCustom, calls=%fused_computation.3.clone | custom fusion | bytes 1048592 | tf_op jit(solution)/shard_map/jit(_take)/gather | solution.py:57
  11.0 0.1 copy.27
  11.1 0.1 copy.23
  11.3 0.1 reshape.162
  11.4 0.1 copy.28
  11.5 0.1 copy.30
  11.6 0.1 reshape.184
  11.7 0.6 gather_fusion
  12.3 0.6 gather_fusion.1
  13.0 0.1 and_convert_fusion
  13.1 0.6 gather_fusion.2
  13.7 35.1 %collective-permute-done.1 = bf16[4,8,128,128]{3,2,1,0:T(8,128)(2,1)S(1)} collective-permute-done((bf16[4,8,128,128]{3,2,1,0:T(8,128)(2,1)}, bf16[4,8,128,128]{3,2,1,0:T(8,128)(2,1)S(1)}, u32[]{:S(2)}, u32[]{:S(2)}) %collective-permute-start.1) | collective-permute-done | bytes 1048608 | tf_op jit(solution)/shard_map/ppermute | solution.py:18
  48.8 1.0 copy-done.2
  49.8 2.0 %pad_maximum_fusion = bf16[12,8,128,128]{3,2,1,0:T(8,128)(2,1)S(1)} fusion(bf16[4,8,128,128]{3,2,1,0:T(8,128)(2,1)} %copy-done.2, bf16[4,8,128,128]{3,2,1,0:T(8,128)(2,1)} %param.11, bf16[4,8,128,128]{3,2,1,0:T(8,128)(2,1)} %collective-permute-done), kind=kLoop, calls=%fused_computation.16 | loop fusion | flops 3145728 | bytes 6291456 | tf_op jit(solution)/shard_map/concatenate | solution.py:19
  51.8 3.0 %gather_fusion.4 = bf16[16,8,128,128]{3,2,1,0:T(8,128)(2,1)} fusion(bf16[12,8,128,128]{3,2,1,0:T(8,128)(2,1)S(1)} %pad_maximum_fusion, s32[1024]{0:T(1024)S(1)} %pad_clamp_fusion), kind=kCustom, calls=%fused_computation.2.clone | custom fusion | bytes 8388672 | tf_op jit(solution)/shard_map/jit(_take)/gather | solution.py:62
  54.8 6.8 %fusion.8 = bf16[4,4,8,128,128]{4,2,3,1,0:T(8,128)(2,1)} fusion(bf16[4,4,8,128,128]{4,3,2,1,0:T(8,128)(2,1)} %bitcast.67, pred[4,4]{1,0:T(4,128)(4,1)S(1)} %copy.28, bf16[4,4,8,8]{3,2,1,0:T(8,128)(2,1)S(1)} %gather_fusion.2, pred[4]{0:T(512)(128)(4,1)S(1)} %compare_and_fusion.2), kind=kOutput, calls=%fused_computation.19 | convolution fusion | flops 37749760 | bytes 8390676 | tf_op jit(solution)/shard_map/rmnq,rmqab->rmnab/dot_general | solution.py:64
  61.7 7.6 %copy.33 = bf16[4,4,8,128,128]{3,4,1,2,0:T(8,128)(2,1)} copy(bf16[4,4,8,128,128]{4,2,3,1,0:T(8,128)(2,1)} %fusion.8) | data formatting | bytes 8388608 | tf_op jit(solution)/shard_map/convert_element_type | solution.py:66
  69.3 3.5 %convolution_bitcast_fusion.3 = f32[4,8,128,128]{2,3,1,0:T(8,128)S(1)} fusion(bf16[4,4,8,128,128]{3,4,1,2,0:T(8,128)(2,1)} %copy.33, bf16[4,4,128,128]{3,2,1,0:T(8,128)(2,1)S(1)} %copy-done.4, pred[4]{0:T(512)(128)(4,1)S(1)} %compare_and_fusion.2), kind=kOutput, calls=%fused_computation.29 | convolution fusion | flops 537133056 | bytes 6815748 | tf_op jit(solution)/shard_map/rmab,rmnbc->rnac/dot_general | solution.py:55
  72.8 4.1 %collective-permute-done.2 = f32[4,8,128,128]{2,3,1,0:T(8,128)S(1)} collective-permute-done((f32[4,8,128,128]{2,3,1,0:T(8,128)S(1)}, f32[4,8,128,128]{2,3,1,0:T(8,128)S(1)}, u32[]{:S(2)}, u32[]{:S(2)}) %collective-permute-start.2) | collective-permute-done | bytes 2097184 | tf_op jit(solution)/shard_map/ppermute | solution.py:24
  77.0 0.3 add_convert_fusion.1
  77.3 0.6 gather_fusion.6
  78.0 3.5 %convolution_bitcast_fusion.2 = f32[4,8,128,128]{2,3,1,0:T(8,128)S(1)} fusion(bf16[4,4,8,128,128]{3,4,1,2,0:T(8,128)(2,1)} %copy.33, bf16[4,4,128,128]{2,3,1,0:T(8,128)(2,1)S(1)} %gather_fusion.6, pred[4]{0:T(512)(128)(4,1)S(1)} %compare_and_fusion.2), kind=kOutput, calls=%fused_computation.28 | convolution fusion | flops 537133056 | bytes 6815748 | tf_op jit(solution)/shard_map/rmab,rmnbc->rnac/dot_general | solution.py:55
  81.5 0.2 collective-permute-start.3
  81.7 4.0 %collective-permute-done.3 = f32[4,8,128,128]{2,3,1,0:T(8,128)S(1)} collective-permute-done((f32[4,8,128,128]{2,3,1,0:T(8,128)S(1)}, f32[4,8,128,128]{2,3,1,0:T(8,128)S(1)}, u32[]{:S(2)}, u32[]{:S(2)}) %collective-permute-start.3) | collective-permute-done | bytes 2097184 | tf_op jit(solution)/shard_map/ppermute | solution.py:24
  85.7 0.5 subtract_convert_fusion.1
  86.3 4.2 %collective-permute-start.5 = (bf16[4,8,128,128]{2,3,1,0:T(8,128)(2,1)S(1)}, bf16[4,8,128,128]{2,3,1,0:T(8,128)(2,1)S(1)}, u32[]{:S(2)}, u32[]{:S(2)}) collective-permute-start(bf16[4,8,128,128]{2,3,1,0:T(8,128)(2,1)S(1)} %subtract_convert_fusion.1), channel_id=1, source_target_pairs={{2,0},{4,2},{6,4},{8,6},{10,8},{12,10},{14,12},{0,14},{3,1},{5,3},... | collective-permute-start | bytes 3145736 | tf_op jit(solution)/shard_map/ppermute | solution.py:18
  90.5 1.4 gather_fusion.8
  91.9 42.1 %collective-permute-done.5 = bf16[4,8,128,128]{2,3,1,0:T(8,128)(2,1)S(1)} collective-permute-done((bf16[4,8,128,128]{2,3,1,0:T(8,128)(2,1)S(1)}, bf16[4,8,128,128]{2,3,1,0:T(8,128)(2,1)S(1)}, u32[]{:S(2)}, u32[]{:S(2)}) %collective-permute-start.5) | collective-permute-done | bytes 1048608 | tf_op jit(solution)/shard_map/ppermute | solution.py:18
  134.0 1.0 copy-done.3
  135.0 2.0 %pad_maximum_fusion.1 = bf16[12,8,128,128]{2,3,1,0:T(8,128)(2,1)S(1)} fusion(bf16[4,8,128,128]{2,3,1,0:T(8,128)(2,1)} %copy-done.3, bf16[4,8,128,128]{2,3,1,0:T(8,128)(2,1)} %copy-done, bf16[4,8,128,128]{2,3,1,0:T(8,128)(2,1)} %collective-permute-done.4), kind=kLoop, calls=%fused_computation.17 | loop fusion | flops 3145728 | bytes 6291456 | tf_op jit(solution)/shard_map/concatenate | solution.py:19
  137.0 3.0 %gather_fusion.7 = bf16[16,8,128,128]{2,3,1,0:T(8,128)(2,1)} fusion(bf16[12,8,128,128]{2,3,1,0:T(8,128)(2,1)S(1)} %pad_maximum_fusion.1, s32[1024]{0:T(1024)S(1)} %pad_clamp_fusion), kind=kCustom, calls=%fused_computation.4.clone | custom fusion | bytes 8388672 | tf_op jit(solution)/shard_map/jit(_take)/gather | solution.py:62
  140.1 7.5 %copy.38 = bf16[4,4,8,128,128]{4,2,3,1,0:T(8,128)(2,1)} copy(bf16[4,4,8,128,128]{3,4,2,1,0:T(8,128)(2,1)} %bitcast.66) | data formatting | bytes 8388608 | tf_op jit(solution)/shard_map/jit(_take)/gather | solution.py:62
  147.6 5.5 %fusion.5 = bf16[4,4,8,128,128]{4,2,3,1,0:T(8,128)(2,1)} fusion(bf16[4,4,8,128,128]{4,2,3,1,0:T(8,128)(2,1)} %copy.38, pred[4,4]{1,0:T(4,128)(4,1)S(1)} %copy.28, bf16[4,4,8,8]{3,2,1,0:T(8,128)(2,1)S(1)} %gather_fusion.2, pred[4]{0:T(512)(128)(4,1)S(1)} %compare_and_fusion.2), kind=kOutput, calls=%fused_computation.18 | convolution fusion | flops 37749760 | bytes 8390676 | tf_op jit(solution)/shard_map/rmnq,rmqab->rmnab/dot_general | solution.py:64
  153.0 7.5 %copy.40 = bf16[4,4,8,128,128]{3,4,1,2,0:T(8,128)(2,1)} copy(bf16[4,4,8,128,128]{4,2,3,1,0:T(8,128)(2,1)} %fusion.5) | data formatting | bytes 8388608 | tf_op jit(solution)/shard_map/convert_element_type | solution.py:66
  160.5 3.5 %convolution_bitcast_fusion.1 = f32[4,8,128,128]{2,3,1,0:T(8,128)S(1)} fusion(bf16[4,4,8,128,128]{3,4,1,2,0:T(8,128)(2,1)} %copy.40, bf16[4,4,128,128]{2,3,1,0:T(8,128)(2,1)S(1)} %copy-done.1, pred[4]{0:T(512)(128)(4,1)S(1)} %compare_and_fusion.2), kind=kOutput, calls=%fused_computation.27 | convolution fusion | flops 537133056 | bytes 6815748 | tf_op jit(solution)/shard_map/rmab,rmnbc->rnac/dot_general | solution.py:55
  164.1 4.1 %collective-permute-done.6 = f32[4,8,128,128]{2,3,1,0:T(8,128)S(1)} collective-permute-done((f32[4,8,128,128]{2,3,1,0:T(8,128)S(1)}, f32[4,8,128,128]{2,3,1,0:T(8,128)S(1)}, u32[]{:S(2)}, u32[]{:S(2)}) %collective-permute-start.6) | collective-permute-done | bytes 2097184 | tf_op jit(solution)/shard_map/ppermute | solution.py:24
  168.3 0.3 add_convert_fusion
  168.6 0.6 gather_fusion.9
  169.3 3.5 %convolution_bitcast_fusion = f32[4,8,128,128]{2,3,1,0:T(8,128)S(1)} fusion(bf16[4,4,8,128,128]{3,4,1,2,0:T(8,128)(2,1)} %copy.40, bf16[4,4,128,128]{2,3,1,0:T(8,128)(2,1)S(1)} %gather_fusion.9, pred[4]{0:T(512)(128)(4,1)S(1)} %compare_and_fusion.2), kind=kOutput, calls=%fused_computation.26 | convolution fusion | flops 537133056 | bytes 6815748 | tf_op jit(solution)/shard_map/rmab,rmnbc->rnac/dot_general | solution.py:55
  172.8 0.2 collective-permute-start.7
  173.0 4.0 %collective-permute-done.7 = f32[4,8,128,128]{2,3,1,0:T(8,128)S(1)} collective-permute-done((f32[4,8,128,128]{2,3,1,0:T(8,128)S(1)}, f32[4,8,128,128]{2,3,1,0:T(8,128)S(1)}, u32[]{:S(2)}, u32[]{:S(2)}) %collective-permute-start.7) | collective-permute-done | bytes 2097184 | tf_op jit(solution)/shard_map/ppermute | solution.py:24
  177.0 0.5 subtract_convert_fusion
  177.6 1.3 copy.44
  (29 shorter events, 0.6 us)
Async XLA Ops:
  0.0 48.8 %collective-permute-start.1 = (bf16[4,8,128,128]{3,2,1,0:T(8,128)(2,1)}, bf16[4,8,128,128]{3,2,1,0:T(8,128)(2,1)S(1)}, u32[]{:S(2)}, u32[]{:S(2)}) collective-permute-start(bf16[4,8,128,128]{3,2,1,0:T(8,128)(2,1)} %param.11), channel_id=1, source_target_pairs={{2,0},{4,2},{6,4},{8,6},{10,8},{12,10},{14,12},{0,14},{3,1},{5,3},... | collective-permute-start | bytes 3145736 | tf_op jit(solution)/shard_map/ppermute | solution.py:18
  6.0 43.8 %collective-permute-start = (bf16[4,8,128,128]{3,2,1,0:T(8,128)(2,1)}, bf16[4,8,128,128]{3,2,1,0:T(8,128)(2,1)}, u32[]{:S(2)}, u32[]{:S(2)}) collective-permute-start(bf16[4,8,128,128]{3,2,1,0:T(8,128)(2,1)} %param.11), channel_id=1, source_target_pairs={{0,2},{2,4},{4,6},{6,8},{8,10},{10,12},{12,14},{14,0},{1,3},{3,5},... | collective-permute-start | bytes 3145736 | tf_op jit(solution)/shard_map/ppermute | solution.py:15
  48.8 1.0 copy-start.2
  61.7 7.6 %copy-start.4 = (bf16[4,4,128,128]{3,2,1,0:T(8,128)(2,1)S(1)}, bf16[4,4,128,128]{3,2,1,0:T(8,128)(2,1)}, u32[]{:S(2)}) copy-start(bf16[4,4,128,128]{3,2,1,0:T(8,128)(2,1)} %gather_fusion.5) | copy-start | bytes 1572868
  72.8 4.2 %collective-permute-start.2 = (f32[4,8,128,128]{2,3,1,0:T(8,128)S(1)}, f32[4,8,128,128]{2,3,1,0:T(8,128)S(1)}, u32[]{:S(2)}, u32[]{:S(2)}) collective-permute-start(f32[4,8,128,128]{2,3,1,0:T(8,128)S(1)} %convolution_bitcast_fusion.3), channel_id=1, source_target_pairs={{0,1},{1,0},{2,3},{3,2},{4,5},{5,4},{6,7},{7,6},{8,9},{9,8},{10,11... | collective-permute-start | bytes 6291464 | tf_op jit(solution)/shard_map/ppermute | solution.py:24
  81.5 4.2 %collective-permute-start.3 = (f32[4,8,128,128]{2,3,1,0:T(8,128)S(1)}, f32[4,8,128,128]{2,3,1,0:T(8,128)S(1)}, u32[]{:S(2)}, u32[]{:S(2)}) collective-permute-start(f32[4,8,128,128]{2,3,1,0:T(8,128)S(1)} %convolution_bitcast_fusion.2), channel_id=1, source_target_pairs={{0,1},{1,0},{2,3},{3,2},{4,5},{5,4},{6,7},{7,6},{8,9},{9,8},{10,11... | collective-permute-start | bytes 6291464 | tf_op jit(solution)/shard_map/ppermute | solution.py:24
  86.3 47.8 %copy-start = (bf16[4,8,128,128]{2,3,1,0:T(8,128)(2,1)}, bf16[4,8,128,128]{2,3,1,0:T(8,128)(2,1)S(1)}, u32[]{:S(2)}) copy-start(bf16[4,8,128,128]{2,3,1,0:T(8,128)(2,1)S(1)} %subtract_convert_fusion.1) | copy-start | bytes 3145732
  86.3 47.8 %collective-permute-start.5 = (bf16[4,8,128,128]{2,3,1,0:T(8,128)(2,1)S(1)}, bf16[4,8,128,128]{2,3,1,0:T(8,128)(2,1)S(1)}, u32[]{:S(2)}, u32[]{:S(2)}) collective-permute-start(bf16[4,8,128,128]{2,3,1,0:T(8,128)(2,1)S(1)} %subtract_convert_fusion.1), channel_id=1, source_target_pairs={{2,0},{4,2},{6,4},{8,6},{10,8},{12,10},{14,12},{0,14},{3,1},{5,3},... | collective-permute-start | bytes 3145736 | tf_op jit(solution)/shard_map/ppermute | solution.py:18
  90.5 44.5 %collective-permute-start.4 = (bf16[4,8,128,128]{2,3,1,0:T(8,128)(2,1)S(1)}, bf16[4,8,128,128]{2,3,1,0:T(8,128)(2,1)}, u32[]{:S(2)}, u32[]{:S(2)}) collective-permute-start(bf16[4,8,128,128]{2,3,1,0:T(8,128)(2,1)S(1)} %subtract_convert_fusion.1), channel_id=1, source_target_pairs={{0,2},{2,4},{4,6},{6,8},{8,10},{10,12},{12,14},{14,0},{1,3},{3,5},... | collective-permute-start | bytes 3145736 | tf_op jit(solution)/shard_map/ppermute | solution.py:15
  134.0 1.0 copy-start.3
  153.0 7.5 %copy-start.1 = (bf16[4,4,128,128]{2,3,1,0:T(8,128)(2,1)S(1)}, bf16[4,4,128,128]{2,3,1,0:T(8,128)(2,1)}, u32[]{:S(2)}) copy-start(bf16[4,4,128,128]{2,3,1,0:T(8,128)(2,1)} %gather_fusion.8) | copy-start | bytes 1572868
  164.1 4.2 %collective-permute-start.6 = (f32[4,8,128,128]{2,3,1,0:T(8,128)S(1)}, f32[4,8,128,128]{2,3,1,0:T(8,128)S(1)}, u32[]{:S(2)}, u32[]{:S(2)}) collective-permute-start(f32[4,8,128,128]{2,3,1,0:T(8,128)S(1)} %convolution_bitcast_fusion.1), channel_id=1, source_target_pairs={{0,1},{1,0},{2,3},{3,2},{4,5},{5,4},{6,7},{7,6},{8,9},{9,8},{10,11... | collective-permute-start | bytes 6291464 | tf_op jit(solution)/shard_map/ppermute | solution.py:24
  172.8 4.2 %collective-permute-start.7 = (f32[4,8,128,128]{2,3,1,0:T(8,128)S(1)}, f32[4,8,128,128]{2,3,1,0:T(8,128)S(1)}, u32[]{:S(2)}, u32[]{:S(2)}) collective-permute-start(f32[4,8,128,128]{2,3,1,0:T(8,128)S(1)} %convolution_bitcast_fusion), channel_id=1, source_target_pairs={{0,1},{1,0},{2,3},{3,2},{4,5},{5,4},{6,7},{7,6},{8,9},{9,8},{10,11... | collective-permute-start | bytes 6291464 | tf_op jit(solution)/shard_map/ppermute | solution.py:24
where the time goes:
time: 180 us; the launch traced here: 179 us
  waiting for transfers between devices  93.5 us (52%)
  local copies, waits for them, and re-layouts  41.1 us (23%)
  matrix products  26.3 us (15%)
  starting transfers between devices  10.7 us (6%)
  other arithmetic  7 us (4%)
    ppermute x2, waiting for transfers between devices, with_halo(): lax.ppermute(lax.slice_in_dim(block, 0, width, axis=dim), axis, backward)  77.2 us
    ppermute x4, waiting for transfers between devices, swapped(): lax.ppermute(value, axis, [(i, i ^ 1 << bit) for i in range(lax.axis_size...  16.3 us
    convert_element_type x2, local copies, waits for them, and re-layouts, per_device(): aligned = jnp.einsum('rmnq,rmqab->rmnab', match, fetched, preferred_eleme...  15.1 us
    gather x4, local copies, waits for them, and re-layouts, per_device(): fetched = jnp.take(extended, jnp.take(ext_index, chosen, axis=1), axis=0)  14.1 us
    dot_general x4, matrix products, contract(): jnp.einsum('rmab,rmnbc->rnac', jnp.take(left, picked, axis=1), aligned, p...  14 us
    dot_general x2, matrix products, per_device(): jnp.einsum('rmnq,rmqab->rmnab', match, fetched, preferred_element_type=jn...  12.3 us
    ppermute x2, starting transfers between devices, with_halo(): lax.ppermute(lax.slice_in_dim(block, 0, width, axis=dim), axis, backward)  10.2 us
    gather x4, local copies, waits for them, and re-layouts, contract(): jnp.take(left, picked, axis=1)  5.41 us
  transfers between devices with their start and end apart: 8, of which 6 were waited for; matrix products, arithmetic and copies ran while one was open for 5% of the time, Pallas kernels for 0%

commit v1 on v0

v1 whole, which is shorter than its diff:
```python
import functools

import jax
import jax.numpy as jnp
from jax import lax
from jax.experimental import pallas as pl
from jax.experimental.pallas import tpu as pltpu
from jax.sharding import PartitionSpec as P

BS = 128
ROWS = 4
HALF = 4
FAR = 8
WINDOW = 16
TILE = 2 * BS


def start_of(row):
    return 5 * row + row * (row - 1) // 2


PACKED = start_of(ROWS)


def place(cols_ref, info_ref, index, slot):
    total = cols_ref.shape[1]
    base, sign = info_ref[0], info_ref[1]
    row = lax.rem(base + sign * (index - FAR) + total, total)
    column = cols_ref[slot, row]
    where = lax.rem(sign * (column - base) + FAR + 2 * total, total)
    return where, (column < total) & (where < WINDOW)


def local_row(info_ref, row):
    return jnp.where(info_ref[1] > 0, row, ROWS - 1 - row)


def block(index, first=0):
    return pl.ds((index - first) * BS, BS)


def pair(index, first=0, count=1):
    return pl.ds((2 * index - first) * BS, count * TILE)


def lanes(index, first=0):
    return pl.ds(pl.multiple_of((index - first) * BS, BS), BS)


def pack_kernel(cols_ref, info_ref, tiles_ref, out_ref):
    out_ref[...] = jnp.zeros_like(out_ref)
    slots = cols_ref.shape[0]
    for row in range(ROWS):
        held = local_row(info_ref, row)
        for slot in range(slots):
            where, filled = place(cols_ref, info_ref, FAR + row, slot)

            @pl.when(filled & (where >= FAR))
            def _():
                out_ref[start_of(row) + where - FAR] = tiles_ref[held, slot]


def spread(cols_ref, info_ref, source_ref, index, target_ref, first_row, first_column, mask_ref=None):
    slots = cols_ref.shape[0]
    for row in range(ROWS):
        held = local_row(info_ref, row)
        for slot in range(slots):
            where, filled = place(cols_ref, info_ref, index + row, slot)

            @pl.when(filled & (where >= first_column))
            def _():
                target_ref[block(index + row, first_row), lanes(where, first_column)] = source_ref[held, slot]


def mark(cols_ref, info_ref, index, mask_ref):
    slots = cols_ref.shape[0]
    for row in range(ROWS):
        for column in range(WINDOW):
            mask_ref[row, column] = 0
        for slot in range(slots):
            where, filled = place(cols_ref, info_ref, index + row, slot)

            @pl.when(filled)
            def _():
                mask_ref[row, where] = 1


def kept(value, mask_ref, row, column):
    parts = []
    for down in range(2):
        across = []
        for right in range(2):
            one = value[down * BS:(down + 1) * BS, right * BS:(right + 1) * BS]
            across.append(jnp.where(mask_ref[row + down, column + right] > 0, one, jnp.zeros_like(one)))
        parts.append(jnp.concatenate(across, axis=1))
    return jnp.concatenate(parts, axis=0)


def product(left, right, row_pair, column_pair, low, high):
    start = max(row_pair - 2, column_pair - 2, low)
    stop = min(row_pair + 2, column_pair + 2, high) + 1
    total = None
    while start < stop:
        end, a, b = start + 1, left(row_pair, start), right(start, column_pair)
        while end < stop:
            a2, b2 = left(row_pair, end), right(end, column_pair)
            if a2[0] is not a[0] or b2[0] is not b[0]:
                break
            end += 1
        count = (end - start) * TILE
        part = jnp.dot(
            a[0][pl.ds(a[1], TILE), pl.ds(a[2], count)],
            b[0][pl.ds(b[1], count), pl.ds(b[2], TILE)],
            preferred_element_type=jnp.float32,
        )
        total = part if total is None else total + part
        start = end
    return total


def view(ref, first_row, first_column):
    return lambda row_pair, column_pair: (
        ref, (2 * row_pair - first_row) * BS, (2 * column_pair - first_column) * BS
    )


def purify(left, right, square_ref, square, mask_ref, first_row, pairs, low, high, column_pairs, write):
    for row_pair in pairs:
        row = 2 * row_pair - first_row
        for column_pair in range(max(row_pair - 2, low), min(row_pair + 2, high) + 1):
            value = product(left, right, row_pair, column_pair, low, high)
            _, r, c = square(row_pair, column_pair)
            square_ref[pl.ds(r, TILE), pl.ds(c, TILE)] = kept(
                value, mask_ref, row, 2 * column_pair
            ).astype(jnp.bfloat16)
    for row_pair in pairs:
        row = 2 * row_pair - first_row
        for column_pair in column_pairs(row_pair):
            cube = product(square, right, row_pair, column_pair, low, high)
            _, r, c = square(row_pair, column_pair)
            own = square_ref[pl.ds(r, TILE), pl.ds(c, TILE)].astype(jnp.float32)
            value = 3.0 * own - 2.0 * kept(cube, mask_ref, row, 2 * column_pair)
            write(row_pair, column_pair, value.astype(jnp.bfloat16))


def own_kernel(cols_ref, info_ref, tiles_ref, near_ref, other_ref, low_ref, own_ref, next_ref, high_ref, square_ref, mask_ref):
    low_ref[...] = jnp.zeros_like(low_ref)
    own_ref[...] = jnp.zeros_like(own_ref)
    high_ref[...] = jnp.zeros_like(high_ref)
    spread(cols_ref, info_ref, near_ref, 4, low_ref, 4, 0)
    spread(cols_ref, info_ref, tiles_ref, 8, own_ref, 8, 4)
    spread(cols_ref, info_ref, other_ref, 12, high_ref, 12, 8)
    mark(cols_ref, info_ref, 8, mask_ref)
    views = {2: view(low_ref, 4, 0), 4: view(own_ref, 8, 4), 6: view(high_ref, 12, 8)}

    def right(row_pair, column_pair):
        return views[row_pair // 2 * 2](row_pair, column_pair)

    square = view(square_ref, 8, 4)

    def write(row_pair, column_pair, value):
        next_ref[pair(row_pair, 8), pair(column_pair, 4)] = value

    next_ref[...] = jnp.zeros_like(next_ref)
    purify(
        view(own_ref, 8, 4), right, square_ref, square, mask_ref, 8, (4, 5), 2, 7,
        lambda p: range(p - 2, p + 3), write,
    )


def far_kernel(cols_ref, info_ref, far_ref, low_ref, own_ref, next_ref, dense_ref, square_ref, mask_ref):
    for row in range(ROWS):
        for column in range(8):
            if column < row + 5:
                dense_ref[block(row), block(column)] = far_ref[start_of(row) + column]
            else:
                dense_ref[block(row), block(column)] = jnp.zeros((BS, BS), jnp.bfloat16)
    mark(cols_ref, info_ref, 4, mask_ref)
    views = {0: view(dense_ref, 0, 0), 2: view(low_ref, 4, 0), 4: view(own_ref, 8, 4)}

    def right(row_pair, column_pair):
        return views[row_pair // 2 * 2](row_pair, column_pair)

    def write(row_pair, column_pair, value):
        next_ref[pair(row_pair, 4), pair(column_pair, 4)] = value

    next_ref[pl.ds(0, TILE), pl.ds(3 * TILE, TILE)] = jnp.zeros((TILE, TILE), jnp.bfloat16)
    purify(
        view(low_ref, 4, 0), right, square_ref, view(square_ref, 4, 0), mask_ref, 4, (2, 3), 0, 5,
        lambda p: range(2, p + 3), write,
    )


def last_kernel(cols_ref, info_ref, low_ref, own_ref, other_ref, out_ref, high_ref, square_ref, mask_ref, dense_ref):
    for row in range(ROWS):
        for column in range(8):
            high_ref[block(3 - row), block(7 - column)] = other_ref[block(row), block(column)]
    mark(cols_ref, info_ref, 8, mask_ref)
    views = {2: view(low_ref, 4, 4), 4: view(own_ref, 8, 4), 6: view(high_ref, 12, 8)}

    def right(row_pair, column_pair):
        return views[row_pair // 2 * 2](row_pair, column_pair)

    def write(row_pair, column_pair, value):
        dense_ref[pair(row_pair, 8), pair(column_pair, 4)] = value

    purify(
        view(own_ref, 8, 4), right, square_ref, view(square_ref, 8, 4), mask_ref, 8, (4, 5), 2, 7,
        lambda p: range(p - 2, p + 3), write,
    )
    slots = cols_ref.shape[0]
    for row in range(ROWS):
        held = local_row(info_ref, row)
        for slot in range(slots):
            where, filled = place(cols_ref, info_ref, FAR + row, slot)

            @pl.when(filled)
            def _():
                out_ref[held, slot] = dense_ref[block(row), lanes(where, 4)]

            @pl.when(jnp.logical_not(filled))
            def _():
                out_ref[held, slot] = jnp.zeros((BS, BS), jnp.bfloat16)


def call(kernel, operands, outs, scratch, name, flops=0):
    smem, vmem = pl.BlockSpec(memory_space=pltpu.SMEM), pl.BlockSpec(memory_space=pltpu.VMEM)
    shapes = [jax.ShapeDtypeStruct(shape, jnp.bfloat16) for shape in outs]
    moved = sum(2 * x.size for x in operands[2:]) + sum(2 * s.size for s in shapes)
    return pl.pallas_call(
        kernel,
        out_shape=shapes,
        in_specs=[smem, smem] + [vmem] * (len(operands) - 2),
        out_specs=[vmem] * len(shapes),
        scratch_shapes=scratch,
        compiler_params=pltpu.CompilerParams(vmem_limit_bytes=40 * 2**20),
        cost_estimate=pl.CostEstimate(flops=flops, bytes_accessed=moved, transcendentals=0),
        name=name,
    )(*operands)


def per_device(cols, tiles):
    devices = lax.axis_size("dev")
    first = lax.axis_index("dev") * ROWS
    layer = lax.axis_index("layer")
    info = jnp.stack([first + layer * (ROWS - 1), 1 - 2 * layer]).astype(jnp.int32)
    cols = cols.T
    axes = ("dev", "layer")

    def shifted(value, step):
        pairs = []
        for i in range(devices):
            pairs.append((2 * i, (i + step) % devices * 2))
            pairs.append((2 * i + 1, (i - step) % devices * 2 + 1))
        return lax.ppermute(value, axes, pairs)

    def swapped(value):
        return lax.ppermute(value, "layer", [(0, 1), (1, 0)])

    bf16 = jnp.bfloat16
    mask = pltpu.SMEM((ROWS, WINDOW), jnp.int32)
    near = shifted(tiles, 1)
    (packed,) = call(pack_kernel, (cols, info, tiles), [(PACKED, BS, BS)], [], "pack")
    far = shifted(packed, 2)
    other = swapped(near)
    unit = 2 * TILE**3
    low, own, current = call(
        own_kernel, (cols, info, tiles, near, other),
        [(ROWS * BS, 12 * BS), (ROWS * BS, 12 * BS), (ROWS * BS, 12 * BS)],
        [pltpu.VMEM((ROWS * BS, 8 * BS), bf16), pltpu.VMEM((ROWS * BS, 12 * BS), bf16), mask],
        "own", 76 * unit,
    )
    (current_low,) = call(
        far_kernel, (cols, info, far, low, own),
        [(ROWS * BS, 8 * BS)],
        [pltpu.VMEM((ROWS * BS, 8 * BS), bf16), pltpu.VMEM((ROWS * BS, 12 * BS), bf16), mask],
        "far", 66 * unit,
    )
    current_other = swapped(current_low)
    (out,) = call(
        last_kernel, (cols, info, current_low, current, current_other),
        [tiles.shape],
        [pltpu.VMEM((ROWS * BS, 8 * BS), bf16), pltpu.VMEM((ROWS * BS, 12 * BS), bf16), mask,
         pltpu.VMEM((ROWS * BS, 12 * BS), bf16)],
        "last", 76 * unit,
    )
    return out


def solution(mesh):
    return jax.shard_map(
        per_device,
        mesh=mesh,
        in_specs=(P("grp", None), P(("grp", "dev"), None, None, None)),
        out_specs=P(("grp", "dev"), None, None, None),
        check_vma=False,
    )
```

time: 180 us -> 65.1 us (0.36)
  waiting for transfers between devices: 93.5 us -> 41.8 us
  local copies, waits for them, and re-layouts: 41.1 us -> 1.91 us
  matrix products: 26.3 us -> 0 us
  Pallas kernels: 0 us -> 16.4 us
  other arithmetic: 7 us -> 0.07 us
  starting transfers between devices: 10.7 us -> 4.64 us
    ppermute x8 -> x4, waiting for transfers between devices: 93.5 us -> 41.8 us  [the longest x2 39.2 us: shifted(): return lax.ppermute(value, axes, pairs)]
    dot_general x6 -> x0, matrix products: 26.3 us -> none  [the longest x4 14 us: contract(): jnp.einsum('rmab,rmnbc->rnac', jnp.take(left, picked, axis=1), aligned, p...]
    gather x11 -> x0, local copies, waits for them, and re-layouts: 21.2 us -> none  [the longest x4 14.1 us: per_device(): fetched = jnp.take(extended, jnp.take(ext_index, chosen, axis=1), axis=0)]
    pallas_call x0 -> x4, Pallas kernels: none -> 16.4 us  [call(): pl.pallas_call(kernel, out_shape=shapes, in_specs=[smem, smem] + [vmem] *...]
    convert_element_type x3 -> x0, local copies, waits for them, and re-layouts: 16.4 us -> none  [the longest x2 15.1 us: per_device(): aligned = jnp.einsum('rmnq,rmqab->rmnab', match, fetched, preferred_eleme...]
    ppermute x8 -> x4, starting transfers between devices: 10.7 us -> 4.64 us  [the longest x2 4.57 us: shifted(): return lax.ppermute(value, axes, pairs)]
    concatenate x2 -> x0, other arithmetic: 4.06 us -> none  [with_halo(): block = jnp.concatenate([low, block, high], axis=dim)]
    convert_element_type x5 -> x0, other arithmetic: 1.84 us -> none  [the longest x2 1.1 us: per_device(): (3.0 * square.astype(jnp.float32) - 2.0 * cube_term).astype(jnp.bfloat16)]
  transfers between devices with their start and end apart: 8 -> 4, of which waited for: 6 -> 3; matrix products, arithmetic and copies ran while one was open for 5% -> 0% of each run, Pallas kernels for 0% -> 12%
where the time goes in v1:
time: 65.1 us; the launch traced here: 64.9 us
  waiting for transfers between devices  41.8 us (64%)
  Pallas kernels  16.4 us (25%)
  starting transfers between devices  4.64 us (7%)
  local copies, waits for them, and re-layouts  1.91 us (3%)
    ppermute x2, waiting for transfers between devices, shifted(): return lax.ppermute(value, axes, pairs)  39.2 us
    pallas_call x4, Pallas kernels, call(): pl.pallas_call(kernel, out_shape=shapes, in_specs=[smem, smem] + [vmem] *...  16.4 us
    ppermute x2, starting transfers between devices, shifted(): return lax.ppermute(value, axes, pairs)  4.57 us
    ppermute x2, waiting for transfers between devices, swapped(): return lax.ppermute(value, 'layer', [(0, 1), (1, 0)])  2.65 us
    unnamed x4, local copies, waits for them, and re-layouts  1.91 us
  transfers between devices with their start and end apart: 4, of which 3 were waited for; matrix products, arithmetic and copies ran while one was open for 0% of the time, Pallas kernels for 12%

profile of v1, /device:TPU:0, one launch (start us, length us, event | category | flops | bytes accessed | tf_op | source)
XLA Modules:
  0.0 64.9 jit_solution(3749204008749180140)
XLA Ops:
  0.0 2.9 %collective-permute-start.1 = (bf16[4,8,128,128]{3,2,1,0:T(8,128)(2,1)}, bf16[4,8,128,128]{3,2,1,0:T(8,128)(2,1)S(1)}, u32[]{:S(2)}, u32[]{:S(2)}) collective-permute-start(bf16[4,8,128,128]{3,2,1,0:T(8,128)(2,1)} %tiles_ref.3), channel_id=1, source_target_pairs={{0,2},{1,15},{2,4},{3,1},{4,6},{5,3},{6,8},{7,5},{8,10},{9,7},{10,... | collective-permute-start | bytes 3145736 | tf_op jit(solution)/shard_map/ppermute | solution.py:255
  2.9 23.6 %collective-permute-done.1.near_ref = bf16[4,8,128,128]{3,2,1,0:T(8,128)(2,1)S(1)} collective-permute-done((bf16[4,8,128,128]{3,2,1,0:T(8,128)(2,1)}, bf16[4,8,128,128]{3,2,1,0:T(8,128)(2,1)S(1)}, u32[]{:S(2)}, u32[]{:S(2)}) %collective-permute-start.1) | collective-permute-done | bytes 1048608 | tf_op jit(solution)/shard_map/ppermute | solution.py:255
  26.6 0.0 collective-permute-start.2
  26.6 0.1 pad_add_fusion.info_ref
  26.6 0.0 copy-start
  26.7 1.2 %copy-done = bf16[4,8,128,128]{3,2,1,0:T(8,128)(2,1)S(1)} copy-done((bf16[4,8,128,128]{3,2,1,0:T(8,128)(2,1)S(1)}, bf16[4,8,128,128]{3,2,1,0:T(8,128)(2,1)}, u32[]{:S(2)}) %copy-start) | copy-done | bytes 1048600
  27.9 0.0 copy-start.1
  27.9 0.7 %copy-done.1 = s32[32,8]{0,1:T(8,128)S(1)} copy-done((s32[32,8]{0,1:T(8,128)S(1)}, s32[32,8]{0,1:T(8,128)}, u32[]{:S(2)}) %copy-start.1) | copy-done | bytes 1048
  28.6 1.5 %pack.1 = bf16[26,128,128]{2,1,0:T(8,128)(2,1)S(1)} custom-call(s32[8,32]{1,0:T(8,128)S(1)} %bitcast.3, s32[2]{0:T(128)S(1)} %pad_add_fusion.info_ref, bf16[4,8,128,128]{3,2,1,0:T(8,128)(2,1)S(1)} %copy-done), custom_call_target="tpu_custom_call" | custom-call | bytes 1900544 | tf_op jit(solution)/shard_map/pack/pallas_call | solution.py:230
  30.0 1.6 %collective-permute-start = (bf16[26,128,128]{2,1,0:T(8,128)(2,1)S(1)}, bf16[26,128,128]{2,1,0:T(8,128)(2,1)S(1)}, u32[]{:S(2)}, u32[]{:S(2)}) collective-permute-start(bf16[26,128,128]{2,1,0:T(8,128)(2,1)S(1)} %pack.1), channel_id=1, source_target_pairs={{0,4},{1,13},{2,6},{3,15},{4,8},{5,1},{6,10},{7,3},{8,12},{9,5},{1... | collective-permute-start | bytes 2555912 | tf_op jit(solution)/shard_map/ppermute | solution.py:255
  31.7 0.0 collective-permute-done.2.other_ref
  31.7 6.3 %own.1 = (bf16[512,1536]{1,0:T(8,128)(2,1)S(1)}, bf16[512,1536]{1,0:T(8,128)(2,1)S(1)}, bf16[512,1536]{1,0:T(8,128)(2,1)S(1)}) custom-call(s32[8,32]{1,0:T(8,128)S(1)} %bitcast.4, s32[2]{0:T(128)S(1)} %pad_add_fusion.info_ref, bf16[4,8,128,128]{3,2,1,0:T(8,128)(2,1)S(1)} %copy-done, bf16[4,8,128,128]{3,2,1,0:T(8,128)(2,1)S(1)} %collective-permute-done.1.near_ref, ...), custom_call_target="tpu_custom_call" | custom-call | flops 2550136832 | bytes 7864320 | tf_op jit(solution)/shard_map/own/pallas_call | solution.py:230
  38.0 15.5 %collective-permute-done.far_ref = bf16[26,128,128]{2,1,0:T(8,128)(2,1)S(1)} collective-permute-done((bf16[26,128,128]{2,1,0:T(8,128)(2,1)S(1)}, bf16[26,128,128]{2,1,0:T(8,128)(2,1)S(1)}, u32[]{:S(2)}, u32[]{:S(2)}) %collective-permute-start) | collective-permute-done | bytes 852000 | tf_op jit(solution)/shard_map/ppermute | solution.py:255
  53.5 3.2 %far.1.low_ref = bf16[512,1024]{1,0:T(8,128)(2,1)S(1)} custom-call(s32[8,32]{1,0:T(8,128)S(1)} %bitcast.5, s32[2]{0:T(128)S(1)} %pad_add_fusion.info_ref, bf16[26,128,128]{2,1,0:T(8,128)(2,1)S(1)} %collective-permute-done.far_ref, bf16[512,1536]{1,0:T(8,128)(2,1)S(1)} %get-tuple-element.8.low_ref, bf16[512,1536]{1,0:T(8,128)(2,1)S(1)} %get-tuple-element.9.own_ref), custom_call_target="tpu_custom_call" | custom-call | flops 2214592512 | bytes 5046272 | tf_op jit(solution)/shard_map/far/pallas_call | solution.py:230
  56.7 0.1 collective-permute-start.3
  56.8 2.6 %collective-permute-done.3.other_ref = bf16[512,1024]{1,0:T(8,128)(2,1)S(1)} collective-permute-done((bf16[512,1024]{1,0:T(8,128)(2,1)S(1)}, bf16[512,1024]{1,0:T(8,128)(2,1)S(1)}, u32[]{:S(2)}, u32[]{:S(2)}) %collective-permute-start.3) | collective-permute-done | bytes 1048608 | tf_op jit(solution)/shard_map/ppermute | solution.py:258
  59.5 5.5 %last.1 = bf16[4,8,128,128]{3,2,1,0:T(8,128)(2,1)} custom-call(s32[8,32]{1,0:T(8,128)S(1)} %bitcast.6, s32[2]{0:T(128)S(1)} %pad_add_fusion.info_ref, bf16[512,1024]{1,0:T(8,128)(2,1)S(1)} %far.1.low_ref, bf16[512,1536]{1,0:T(8,128)(2,1)S(1)} %get-tuple-element.10.own_ref, bf16[512,1024]{1,0:T(8,128)(2,1)S(1)} %collective-permute-done.3.other_ref), custom_call_target="tpu_custom_call" | custom-call | flops 2550136832 | bytes 4718592 | tf_op jit(solution)/shard_map/last/pallas_call | solution.py:230
Async XLA Ops:
  0.0 26.6 %collective-permute-start.1 = (bf16[4,8,128,128]{3,2,1,0:T(8,128)(2,1)}, bf16[4,8,128,128]{3,2,1,0:T(8,128)(2,1)S(1)}, u32[]{:S(2)}, u32[]{:S(2)}) collective-permute-start(bf16[4,8,128,128]{3,2,1,0:T(8,128)(2,1)} %tiles_ref.3), channel_id=1, source_target_pairs={{0,2},{1,15},{2,4},{3,1},{4,6},{5,3},{6,8},{7,5},{8,10},{9,7},{10,... | collective-permute-start | bytes 3145736 | tf_op jit(solution)/shard_map/ppermute | solution.py:255
  26.6 5.1 %collective-permute-start.2 = (bf16[4,8,128,128]{3,2,1,0:T(8,128)(2,1)S(1)}, bf16[4,8,128,128]{3,2,1,0:T(8,128)(2,1)S(1)}, u32[]{:S(2)}, u32[]{:S(2)}) collective-permute-start(bf16[4,8,128,128]{3,2,1,0:T(8,128)(2,1)S(1)} %collective-permute-done.1.near_ref), channel_id=1, source_target_pairs={{0,1},{1,0},{2,3},{3,2},{4,5},{5,4},{6,7},{7,6},{8,9},{9,8},{10,11... | collective-permute-start | bytes 3145736 | tf_op jit(solution)/shard_map/ppermute | solution.py:258
  26.6 1.2 %copy-start = (bf16[4,8,128,128]{3,2,1,0:T(8,128)(2,1)S(1)}, bf16[4,8,128,128]{3,2,1,0:T(8,128)(2,1)}, u32[]{:S(2)}) copy-start(bf16[4,8,128,128]{3,2,1,0:T(8,128)(2,1)} %tiles_ref.3) | copy-start | bytes 3145732
  27.9 0.7 %copy-start.1 = (s32[32,8]{0,1:T(8,128)S(1)}, s32[32,8]{0,1:T(8,128)}, u32[]{:S(2)}) copy-start(s32[32,8]{0,1:T(8,128)} %param.2) | copy-start | bytes 3076
  30.0 23.5 %collective-permute-start = (bf16[26,128,128]{2,1,0:T(8,128)(2,1)S(1)}, bf16[26,128,128]{2,1,0:T(8,128)(2,1)S(1)}, u32[]{:S(2)}, u32[]{:S(2)}) collective-permute-start(bf16[26,128,128]{2,1,0:T(8,128)(2,1)S(1)} %pack.1), channel_id=1, source_target_pairs={{0,4},{1,13},{2,6},{3,15},{4,8},{5,1},{6,10},{7,3},{8,12},{9,5},{1... | collective-permute-start | bytes 2555912 | tf_op jit(solution)/shard_map/ppermute | solution.py:255
  56.7 2.7 %collective-permute-start.3 = (bf16[512,1024]{1,0:T(8,128)(2,1)S(1)}, bf16[512,1024]{1,0:T(8,128)(2,1)S(1)}, u32[]{:S(2)}, u32[]{:S(2)}) collective-permute-start(bf16[512,1024]{1,0:T(8,128)(2,1)S(1)} %far.1.low_ref), channel_id=1, source_target_pairs={{0,1},{1,0},{2,3},{3,2},{4,5},{5,4},{6,7},{7,6},{8,9},{9,8},{10,11... | collective-permute-start | bytes 3145736 | tf_op jit(solution)/shard_map/ppermute | solution.py:258

commit v2 on v1

--- a/solution.py
+++ b/solution.py
@@ -60,7 +60,7 @@
                 out_ref[start_of(row) + where - FAR] = tiles_ref[held, slot]
 
 
-def spread(cols_ref, info_ref, source_ref, index, target_ref, first_row, first_column, mask_ref=None):
+def spread(cols_ref, info_ref, fetch, index, target_ref, first_row, first_column):
     slots = cols_ref.shape[0]
     for row in range(ROWS):
         held = local_row(info_ref, row)
@@ -69,7 +69,7 @@
 
             @pl.when(filled & (where >= first_column))
             def _():
-                target_ref[block(index + row, first_row), lanes(where, first_column)] = source_ref[held, slot]
+                target_ref[block(index + row, first_row), lanes(where, first_column)] = fetch(held, slot)
 
 
 def mark(cols_ref, info_ref, index, mask_ref):
@@ -143,13 +143,17 @@
             write(row_pair, column_pair, value.astype(jnp.bfloat16))
 
 
-def own_kernel(cols_ref, info_ref, tiles_ref, near_ref, other_ref, low_ref, own_ref, next_ref, high_ref, square_ref, mask_ref):
+def own_kernel(cols_ref, info_ref, tiles_ref, near_ref, other0_ref, other1_ref, low_ref, own_ref, next_ref, high_ref, square_ref, mask_ref):
     low_ref[...] = jnp.zeros_like(low_ref)
     own_ref[...] = jnp.zeros_like(own_ref)
     high_ref[...] = jnp.zeros_like(high_ref)
-    spread(cols_ref, info_ref, near_ref, 4, low_ref, 4, 0)
-    spread(cols_ref, info_ref, tiles_ref, 8, own_ref, 8, 4)
-    spread(cols_ref, info_ref, other_ref, 12, high_ref, 12, 8)
+    spread(cols_ref, info_ref, lambda row, slot: near_ref[row, slot], 4, low_ref, 4, 0)
+    spread(cols_ref, info_ref, lambda row, slot: tiles_ref[row, slot], 8, own_ref, 8, 4)
+    spread(
+        cols_ref, info_ref,
+        lambda row, slot: jnp.where(row < 2, other0_ref[row % 2, slot], other1_ref[row % 2, slot]),
+        12, high_ref, 12, 8,
+    )
     mark(cols_ref, info_ref, 8, mask_ref)
     views = {2: view(low_ref, 4, 0), 4: view(own_ref, 8, 4), 6: view(high_ref, 12, 8)}
 
@@ -262,10 +266,11 @@
     near = shifted(tiles, 1)
     (packed,) = call(pack_kernel, (cols, info, tiles), [(PACKED, BS, BS)], [], "pack")
     far = shifted(packed, 2)
-    other = swapped(near)
+    near, packed = lax.optimization_barrier((near, packed))
+    other = [swapped(near[:2]), swapped(near[2:])]
     unit = 2 * TILE**3
     low, own, current = call(
-        own_kernel, (cols, info, tiles, near, other),
+        own_kernel, (cols, info, tiles, near, *other),
         [(ROWS * BS, 12 * BS), (ROWS * BS, 12 * BS), (ROWS * BS, 12 * BS)],
         [pltpu.VMEM((ROWS * BS, 8 * BS), bf16), pltpu.VMEM((ROWS * BS, 12 * BS), bf16), mask],
         "own", 76 * unit,

time: 65.1 us -> 48.3 us (0.74)
  waiting for transfers between devices: 41.8 us -> 23.9 us
  starting transfers between devices: 4.64 us -> 5.34 us
    ppermute x2, waiting for transfers between devices: 39.2 us -> 19.3 us  [shifted(): return lax.ppermute(value, axes, pairs)]
    ppermute x2 -> x3, waiting for transfers between devices: 2.65 us -> 4.67 us  [swapped(): return lax.ppermute(value, 'layer', [(0, 1), (1, 0)])]
    ppermute x2 -> x3, starting transfers between devices: 0.07 us -> 0.78 us  [swapped(): return lax.ppermute(value, 'layer', [(0, 1), (1, 0)])]
  transfers between devices with their start and end apart: 4 -> 5, of which waited for: 3 -> 4; matrix products, arithmetic and copies ran while one was open for 0% -> 0% of each run, Pallas kernels for 12% -> 17%
where the time goes in v2:
time: 48.3 us; the launch traced here: 48.1 us
  waiting for transfers between devices  23.9 us (49%)
  Pallas kernels  16.7 us (35%)
  starting transfers between devices  5.34 us (11%)
  local copies, waits for them, and re-layouts  1.98 us (4%)
    ppermute x2, waiting for transfers between devices, shifted(): return lax.ppermute(value, axes, pairs)  19.3 us
    pallas_call x4, Pallas kernels, call(): pl.pallas_call(kernel, out_shape=shapes, in_specs=[smem, smem] + [vmem] *...  16.7 us
    ppermute x3, waiting for transfers between devices, swapped(): return lax.ppermute(value, 'layer', [(0, 1), (1, 0)])  4.67 us
    ppermute x2, starting transfers between devices, shifted(): return lax.ppermute(value, axes, pairs)  4.57 us
    unnamed x4, local copies, waits for them, and re-layouts  1.91 us
  transfers between devices with their start and end apart: 5, of which 4 were waited for; matrix products, arithmetic and copies ran while one was open for 0% of the time, Pallas kernels for 17%

profile of v2, /device:TPU:0, one launch (start us, length us, event | category | flops | bytes accessed | tf_op | source)
XLA Modules:
  0.0 48.1 jit_solution(17159963297134730090)
XLA Ops:
  0.0 2.9 %collective-permute-start.1 = (bf16[4,8,128,128]{3,2,1,0:T(8,128)(2,1)}, bf16[4,8,128,128]{3,2,1,0:T(8,128)(2,1)S(1)}, u32[]{:S(2)}, u32[]{:S(2)}) collective-permute-start(bf16[4,8,128,128]{3,2,1,0:T(8,128)(2,1)} %tiles_ref.3), channel_id=1, source_target_pairs={{0,2},{1,15},{2,4},{3,1},{4,6},{5,3},{6,8},{7,5},{8,10},{9,7},{10,... | collective-permute-start | bytes 3145736 | tf_op jit(solution)/shard_map/ppermute | solution.py:259
  2.9 0.1 pad_add_fusion.info_ref
  3.0 0.0 copy-start
  3.0 1.2 %copy-done = bf16[4,8,128,128]{3,2,1,0:T(8,128)(2,1)S(1)} copy-done((bf16[4,8,128,128]{3,2,1,0:T(8,128)(2,1)S(1)}, bf16[4,8,128,128]{3,2,1,0:T(8,128)(2,1)}, u32[]{:S(2)}) %copy-start) | copy-done | bytes 1048600
  4.2 0.0 copy-start.1
  4.2 0.7 %copy-done.1 = s32[32,8]{0,1:T(8,128)S(1)} copy-done((s32[32,8]{0,1:T(8,128)S(1)}, s32[32,8]{0,1:T(8,128)}, u32[]{:S(2)}) %copy-start.1) | copy-done | bytes 1048
  4.9 1.5 %pack.1 = bf16[26,128,128]{2,1,0:T(8,128)(2,1)S(1)} custom-call(s32[8,32]{1,0:T(8,128)S(1)} %bitcast.3, s32[2]{0:T(128)S(1)} %pad_add_fusion.info_ref, bf16[4,8,128,128]{3,2,1,0:T(8,128)(2,1)S(1)} %copy-done), custom_call_target="tpu_custom_call" | custom-call | bytes 1900544 | tf_op jit(solution)/shard_map/pack/pallas_call | solution.py:234
  6.4 1.6 %collective-permute-start = (bf16[26,128,128]{2,1,0:T(8,128)(2,1)S(1)}, bf16[26,128,128]{2,1,0:T(8,128)(2,1)S(1)}, u32[]{:S(2)}, u32[]{:S(2)}) collective-permute-start(bf16[26,128,128]{2,1,0:T(8,128)(2,1)S(1)} %pack.1), channel_id=1, source_target_pairs={{0,4},{1,13},{2,6},{3,15},{4,8},{5,1},{6,10},{7,3},{8,12},{9,5},{1... | collective-permute-start | bytes 2555912 | tf_op jit(solution)/shard_map/ppermute | solution.py:259
  8.0 19.3 %collective-permute-done.1.near_ref = bf16[4,8,128,128]{3,2,1,0:T(8,128)(2,1)S(1)} collective-permute-done((bf16[4,8,128,128]{3,2,1,0:T(8,128)(2,1)}, bf16[4,8,128,128]{3,2,1,0:T(8,128)(2,1)S(1)}, u32[]{:S(2)}, u32[]{:S(2)}) %collective-permute-start.1) | collective-permute-done | bytes 1048608 | tf_op jit(solution)/shard_map/ppermute | solution.py:259
  27.3 0.1 fusion
  27.3 0.1 collective-permute-start.3
  27.4 0.5 %collective-permute-start.2 = (bf16[2,8,128,128]{3,2,1,0:T(8,128)(2,1)S(1)}, bf16[2,8,128,128]{3,2,1,0:T(8,128)(2,1)S(1)}, u32[]{:S(2)}, u32[]{:S(2)}) collective-permute-start(bf16[2,8,128,128]{3,2,1,0:T(8,128)(2,1)S(1)} %get-tuple-element.14), channel_id=1, source_target_pairs={{0,1},{1,0},{2,3},{3,2},{4,5},{5,4},{6,7},{7,6},{8,9},{9,8},{10,11... | collective-permute-start | bytes 1572872 | tf_op jit(solution)/shard_map/ppermute | solution.py:262
  27.9 1.4 %collective-permute-done.3.other1_ref = bf16[2,8,128,128]{3,2,1,0:T(8,128)(2,1)S(1)} collective-permute-done((bf16[2,8,128,128]{3,2,1,0:T(8,128)(2,1)S(1)}, bf16[2,8,128,128]{3,2,1,0:T(8,128)(2,1)S(1)}, u32[]{:S(2)}, u32[]{:S(2)}) %collective-permute-start.3) | collective-permute-done | bytes 524320 | tf_op jit(solution)/shard_map/ppermute | solution.py:262
  29.3 0.7 %collective-permute-done.2.other0_ref = bf16[2,8,128,128]{3,2,1,0:T(8,128)(2,1)S(1)} collective-permute-done((bf16[2,8,128,128]{3,2,1,0:T(8,128)(2,1)S(1)}, bf16[2,8,128,128]{3,2,1,0:T(8,128)(2,1)S(1)}, u32[]{:S(2)}, u32[]{:S(2)}) %collective-permute-start.2) | collective-permute-done | bytes 524320 | tf_op jit(solution)/shard_map/ppermute | solution.py:262
  30.1 6.6 %own.1 = (bf16[512,1536]{1,0:T(8,128)(2,1)S(1)}, bf16[512,1536]{1,0:T(8,128)(2,1)S(1)}, bf16[512,1536]{1,0:T(8,128)(2,1)S(1)}) custom-call(s32[8,32]{1,0:T(8,128)S(1)} %bitcast.4, s32[2]{0:T(128)S(1)} %pad_add_fusion.info_ref, bf16[4,8,128,128]{3,2,1,0:T(8,128)(2,1)S(1)} %copy-done, bf16[4,8,128,128]{3,2,1,0:T(8,128)(2,1)S(1)} %collective-permute-done.1.near_ref, ...), custom_call_target="tpu_custom_call" | custom-call | flops 2550136832 | bytes 7864320 | tf_op jit(solution)/shard_map/own/pallas_call | solution.py:234
  36.6 0.0 collective-permute-done.far_ref
  36.6 3.2 %far.1.low_ref = bf16[512,1024]{1,0:T(8,128)(2,1)S(1)} custom-call(s32[8,32]{1,0:T(8,128)S(1)} %bitcast.5, s32[2]{0:T(128)S(1)} %pad_add_fusion.info_ref, bf16[26,128,128]{2,1,0:T(8,128)(2,1)S(1)} %collective-permute-done.far_ref, bf16[512,1536]{1,0:T(8,128)(2,1)S(1)} %get-tuple-element.10.low_ref, bf16[512,1536]{1,0:T(8,128)(2,1)S(1)} %get-tuple-element.11.own_ref), custom_call_target="tpu_custom_call" | custom-call | flops 2214592512 | bytes 5046272 | tf_op jit(solution)/shard_map/far/pallas_call | solution.py:234
  39.9 0.2 collective-permute-start.4
  40.1 2.5 %collective-permute-done.4.other_ref = bf16[512,1024]{1,0:T(8,128)(2,1)S(1)} collective-permute-done((bf16[512,1024]{1,0:T(8,128)(2,1)S(1)}, bf16[512,1024]{1,0:T(8,128)(2,1)S(1)}, u32[]{:S(2)}, u32[]{:S(2)}) %collective-permute-start.4) | collective-permute-done | bytes 1048608 | tf_op jit(solution)/shard_map/ppermute | solution.py:262
  42.6 5.5 %last.1 = bf16[4,8,128,128]{3,2,1,0:T(8,128)(2,1)} custom-call(s32[8,32]{1,0:T(8,128)S(1)} %bitcast.6, s32[2]{0:T(128)S(1)} %pad_add_fusion.info_ref, bf16[512,1024]{1,0:T(8,128)(2,1)S(1)} %far.1.low_ref, bf16[512,1536]{1,0:T(8,128)(2,1)S(1)} %get-tuple-element.12.own_ref, bf16[512,1024]{1,0:T(8,128)(2,1)S(1)} %collective-permute-done.4.other_ref), custom_call_target="tpu_custom_call" | custom-call | flops 2550136832 | bytes 4718592 | tf_op jit(solution)/shard_map/last/pallas_call | solution.py:234
Async XLA Ops:
  0.0 27.3 %collective-permute-start.1 = (bf16[4,8,128,128]{3,2,1,0:T(8,128)(2,1)}, bf16[4,8,128,128]{3,2,1,0:T(8,128)(2,1)S(1)}, u32[]{:S(2)}, u32[]{:S(2)}) collective-permute-start(bf16[4,8,128,128]{3,2,1,0:T(8,128)(2,1)} %tiles_ref.3), channel_id=1, source_target_pairs={{0,2},{1,15},{2,4},{3,1},{4,6},{5,3},{6,8},{7,5},{8,10},{9,7},{10,... | collective-permute-start | bytes 3145736 | tf_op jit(solution)/shard_map/ppermute | solution.py:259
  3.0 1.2 %copy-start = (bf16[4,8,128,128]{3,2,1,0:T(8,128)(2,1)S(1)}, bf16[4,8,128,128]{3,2,1,0:T(8,128)(2,1)}, u32[]{:S(2)}) copy-start(bf16[4,8,128,128]{3,2,1,0:T(8,128)(2,1)} %tiles_ref.3) | copy-start | bytes 3145732
  4.2 0.7 %copy-start.1 = (s32[32,8]{0,1:T(8,128)S(1)}, s32[32,8]{0,1:T(8,128)}, u32[]{:S(2)}) copy-start(s32[32,8]{0,1:T(8,128)} %param.2) | copy-start | bytes 3076
  6.4 30.3 %collective-permute-start = (bf16[26,128,128]{2,1,0:T(8,128)(2,1)S(1)}, bf16[26,128,128]{2,1,0:T(8,128)(2,1)S(1)}, u32[]{:S(2)}, u32[]{:S(2)}) collective-permute-start(bf16[26,128,128]{2,1,0:T(8,128)(2,1)S(1)} %pack.1), channel_id=1, source_target_pairs={{0,4},{1,13},{2,6},{3,15},{4,8},{5,1},{6,10},{7,3},{8,12},{9,5},{1... | collective-permute-start | bytes 2555912 | tf_op jit(solution)/shard_map/ppermute | solution.py:259
  27.3 2.0 %collective-permute-start.3 = (bf16[2,8,128,128]{3,2,1,0:T(8,128)(2,1)S(1)}, bf16[2,8,128,128]{3,2,1,0:T(8,128)(2,1)S(1)}, u32[]{:S(2)}, u32[]{:S(2)}) collective-permute-start(bf16[2,8,128,128]{3,2,1,0:T(8,128)(2,1)S(1)} %get-tuple-element.13), channel_id=1, source_target_pairs={{0,1},{1,0},{2,3},{3,2},{4,5},{5,4},{6,7},{7,6},{8,9},{9,8},{10,11... | collective-permute-start | bytes 1572872 | tf_op jit(solution)/shard_map/ppermute | solution.py:262
  27.4 2.6 %collective-permute-start.2 = (bf16[2,8,128,128]{3,2,1,0:T(8,128)(2,1)S(1)}, bf16[2,8,128,128]{3,2,1,0:T(8,128)(2,1)S(1)}, u32[]{:S(2)}, u32[]{:S(2)}) collective-permute-start(bf16[2,8,128,128]{3,2,1,0:T(8,128)(2,1)S(1)} %get-tuple-element.14), channel_id=1, source_target_pairs={{0,1},{1,0},{2,3},{3,2},{4,5},{5,4},{6,7},{7,6},{8,9},{9,8},{10,11... | collective-permute-start | bytes 1572872 | tf_op jit(solution)/shard_map/ppermute | solution.py:262
  39.9 2.7 %collective-permute-start.4 = (bf16[512,1024]{1,0:T(8,128)(2,1)S(1)}, bf16[512,1024]{1,0:T(8,128)(2,1)S(1)}, u32[]{:S(2)}, u32[]{:S(2)}) collective-permute-start(bf16[512,1024]{1,0:T(8,128)(2,1)S(1)} %far.1.low_ref), channel_id=1, source_target_pairs={{0,1},{1,0},{2,3},{3,2},{4,5},{5,4},{6,7},{7,6},{8,9},{9,8},{10,11... | collective-permute-start | bytes 3145736 | tf_op jit(solution)/shard_map/ppermute | solution.py:262

commit v3 on v0

v3 whole, which is shorter than its diff:
```python
import functools

import jax
import jax.numpy as jnp
from jax import lax
from jax.experimental import pallas as pl
from jax.experimental.pallas import tpu as pltpu
from jax.sharding import PartitionSpec as P

BS = 128
ROWS = 4
HALF = 4
FAR = 8
WINDOW = 16
TILE = 2 * BS


def start_of(row):
    return 5 * row + row * (row - 1) // 2


PACKED = start_of(ROWS)
SLOTS = 2 * HALF


def block(index, first=0):
    return pl.ds((index - first) * BS, BS)


def lanes(index, first=0):
    return pl.ds(pl.multiple_of((index - first) * BS, BS), BS)


def tile(index, first=0):
    return pl.ds((2 * index - first) * BS, TILE)


def local_row(info_ref, row):
    return jnp.where(info_ref[1] > 0, row, ROWS - 1 - row)


def pack_kernel(info_ref, cols_ref, tiles_ref, out_ref, table_ref, sem):
    total = cols_ref.shape[1]
    table = pltpu.make_async_copy(cols_ref, table_ref, sem)
    table.start()
    out_ref[...] = jnp.zeros_like(out_ref)
    table.wait()
    base, sign = info_ref[0], info_ref[1]
    copies = []
    for row in range(ROWS):
        held = local_row(info_ref, row)
        for slot in range(SLOTS):
            column = table_ref[slot, base + sign * row]
            where = lax.rem(sign * (column - base) + total, total)
            wanted = (column < total) & (where < HALF + ROWS)
            target = jnp.where(wanted, start_of(row) + where, 0)
            copy = pltpu.make_async_copy(tiles_ref.at[held, slot], out_ref.at[target], sem)
            copies.append((wanted, copy))
            pl.when(wanted)(copy.start)
    for wanted, copy in copies:
        pl.when(wanted)(copy.wait)


def spread(info_ref, place_ref, sources, index, target_ref, first_column):
    last = target_ref.shape[1] // BS - 1
    count = ROWS // len(sources)
    for row in range(ROWS):
        held = local_row(info_ref, row)
        for slot in range(SLOTS):
            where = jnp.minimum(place_ref[(index + row) * SLOTS + slot] - first_column, last)
            value = sources[0][held % count, slot]
            for i in range(1, len(sources)):
                value = jnp.where(held >= i * count, sources[i][held % count, slot], value)
            target_ref[block(row), lanes(where)] = value


def kept(value, mask_ref, row_pair, column_pair):
    parts = []
    for down in range(2):
        across = []
        for right in range(2):
            one = value[down * BS:(down + 1) * BS, right * BS:(right + 1) * BS]
            there = mask_ref[(2 * row_pair + down) * WINDOW + 2 * column_pair + right] > 0
            across.append(jnp.where(there, one, jnp.zeros_like(one)))
        parts.append(jnp.concatenate(across, axis=1))
    return jnp.concatenate(parts, axis=0)


class Dense:
    def __init__(self, ref, first_row, first_column):
        self.ref, self.first_row, self.first_column = ref, first_row, first_column

    def rows(self, row_pair, count=1):
        return pl.ds((2 * row_pair - self.first_row) * BS, count * TILE)

    def columns(self, column_pair, count=1):
        return pl.ds((2 * column_pair - self.first_column) * BS, count * TILE)

    def __getitem__(self, at):
        return self.ref[self.rows(at[0]), self.columns(at[1])]

    def __setitem__(self, at, value):
        self.ref[self.rows(at[0]), self.columns(at[1])] = value


def product(left, right, row_pair, column_pair, ks):
    ks = [k for k in sorted(ks) if abs(k - row_pair) <= 2 and abs(k - column_pair) <= 2]
    total = None
    while ks:
        source = right[ks[0]]
        count = 1
        while count < len(ks) and ks[count] == ks[0] + count and right[ks[count]].ref is source.ref:
            count += 1
        part = jnp.dot(
            left.ref[left.rows(row_pair), left.columns(ks[0], count)],
            source.ref[source.rows(ks[0], count), source.columns(column_pair)],
            preferred_element_type=jnp.float32,
        )
        total = part if total is None else total + part
        ks = ks[count:]
    return total


class Step:
    def __init__(self, pairs, low, high, early, late, wanted):
        self.pairs, self.low, self.high, self.early, self.late, self.wanted = pairs, low, high, early, late, wanted

    def columns(self, row_pair):
        return range(max(row_pair - 2, self.low), min(row_pair + 2, self.high) + 1)

    def whole(self, row_pair, column_pair):
        return not any(abs(k - row_pair) <= 2 and abs(k - column_pair) <= 2 for k in self.late)

    def open(self):
        squares = [(p, c) for p in self.pairs for c in self.columns(p) if not self.whole(p, c)]
        cubes = [(p, c) for p in self.pairs for c in self.wanted(p) if self.done(p, c)]
        return {at: i for i, at in enumerate(squares)}, {at: i for i, at in enumerate(cubes)}

    def done(self, row_pair, column_pair):
        return [k for k in self.columns(row_pair) if self.whole(row_pair, k) and abs(k - column_pair) <= 2]

    def first(self, left, right, square, mask_ref, square_part, cube_part):
        squares, cubes = self.open()
        for p in self.pairs:
            for c in self.columns(p):
                value = product(left, right, p, c, self.early)
                if (p, c) in squares:
                    square_part[squares[p, c]] = value
                else:
                    square[p, c] = kept(value, mask_ref, p, c).astype(jnp.bfloat16)
        for (p, c), i in cubes.items():
            cube_part[i] = product(square, right, p, c, self.done(p, c))

    def second(self, left, right, square, ready, mask_ref, square_part, cube_part, write):
        squares, cubes = self.open()
        for (p, c), i in squares.items():
            value = square_part[i] + product(left, right, p, c, self.late)
            square[p, c] = kept(value, mask_ref, p, c).astype(jnp.bfloat16)
        for p in self.pairs:
            for c in self.wanted(p):
                rest = [k for k in self.columns(p) if not self.whole(p, k)]
                cube = product(square, right, p, c, rest)
                if (p, c) in cubes:
                    cube = cube_part[cubes[p, c]] if cube is None else cube_part[cubes[p, c]] + cube
                own = (square if (p, c) in squares else ready)[p, c].astype(jnp.float32)
                write(p, c, (3.0 * own - 2.0 * kept(cube, mask_ref, p, c)).astype(jnp.bfloat16))

    def all(self, left, right, square, mask_ref, write):
        for p in self.pairs:
            for c in self.columns(p):
                value = product(left, right, p, c, self.early)
                square[p, c] = kept(value, mask_ref, p, c).astype(jnp.bfloat16)
        for p in self.pairs:
            for c in self.wanted(p):
                cube = product(square, right, p, c, self.early)
                own = square[p, c].astype(jnp.float32)
                write(p, c, (3.0 * own - 2.0 * kept(cube, mask_ref, p, c)).astype(jnp.bfloat16))


OWN = Step((4, 5), 2, 7, (2, 3, 4, 5, 6, 7), (), lambda p: range(p - 2, p + 3))
LOW = Step((2, 3), 0, 5, (2, 3, 4, 5), (0, 1), lambda p: range(2, p + 3))
LAST = Step((4, 5), 2, 7, (2, 3, 4, 5), (6, 7), lambda p: range(p - 2, p + 3))


def own_rows_kernel(info_ref, place_ref, tiles_ref, own_ref):
    own_ref[...] = jnp.zeros_like(own_ref)
    spread(info_ref, place_ref, (tiles_ref,), 8, own_ref, 4)


def low_first_kernel(info_ref, place_ref, mask_ref, near_ref, own_ref, low_ref, square_ref, square_part, cube_part):
    low_ref[...] = jnp.zeros_like(low_ref)
    spread(info_ref, place_ref, (near_ref,), 4, low_ref, 0)
    low, own = Dense(low_ref, 4, 0), Dense(own_ref, 8, 4)
    LOW.first(low, {2: low, 3: low, 4: own, 5: own}, Dense(square_ref, 4, 8), mask_ref, square_part, cube_part)


def own_kernel(info_ref, place_ref, mask_ref, low_ref, own_ref, other0_ref, other1_ref, next_ref, high_ref, square_ref):
    high_ref[...] = jnp.zeros_like(high_ref)
    spread(info_ref, place_ref, (other0_ref, other1_ref), 12, high_ref, 8)
    low, own, high = Dense(low_ref, 4, 0), Dense(own_ref, 8, 4), Dense(high_ref, 12, 8)
    result = Dense(next_ref, 8, 4)
    next_ref[tile(4, 8), tile(7, 4)] = jnp.zeros((TILE, TILE), jnp.bfloat16)
    next_ref[tile(5, 8), tile(2, 4)] = jnp.zeros((TILE, TILE), jnp.bfloat16)

    def write(p, c, value):
        result[p, c] = value

    OWN.all(own, {2: low, 3: low, 4: own, 5: own, 6: high, 7: high}, Dense(square_ref, 8, 4), mask_ref, write)


def low_second_kernel(mask_ref, far_ref, low_ref, ready_ref, square_part, cube_part, next_ref, sent_ref, far_dense_ref, square_ref):
    for row in range(ROWS):
        for column in range(8):
            if column < row + 5:
                far_dense_ref[block(row), block(column)] = far_ref[start_of(row) + column]
            else:
                far_dense_ref[block(row), block(column)] = jnp.zeros((BS, BS), jnp.bfloat16)
    low, far = Dense(low_ref, 4, 0), Dense(far_dense_ref, 0, 0)
    result = Dense(next_ref, 4, 4)
    next_ref[tile(2, 4), tile(5, 4)] = jnp.zeros((TILE, TILE), jnp.bfloat16)

    def write(p, c, value):
        result[p, c] = value
        for down in range(2):
            for right in range(2):
                row, column = 2 * p + down - 4, 2 * c + right - 4
                if column < row + 5:
                    sent_ref[start_of(row) + column] = value[down * BS:(down + 1) * BS, right * BS:(right + 1) * BS]

    LOW.second(
        low, {0: far, 1: far, 2: low, 3: low}, Dense(square_ref, 4, 0), Dense(ready_ref, 4, 8), mask_ref,
        square_part, cube_part, write,
    )


def last_first_kernel(mask_ref, low_ref, own_ref, square_ref, square_part, cube_part):
    low, own = Dense(low_ref, 4, 4), Dense(own_ref, 8, 4)
    LAST.first(own, {2: low, 3: low, 4: own, 5: own}, Dense(square_ref, 8, 4), mask_ref, square_part, cube_part)


def last_second_kernel(info_ref, place_ref, mask_ref, own_ref, other_ref, ready_ref, square_part, cube_part,
                       out_ref, high_ref, square_ref, dense_ref):
    for row in range(ROWS):
        for column in range(8):
            if column < row + 5:
                high_ref[block(3 - row), block(7 - column)] = other_ref[start_of(row) + column]
            else:
                high_ref[block(3 - row), block(7 - column)] = jnp.zeros((BS, BS), jnp.bfloat16)
    own, high = Dense(own_ref, 8, 4), Dense(high_ref, 12, 8)
    result = Dense(dense_ref, 8, 4)
    empty = dense_ref.shape[1] // BS - 1
    dense_ref[:, block(empty)] = jnp.zeros((ROWS * BS, BS), jnp.bfloat16)

    def write(p, c, value):
        result[p, c] = value

    LAST.second(
        own, {4: own, 5: own, 6: high, 7: high}, Dense(square_ref, 8, 4), Dense(ready_ref, 8, 4), mask_ref,
        square_part, cube_part, write,
    )
    for row in range(ROWS):
        held = local_row(info_ref, row)
        for slot in range(SLOTS):
            where = place_ref[(8 + row) * SLOTS + slot] - 4
            out_ref[held, slot] = dense_ref[block(row), lanes(jnp.minimum(where, empty))]


def call(kernel, scalars, operands, outs, scratch, name, space=pltpu.VMEM, limit=12):
    smem, vmem = pl.BlockSpec(memory_space=pltpu.SMEM), pl.BlockSpec(memory_space=pltpu.VMEM)
    return pl.pallas_call(
        kernel,
        out_shape=outs,
        in_specs=[smem] * len(scalars) + [pl.BlockSpec(memory_space=space)] * len(operands),
        out_specs=[vmem] * len(outs),
        scratch_shapes=scratch,
        compiler_params=pltpu.CompilerParams(vmem_limit_bytes=limit * 2**20),
        cost_estimate=pl.CostEstimate(flops=0, bytes_accessed=0, transcendentals=0),
        name=name,
    )(*scalars, *operands)


def dense(columns, rows=ROWS):
    return jax.ShapeDtypeStruct((rows * BS, columns * BS), jnp.bfloat16)


def partial_sums(step):
    return [jax.ShapeDtypeStruct((len(part), TILE, TILE), jnp.float32) for part in step.open()]


def scratch(columns, rows=ROWS):
    return pltpu.VMEM((rows * BS, columns * BS), jnp.bfloat16)


def per_device(cols, tiles):
    devices = lax.axis_size("dev")
    total = cols.shape[0]
    layer = lax.axis_index("layer")
    base = lax.axis_index("dev") * ROWS + layer * (ROWS - 1)
    sign = 1 - 2 * layer
    info = jnp.stack([base, sign]).astype(jnp.int32)
    axes = ("dev", "layer")

    def shifted(value, step):
        pairs = []
        for i in range(devices):
            pairs.append((2 * i, (i + step) % devices * 2))
            pairs.append((2 * i + 1, (i - step) % devices * 2 + 1))
        return lax.ppermute(value, axes, pairs)

    def swapped(value):
        return lax.ppermute(value, "layer", [(0, 1), (1, 0)])

    near = shifted(tiles, 1)
    packed = jax.ShapeDtypeStruct((PACKED, BS, BS), jnp.bfloat16)
    (packed_rows,) = call(
        pack_kernel, (info,), (cols.T, tiles), [packed],
        [pltpu.SMEM(cols.T.shape, jnp.int32), pltpu.SemaphoreType.DMA], "pack", pltpu.HBM, 56,
    )
    far = shifted(packed_rows, 2)
    rows = (base + sign * (jnp.arange(WINDOW, dtype=jnp.int32) - FAR) + total) % total
    window = jnp.take(cols, rows, axis=0)
    where = (sign * (window - base) + FAR + 2 * total) % total
    where = jnp.where((window < total) & (where < WINDOW), where, WINDOW)
    place = where.reshape(-1)
    pattern = jnp.any(where[:, :, None] == jnp.arange(WINDOW, dtype=jnp.int32), axis=1)
    mask = pattern.astype(jnp.int32).reshape(-1)

    (own,) = call(own_rows_kernel, (info, place), (tiles,), [dense(13)], [], "own_rows")

    near, packed_rows, own, mask = lax.optimization_barrier((near, packed_rows, own, mask))
    other = [swapped(near[:2]), swapped(near[2:])]
    low, ready, *parts = call(
        low_first_kernel, (info, place, mask), (near, own), [dense(13), dense(4), *partial_sums(LOW)], [], "low_first"
    )
    (current,) = call(
        own_kernel, (info, place, mask), (low, own, *other), [dense(12)], [scratch(9), scratch(12)], "own"
    )
    low, current = lax.optimization_barrier((low, current))
    current_low, sent = call(
        low_second_kernel, (mask,), (far, low, ready, *parts), [dense(8), packed], [scratch(8), scratch(12)], "low_second"
    )
    current_other = swapped(sent)
    ready, *parts = call(
        last_first_kernel, (mask,), (current_low, current), [dense(4), *partial_sums(LAST)], [], "last_first"
    )
    (out,) = call(
        last_second_kernel, (info, place, mask), (current, current_other, ready, *parts),
        [jax.ShapeDtypeStruct(tiles.shape, tiles.dtype)], [scratch(8), scratch(12), scratch(13)], "last_second",
    )
    return out


def solution(mesh):
    return jax.shard_map(
        per_device,
        mesh=mesh,
        in_specs=(P("grp", None), P(("grp", "dev"), None, None, None)),
        out_specs=P(("grp", "dev"), None, None, None),
        check_vma=False,
    )
```

time: 180 us -> 43.6 us (0.24)
  waiting for transfers between devices: 93.5 us -> 15.9 us
  local copies, waits for them, and re-layouts: 41.1 us -> 0.99 us
  matrix products: 26.3 us -> 0 us
  Pallas kernels: 0 us -> 18 us
  other arithmetic: 7 us -> 0.86 us
  starting transfers between devices: 10.7 us -> 7.55 us
    ppermute x8 -> x5, waiting for transfers between devices: 93.5 us -> 15.9 us  [the longest x2 15.9 us: shifted(): return lax.ppermute(value, axes, pairs)]
    dot_general x6 -> x0, matrix products: 26.3 us -> none  [the longest x4 14 us: contract(): jnp.einsum('rmab,rmnbc->rnac', jnp.take(left, picked, axis=1), aligned, p...]
    gather x11 -> x1, local copies, waits for them, and re-layouts: 21.2 us -> 0.56 us  [per_device(): window = jnp.take(cols, rows, axis=0)]
    pallas_call x0 -> x7, Pallas kernels: none -> 18 us  [call(): pl.pallas_call(kernel, out_shape=outs, in_specs=[smem] * len(scalars) + [...]
    convert_element_type x3 -> x1, local copies, waits for them, and re-layouts: 16.4 us -> 0.08 us  [per_device(): mask = pattern.astype(jnp.int32).reshape(-1)]
    concatenate x2 -> x0, other arithmetic: 4.06 us -> none  [with_halo(): block = jnp.concatenate([low, block, high], axis=dim)]
    ppermute x8 -> x5, starting transfers between devices: 10.7 us -> 7.55 us  [the longest x2 4.53 us: shifted(): return lax.ppermute(value, axes, pairs)]
    unnamed x11 -> x7, local copies, waits for them, and re-layouts: 2.71 us -> 0.09 us
  transfers between devices with their start and end apart: 8 -> 5, of which waited for: 6 -> 1; matrix products, arithmetic and copies ran while one was open for 5% -> 4% of each run, Pallas kernels for 0% -> 29%
where the time goes in v3:
time: 43.6 us; the launch traced here: 43.4 us
  Pallas kernels  18 us (41%)
  waiting for transfers between devices  15.9 us (36%)
  starting transfers between devices  7.55 us (17%)
  local copies, waits for them, and re-layouts  0.99 us (2%)
  other arithmetic  0.86 us (2%)
    pallas_call x7, Pallas kernels, call(): pl.pallas_call(kernel, out_shape=outs, in_specs=[smem] * len(scalars) + [...  18 us
    ppermute x2, waiting for transfers between devices, shifted(): return lax.ppermute(value, axes, pairs)  15.9 us
    ppermute x2, starting transfers between devices, shifted(): return lax.ppermute(value, axes, pairs)  4.53 us
    ppermute x3, starting transfers between devices, swapped(): return lax.ppermute(value, 'layer', [(0, 1), (1, 0)])  3.02 us
  transfers between devices with their start and end apart: 5, of which 1 were waited for; matrix products, arithmetic and copies ran while one was open for 4% of the time, Pallas kernels for 29%

profile of v3, /device:TPU:0, one launch (start us, length us, event | category | flops | bytes accessed | tf_op | source)
XLA Modules:
  0.0 43.4 jit_solution(6874014569572502435)
XLA Ops:
  0.0 0.0 copy-start
  0.0 0.0 copy-start.2
  0.0 2.9 %collective-permute-start = (bf16[4,8,128,128]{3,2,1,0:T(8,128)(2,1)}, bf16[4,8,128,128]{3,2,1,0:T(8,128)(2,1)S(1)}, u32[]{:S(2)}, u32[]{:S(2)}) collective-permute-start(bf16[4,8,128,128]{3,2,1,0:T(8,128)(2,1)} %tiles_ref.3), channel_id=1, source_target_pairs={{0,2},{1,15},{2,4},{3,1},{4,6},{5,3},{6,8},{7,5},{8,10},{9,7},{10,... | collective-permute-start | bytes 3145736 | tf_op jit(solution)/shard_map/ppermute | solution.py:308
  2.9 0.6 %pad_add_fusion.info_ref = s32[2]{0:T(128)} fusion(s32[1]{0:T(128)} %bitcast.1, s32[1]{0:T(128)} %bitcast), kind=kLoop, calls=%fused_computation.28 | loop fusion | flops 2 | bytes 16 | tf_op jit(solution)/shard_map/stack | solution.py:300
  3.6 0.0 copy-start.1
  3.6 3.5 %pack.1 = bf16[26,128,128]{2,1,0:T(8,128)(2,1)} custom-call(s32[2]{0:T(128)} %pad_add_fusion.info_ref, s32[8,32]{1,0:T(8,128)} %bitcast.5, bf16[4,8,128,128]{3,2,1,0:T(8,128)(2,1)} %tiles_ref.3), custom_call_target="tpu_custom_call" | custom-call | tf_op jit(solution)/shard_map/pack/pallas_call | solution.py:270
  7.1 1.6 %collective-permute-start.3 = (bf16[26,128,128]{2,1,0:T(8,128)(2,1)}, bf16[26,128,128]{2,1,0:T(8,128)(2,1)S(1)}, u32[]{:S(2)}, u32[]{:S(2)}) collective-permute-start(bf16[26,128,128]{2,1,0:T(8,128)(2,1)} %pack.1), channel_id=1, source_target_pairs={{0,4},{1,13},{2,6},{3,15},{4,8},{5,1},{6,10},{7,3},{8,12},{9,5},{1... | collective-permute-start | bytes 2555912 | tf_op jit(solution)/shard_map/ppermute | solution.py:308
  8.7 0.0 copy-done.2
  8.7 0.1 copy.5
  8.8 0.6 %gather_fusion = s32[16,8]{1,0:T(8,128)S(1)} fusion(s32[32,8]{1,0:T(8,128)S(1)} %copy.5, s32[1024]{0:T(1024)S(1)} %pad_clamp_fusion), kind=kCustom, calls=%fused_computation | custom fusion | bytes 1088 | tf_op jit(solution)/shard_map/jit(_take)/gather | solution.py:321
  9.4 0.1 and_select_fusion
  9.5 0.1 add.122
  9.6 0.1 lt.68
  9.7 0.1 fusion
  9.8 0.1 reshape.114.mask_ref
  9.9 0.0 copy-done
  9.9 0.0 copy-done.1
  9.9 0.9 %own_rows.1.own_ref = bf16[512,1664]{1,0:T(8,128)(2,1)S(1)} custom-call(s32[2]{0:T(128)S(1)} %copy-done.1, s32[128]{0:T(128)S(1)} %and_select_fusion.1.place_ref, bf16[4,8,128,128]{3,2,1,0:T(8,128)(2,1)S(1)} %copy-done), custom_call_target="tpu_custom_call" | custom-call | tf_op jit(solution)/shard_map/own_rows/pallas_call | solution.py:270
  10.7 15.9 %collective-permute-done.near_ref = bf16[4,8,128,128]{3,2,1,0:T(8,128)(2,1)S(1)} collective-permute-done((bf16[4,8,128,128]{3,2,1,0:T(8,128)(2,1)}, bf16[4,8,128,128]{3,2,1,0:T(8,128)(2,1)S(1)}, u32[]{:S(2)}, u32[]{:S(2)}) %collective-permute-start) | collective-permute-done | bytes 1048608 | tf_op jit(solution)/shard_map/ppermute | solution.py:308
  26.6 0.1 fusion.6
  26.7 0.1 collective-permute-start.2
  26.8 0.5 %collective-permute-start.1 = (bf16[2,8,128,128]{3,2,1,0:T(8,128)(2,1)S(1)}, bf16[2,8,128,128]{3,2,1,0:T(8,128)(2,1)S(1)}, u32[]{:S(2)}, u32[]{:S(2)}) collective-permute-start(bf16[2,8,128,128]{3,2,1,0:T(8,128)(2,1)S(1)} %get-tuple-element.37), channel_id=1, source_target_pairs={{0,1},{1,0},{2,3},{3,2},{4,5},{5,4},{6,7},{7,6},{8,9},{9,8},{10,11... | collective-permute-start | bytes 1572872 | tf_op jit(solution)/shard_map/ppermute | solution.py:311
  27.3 2.3 %low_first.1 = (bf16[512,1664]{1,0:T(8,128)(2,1)S(1)}, bf16[512,512]{1,0:T(8,128)(2,1)S(1)}, f32[7,256,256]{2,1,0:T(8,128)S(1)}, f32[7,256,256]{2,1,0:T(8,128)S(1)}) custom-call(s32[2]{0:T(128)S(1)} %copy-done.1, s32[128]{0:T(128)S(1)} %and_select_fusion.1.place_ref, s32[256]{0:T(256)S(1)} %reshape.114.mask_ref, ...), custom_call_target="tpu_custom_call" | custom-call | tf_op jit(solution)/shard_map/low_first/pallas_call | solution.py:270
  29.6 0.0 collective-permute-done.2.other1_ref
  29.6 0.0 collective-permute-done.1.other0_ref
  29.6 3.8 %own.1.own_ref = bf16[512,1536]{1,0:T(8,128)(2,1)S(1)} custom-call(s32[2]{0:T(128)S(1)} %copy-done.1, s32[128]{0:T(128)S(1)} %and_select_fusion.1.place_ref, s32[256]{0:T(256)S(1)} %reshape.114.mask_ref, bf16[512,1664]{1,0:T(8,128)(2,1)S(1)} %get-tuple-element.24.low_ref, bf16[512,1664]{1,0:T(8,128)(2,1)S(1)} %own_rows.1.own_ref, ...), custom_call_target="tpu_custom_call" | custom-call | tf_op jit(solution)/shard_map/own/pallas_call | solution.py:270
  33.5 0.0 collective-permute-done.3.far_ref
  33.5 1.9 %low_second.1 = (bf16[512,1024]{1,0:T(8,128)(2,1)S(1)}, bf16[26,128,128]{2,1,0:T(8,128)(2,1)S(1)}) custom-call(s32[256]{0:T(256)S(1)} %reshape.114.mask_ref, bf16[26,128,128]{2,1,0:T(8,128)(2,1)S(1)} %collective-permute-done.3.far_ref, bf16[512,1664]{1,0:T(8,128)(2,1)S(1)} %get-tuple-element.24.low_ref, bf16[512,512]{1,0:T(8,128)(2,1)S(1)} %get-tuple-element.25.ready_ref, ...), custom_call_target="tpu_custom_call" | custom-call | tf_op jit(solution)/shard_map/low_second/pallas_call | solution.py:270
  35.4 2.5 %collective-permute-start.4 = (bf16[26,128,128]{2,1,0:T(8,128)(2,1)S(1)}, bf16[26,128,128]{2,1,0:T(8,128)(2,1)S(1)}, u32[]{:S(2)}, u32[]{:S(2)}) collective-permute-start(bf16[26,128,128]{2,1,0:T(8,128)(2,1)S(1)} %get-tuple-element.28), channel_id=1, source_target_pairs={{0,1},{1,0},{2,3},{3,2},{4,5},{5,4},{6,7},{7,6},{8,9},{9,8},{10,11... | collective-permute-start | bytes 2555912 | tf_op jit(solution)/shard_map/ppermute | solution.py:311
  37.8 2.0 %last_first.1 = (bf16[512,512]{1,0:T(8,128)(2,1)S(1)}, f32[7,256,256]{2,1,0:T(8,128)S(1)}, f32[7,256,256]{2,1,0:T(8,128)S(1)}) custom-call(s32[256]{0:T(256)S(1)} %reshape.114.mask_ref, bf16[512,1024]{1,0:T(8,128)(2,1)S(1)} %get-tuple-element.29.low_ref, bf16[512,1536]{1,0:T(8,128)(2,1)S(1)} %own.1.own_ref), custom_call_target="tpu_custom_call" | custom-call | tf_op jit(solution)/shard_map/last_first/pallas_call | solution.py:270
  39.8 0.0 collective-permute-done.4.other_ref
  39.9 3.5 %last_second.1 = bf16[4,8,128,128]{3,2,1,0:T(8,128)(2,1)} custom-call(s32[2]{0:T(128)S(1)} %copy-done.1, s32[128]{0:T(128)S(1)} %and_select_fusion.1.place_ref, s32[256]{0:T(256)S(1)} %reshape.114.mask_ref, bf16[512,1536]{1,0:T(8,128)(2,1)S(1)} %own.1.own_ref, bf16[26,128,128]{2,1,0:T(8,128)(2,1)S(1)} %collective-permute-done.4.other_ref, ...), custom_call_target="tpu_custom_call" | custom-call | tf_op jit(solution)/shard_map/last_second/pallas_call | solution.py:270
  (5 shorter events, 0.1 us)
Async XLA Ops:
  0.0 9.9 %copy-start = (bf16[4,8,128,128]{3,2,1,0:T(8,128)(2,1)S(1)}, bf16[4,8,128,128]{3,2,1,0:T(8,128)(2,1)}, u32[]{:S(2)}) copy-start(bf16[4,8,128,128]{3,2,1,0:T(8,128)(2,1)} %tiles_ref.3) | copy-start | bytes 3145732
  0.0 8.7 %copy-start.2 = (s32[32,8]{0,1:T(8,128)S(1)}, s32[32,8]{0,1:T(8,128)}, u32[]{:S(2)}) copy-start(s32[32,8]{0,1:T(8,128)} %param.2) | copy-start | bytes 3076
  0.0 26.6 %collective-permute-start = (bf16[4,8,128,128]{3,2,1,0:T(8,128)(2,1)}, bf16[4,8,128,128]{3,2,1,0:T(8,128)(2,1)S(1)}, u32[]{:S(2)}, u32[]{:S(2)}) collective-permute-start(bf16[4,8,128,128]{3,2,1,0:T(8,128)(2,1)} %tiles_ref.3), channel_id=1, source_target_pairs={{0,2},{1,15},{2,4},{3,1},{4,6},{5,3},{6,8},{7,5},{8,10},{9,7},{10,... | collective-permute-start | bytes 3145736 | tf_op jit(solution)/shard_map/ppermute | solution.py:308
  3.6 6.3 %copy-start.1 = (s32[2]{0:T(128)S(1)}, s32[2]{0:T(128)}, u32[]{:S(2)}) copy-start(s32[2]{0:T(128)} %pad_add_fusion.info_ref) | copy-start | bytes 28
  7.1 26.4 %collective-permute-start.3 = (bf16[26,128,128]{2,1,0:T(8,128)(2,1)}, bf16[26,128,128]{2,1,0:T(8,128)(2,1)S(1)}, u32[]{:S(2)}, u32[]{:S(2)}) collective-permute-start(bf16[26,128,128]{2,1,0:T(8,128)(2,1)} %pack.1), channel_id=1, source_target_pairs={{0,4},{1,13},{2,6},{3,15},{4,8},{5,1},{6,10},{7,3},{8,12},{9,5},{1... | collective-permute-start | bytes 2555912 | tf_op jit(solution)/shard_map/ppermute | solution.py:308
  26.7 2.9 %collective-permute-start.2 = (bf16[2,8,128,128]{3,2,1,0:T(8,128)(2,1)S(1)}, bf16[2,8,128,128]{3,2,1,0:T(8,128)(2,1)S(1)}, u32[]{:S(2)}, u32[]{:S(2)}) collective-permute-start(bf16[2,8,128,128]{3,2,1,0:T(8,128)(2,1)S(1)} %get-tuple-element.36), channel_id=1, source_target_pairs={{0,1},{1,0},{2,3},{3,2},{4,5},{5,4},{6,7},{7,6},{8,9},{9,8},{10,11... | collective-permute-start | bytes 1572872 | tf_op jit(solution)/shard_map/ppermute | solution.py:311
  26.8 2.8 %collective-permute-start.1 = (bf16[2,8,128,128]{3,2,1,0:T(8,128)(2,1)S(1)}, bf16[2,8,128,128]{3,2,1,0:T(8,128)(2,1)S(1)}, u32[]{:S(2)}, u32[]{:S(2)}) collective-permute-start(bf16[2,8,128,128]{3,2,1,0:T(8,128)(2,1)S(1)} %get-tuple-element.37), channel_id=1, source_target_pairs={{0,1},{1,0},{2,3},{3,2},{4,5},{5,4},{6,7},{7,6},{8,9},{9,8},{10,11... | collective-permute-start | bytes 1572872 | tf_op jit(solution)/shard_map/ppermute | solution.py:311
  35.4 4.5 %collective-permute-start.4 = (bf16[26,128,128]{2,1,0:T(8,128)(2,1)S(1)}, bf16[26,128,128]{2,1,0:T(8,128)(2,1)S(1)}, u32[]{:S(2)}, u32[]{:S(2)}) collective-permute-start(bf16[26,128,128]{2,1,0:T(8,128)(2,1)S(1)} %get-tuple-element.28), channel_id=1, source_target_pairs={{0,1},{1,0},{2,3},{3,2},{4,5},{5,4},{6,7},{7,6},{8,9},{9,8},{10,11... | collective-permute-start | bytes 2555912 | tf_op jit(solution)/shard_map/ppermute | solution.py:311

commit v4 on v3

--- a/solution.py
+++ b/solution.py
@@ -151,7 +151,7 @@
         for (p, c), i in cubes.items():
             cube_part[i] = product(square, right, p, c, self.done(p, c))
 
-    def second(self, left, right, square, ready, mask_ref, square_part, cube_part, write):
+    def second(self, left, right, square, ready, mask_ref, square_part, cube_part, write, finish=lambda p: None):
         squares, cubes = self.open()
         for (p, c), i in squares.items():
             value = square_part[i] + product(left, right, p, c, self.late)
@@ -164,6 +164,7 @@
                     cube = cube_part[cubes[p, c]] if cube is None else cube_part[cubes[p, c]] + cube
                 own = (square if (p, c) in squares else ready)[p, c].astype(jnp.float32)
                 write(p, c, (3.0 * own - 2.0 * kept(cube, mask_ref, p, c)).astype(jnp.bfloat16))
+            finish(p)
 
     def all(self, left, right, square, mask_ref, write):
         for p in self.pairs:
@@ -208,7 +209,7 @@
     OWN.all(own, {2: low, 3: low, 4: own, 5: own, 6: high, 7: high}, Dense(square_ref, 8, 4), mask_ref, write)
 
 
-def low_second_kernel(mask_ref, far_ref, low_ref, ready_ref, square_part, cube_part, next_ref, sent_ref, far_dense_ref, square_ref):
+def low_second_kernel(mask_ref, far_ref, low_ref, ready_ref, square_part, cube_part, sent_ref, far_dense_ref, square_ref):
     for row in range(ROWS):
         for column in range(8):
             if column < row + 5:
@@ -216,11 +217,8 @@
             else:
                 far_dense_ref[block(row), block(column)] = jnp.zeros((BS, BS), jnp.bfloat16)
     low, far = Dense(low_ref, 4, 0), Dense(far_dense_ref, 0, 0)
-    result = Dense(next_ref, 4, 4)
-    next_ref[tile(2, 4), tile(5, 4)] = jnp.zeros((TILE, TILE), jnp.bfloat16)
 
     def write(p, c, value):
-        result[p, c] = value
         for down in range(2):
             for right in range(2):
                 row, column = 2 * p + down - 4, 2 * c + right - 4
@@ -233,13 +231,19 @@
     )
 
 
-def last_first_kernel(mask_ref, low_ref, own_ref, square_ref, square_part, cube_part):
+def last_first_kernel(mask_ref, sent_ref, own_ref, square_ref, square_part, cube_part, low_ref):
+    for row in range(ROWS):
+        for column in range(8):
+            if column < row + 5:
+                low_ref[block(row), block(column)] = sent_ref[start_of(row) + column]
+            else:
+                low_ref[block(row), block(column)] = jnp.zeros((BS, BS), jnp.bfloat16)
     low, own = Dense(low_ref, 4, 4), Dense(own_ref, 8, 4)
     LAST.first(own, {2: low, 3: low, 4: own, 5: own}, Dense(square_ref, 8, 4), mask_ref, square_part, cube_part)
 
 
 def last_second_kernel(info_ref, place_ref, mask_ref, own_ref, other_ref, ready_ref, square_part, cube_part,
-                       out_ref, high_ref, square_ref, dense_ref):
+                       out_ref, high_ref, square_ref, dense_ref, rows_ref, sems):
     for row in range(ROWS):
         for column in range(8):
             if column < row + 5:
@@ -254,24 +258,31 @@
     def write(p, c, value):
         result[p, c] = value
 
+    copies = []
+
+    def finish(p):
+        for row in (2 * p - 8, 2 * p - 7):
+            for slot in range(SLOTS):
+                where = place_ref[(8 + row) * SLOTS + slot] - 4
+                rows_ref[row, slot] = dense_ref[block(row), lanes(jnp.minimum(where, empty))]
+            copies.append(pltpu.make_async_copy(rows_ref.at[row], out_ref.at[local_row(info_ref, row)], sems.at[row]))
+            copies[-1].start()
+
     LAST.second(
         own, {4: own, 5: own, 6: high, 7: high}, Dense(square_ref, 8, 4), Dense(ready_ref, 8, 4), mask_ref,
-        square_part, cube_part, write,
-    )
-    for row in range(ROWS):
-        held = local_row(info_ref, row)
-        for slot in range(SLOTS):
-            where = place_ref[(8 + row) * SLOTS + slot] - 4
-            out_ref[held, slot] = dense_ref[block(row), lanes(jnp.minimum(where, empty))]
-
-
-def call(kernel, scalars, operands, outs, scratch, name, space=pltpu.VMEM, limit=12):
+        square_part, cube_part, write, finish,
+    )
+    for copy in copies:
+        copy.wait()
+
+
+def call(kernel, scalars, operands, outs, scratch, name, space=pltpu.VMEM, limit=12, out_space=pltpu.VMEM):
     smem, vmem = pl.BlockSpec(memory_space=pltpu.SMEM), pl.BlockSpec(memory_space=pltpu.VMEM)
     return pl.pallas_call(
         kernel,
         out_shape=outs,
         in_specs=[smem] * len(scalars) + [pl.BlockSpec(memory_space=space)] * len(operands),
-        out_specs=[vmem] * len(outs),
+        out_specs=[pl.BlockSpec(memory_space=out_space)] * len(outs),
         scratch_shapes=scratch,
         compiler_params=pltpu.CompilerParams(vmem_limit_bytes=limit * 2**20),
         cost_estimate=pl.CostEstimate(flops=0, bytes_accessed=0, transcendentals=0),
@@ -336,16 +347,18 @@
         own_kernel, (info, place, mask), (low, own, *other), [dense(12)], [scratch(9), scratch(12)], "own"
     )
     low, current = lax.optimization_barrier((low, current))
-    current_low, sent = call(
-        low_second_kernel, (mask,), (far, low, ready, *parts), [dense(8), packed], [scratch(8), scratch(12)], "low_second"
+    (sent,) = call(
+        low_second_kernel, (mask,), (far, low, ready, *parts), [packed], [scratch(8), scratch(12)], "low_second"
     )
     current_other = swapped(sent)
     ready, *parts = call(
-        last_first_kernel, (mask,), (current_low, current), [dense(4), *partial_sums(LAST)], [], "last_first"
+        last_first_kernel, (mask,), (sent, current), [dense(4), *partial_sums(LAST)], [scratch(8)], "last_first"
     )
     (out,) = call(
         last_second_kernel, (info, place, mask), (current, current_other, ready, *parts),
-        [jax.ShapeDtypeStruct(tiles.shape, tiles.dtype)], [scratch(8), scratch(12), scratch(13)], "last_second",
+        [jax.ShapeDtypeStruct(tiles.shape, tiles.dtype)], [scratch(8), scratch(12), scratch(13),
+         pltpu.VMEM(tiles.shape, tiles.dtype), pltpu.SemaphoreType.DMA((ROWS,))],
+        "last_second", out_space=pltpu.HBM,
     )
     return out
 

time: 43.6 us -> 43.4 us (level)
  no operation moved by 1% of the time
where the time goes in v4:
time: 43.4 us; the launch traced here: 43.1 us
  Pallas kernels  17.6 us (41%)
  waiting for transfers between devices  15.7 us (36%)
  starting transfers between devices  7.74 us (18%)
  local copies, waits for them, and re-layouts  1.01 us (2%)
  other arithmetic  0.9 us (2%)
    pallas_call x7, Pallas kernels, call(): pl.pallas_call(kernel, out_shape=outs, in_specs=[smem] * len(scalars) + [...  17.6 us
    ppermute x2, waiting for transfers between devices, shifted(): return lax.ppermute(value, axes, pairs)  15.7 us
    ppermute x2, starting transfers between devices, shifted(): return lax.ppermute(value, axes, pairs)  4.58 us
    ppermute x3, starting transfers between devices, swapped(): return lax.ppermute(value, 'layer', [(0, 1), (1, 0)])  3.16 us
  transfers between devices with their start and end apart: 5, of which 1 were waited for; matrix products, arithmetic and copies ran while one was open for 4% of the time, Pallas kernels for 29%

profile of v4, /device:TPU:0, one launch (start us, length us, event | category | flops | bytes accessed | tf_op | source)
XLA Modules:
  0.0 43.1 jit_solution(8050684798177848273)
XLA Ops:
  0.0 0.0 copy-start
  0.0 0.0 copy-start.2
  0.0 2.9 %collective-permute-start = (bf16[4,8,128,128]{3,2,1,0:T(8,128)(2,1)}, bf16[4,8,128,128]{3,2,1,0:T(8,128)(2,1)S(1)}, u32[]{:S(2)}, u32[]{:S(2)}) collective-permute-start(bf16[4,8,128,128]{3,2,1,0:T(8,128)(2,1)} %tiles_ref.3), channel_id=1, source_target_pairs={{0,2},{1,15},{2,4},{3,1},{4,6},{5,3},{6,8},{7,5},{8,10},{9,7},{10,... | collective-permute-start | bytes 3145736 | tf_op jit(solution)/shard_map/ppermute | solution.py:319
  2.9 0.6 %pad_add_fusion.info_ref = s32[2]{0:T(128)} fusion(s32[1]{0:T(128)} %bitcast.1, s32[1]{0:T(128)} %bitcast), kind=kLoop, calls=%fused_computation.28 | loop fusion | flops 2 | bytes 16 | tf_op jit(solution)/shard_map/stack | solution.py:311
  3.6 0.0 copy-start.1
  3.6 3.6 %pack.1 = bf16[26,128,128]{2,1,0:T(8,128)(2,1)} custom-call(s32[2]{0:T(128)} %pad_add_fusion.info_ref, s32[8,32]{1,0:T(8,128)} %bitcast.5, bf16[4,8,128,128]{3,2,1,0:T(8,128)(2,1)} %tiles_ref.3), custom_call_target="tpu_custom_call" | custom-call | tf_op jit(solution)/shard_map/pack/pallas_call | solution.py:281
  7.2 1.6 %collective-permute-start.3 = (bf16[26,128,128]{2,1,0:T(8,128)(2,1)}, bf16[26,128,128]{2,1,0:T(8,128)(2,1)S(1)}, u32[]{:S(2)}, u32[]{:S(2)}) collective-permute-start(bf16[26,128,128]{2,1,0:T(8,128)(2,1)} %pack.1), channel_id=1, source_target_pairs={{0,4},{1,13},{2,6},{3,15},{4,8},{5,1},{6,10},{7,3},{8,12},{9,5},{1... | collective-permute-start | bytes 2555912 | tf_op jit(solution)/shard_map/ppermute | solution.py:319
  8.8 0.0 copy-done.2
  8.8 0.1 copy.5
  8.9 0.6 %gather_fusion = s32[16,8]{1,0:T(8,128)S(1)} fusion(s32[32,8]{1,0:T(8,128)S(1)} %copy.5, s32[1024]{0:T(1024)S(1)} %pad_clamp_fusion), kind=kCustom, calls=%fused_computation | custom fusion | bytes 1088 | tf_op jit(solution)/shard_map/jit(_take)/gather | solution.py:332
  9.5 0.1 and_select_fusion
  9.6 0.1 add.122
  9.7 0.1 lt.68
  9.8 0.1 fusion
  9.9 0.1 reshape.114.mask_ref
  10.0 0.0 copy-done
  10.0 0.0 copy-done.1
  10.0 0.9 %own_rows.1.own_ref = bf16[512,1664]{1,0:T(8,128)(2,1)S(1)} custom-call(s32[2]{0:T(128)S(1)} %copy-done.1, s32[128]{0:T(128)S(1)} %and_select_fusion.1.place_ref, bf16[4,8,128,128]{3,2,1,0:T(8,128)(2,1)S(1)} %copy-done), custom_call_target="tpu_custom_call" | custom-call | tf_op jit(solution)/shard_map/own_rows/pallas_call | solution.py:281
  10.9 15.7 %collective-permute-done.near_ref = bf16[4,8,128,128]{3,2,1,0:T(8,128)(2,1)S(1)} collective-permute-done((bf16[4,8,128,128]{3,2,1,0:T(8,128)(2,1)}, bf16[4,8,128,128]{3,2,1,0:T(8,128)(2,1)S(1)}, u32[]{:S(2)}, u32[]{:S(2)}) %collective-permute-start) | collective-permute-done | bytes 1048608 | tf_op jit(solution)/shard_map/ppermute | solution.py:319
  26.6 0.1 fusion.6
  26.7 0.1 collective-permute-start.2
  26.8 0.5 %collective-permute-start.1 = (bf16[2,8,128,128]{3,2,1,0:T(8,128)(2,1)S(1)}, bf16[2,8,128,128]{3,2,1,0:T(8,128)(2,1)S(1)}, u32[]{:S(2)}, u32[]{:S(2)}) collective-permute-start(bf16[2,8,128,128]{3,2,1,0:T(8,128)(2,1)S(1)} %get-tuple-element.33), channel_id=1, source_target_pairs={{0,1},{1,0},{2,3},{3,2},{4,5},{5,4},{6,7},{7,6},{8,9},{9,8},{10,11... | collective-permute-start | bytes 1572872 | tf_op jit(solution)/shard_map/ppermute | solution.py:322
  27.3 2.3 %low_first.1 = (bf16[512,1664]{1,0:T(8,128)(2,1)S(1)}, bf16[512,512]{1,0:T(8,128)(2,1)S(1)}, f32[7,256,256]{2,1,0:T(8,128)S(1)}, f32[7,256,256]{2,1,0:T(8,128)S(1)}) custom-call(s32[2]{0:T(128)S(1)} %copy-done.1, s32[128]{0:T(128)S(1)} %and_select_fusion.1.place_ref, s32[256]{0:T(256)S(1)} %reshape.114.mask_ref, ...), custom_call_target="tpu_custom_call" | custom-call | tf_op jit(solution)/shard_map/low_first/pallas_call | solution.py:281
  29.6 0.0 collective-permute-done.2.other1_ref
  29.6 0.0 collective-permute-done.1.other0_ref
  29.6 3.7 %own.1.own_ref = bf16[512,1536]{1,0:T(8,128)(2,1)S(1)} custom-call(s32[2]{0:T(128)S(1)} %copy-done.1, s32[128]{0:T(128)S(1)} %and_select_fusion.1.place_ref, s32[256]{0:T(256)S(1)} %reshape.114.mask_ref, bf16[512,1664]{1,0:T(8,128)(2,1)S(1)} %get-tuple-element.22.low_ref, bf16[512,1664]{1,0:T(8,128)(2,1)S(1)} %own_rows.1.own_ref, ...), custom_call_target="tpu_custom_call" | custom-call | tf_op jit(solution)/shard_map/own/pallas_call | solution.py:281
  33.3 0.0 collective-permute-done.3.far_ref
  33.3 1.8 %low_second.1.sent_ref = bf16[26,128,128]{2,1,0:T(8,128)(2,1)S(1)} custom-call(s32[256]{0:T(256)S(1)} %reshape.114.mask_ref, bf16[26,128,128]{2,1,0:T(8,128)(2,1)S(1)} %collective-permute-done.3.far_ref, bf16[512,1664]{1,0:T(8,128)(2,1)S(1)} %get-tuple-element.22.low_ref, bf16[512,512]{1,0:T(8,128)(2,1)S(1)} %get-tuple-element.23.ready_ref, ...), custom_call_target="tpu_custom_call" | custom-call | tf_op jit(solution)/shard_map/low_second/pallas_call | solution.py:281
  35.1 2.6 %collective-permute-start.4 = (bf16[26,128,128]{2,1,0:T(8,128)(2,1)S(1)}, bf16[26,128,128]{2,1,0:T(8,128)(2,1)S(1)}, u32[]{:S(2)}, u32[]{:S(2)}) collective-permute-start(bf16[26,128,128]{2,1,0:T(8,128)(2,1)S(1)} %low_second.1.sent_ref), channel_id=1, source_target_pairs={{0,1},{1,0},{2,3},{3,2},{4,5},{5,4},{6,7},{7,6},{8,9},{9,8},{10,11... | collective-permute-start | bytes 2555912 | tf_op jit(solution)/shard_map/ppermute | solution.py:322
  37.7 2.1 %last_first.1 = (bf16[512,512]{1,0:T(8,128)(2,1)S(1)}, f32[7,256,256]{2,1,0:T(8,128)S(1)}, f32[7,256,256]{2,1,0:T(8,128)S(1)}) custom-call(s32[256]{0:T(256)S(1)} %reshape.114.mask_ref, bf16[26,128,128]{2,1,0:T(8,128)(2,1)S(1)} %low_second.1.sent_ref, bf16[512,1536]{1,0:T(8,128)(2,1)S(1)} %own.1.own_ref), custom_call_target="tpu_custom_call" | custom-call | tf_op jit(solution)/shard_map/last_first/pallas_call | solution.py:281
  39.8 0.0 collective-permute-done.4.other_ref
  39.8 3.3 %last_second.1 = bf16[4,8,128,128]{3,2,1,0:T(8,128)(2,1)} custom-call(s32[2]{0:T(128)S(1)} %copy-done.1, s32[128]{0:T(128)S(1)} %and_select_fusion.1.place_ref, s32[256]{0:T(256)S(1)} %reshape.114.mask_ref, bf16[512,1536]{1,0:T(8,128)(2,1)S(1)} %own.1.own_ref, bf16[26,128,128]{2,1,0:T(8,128)(2,1)S(1)} %collective-permute-done.4.other_ref, ...), custom_call_target="tpu_custom_call" | custom-call | tf_op jit(solution)/shard_map/last_second/pallas_call | solution.py:281
  (5 shorter events, 0.1 us)
Async XLA Ops:
  0.0 10.0 %copy-start = (bf16[4,8,128,128]{3,2,1,0:T(8,128)(2,1)S(1)}, bf16[4,8,128,128]{3,2,1,0:T(8,128)(2,1)}, u32[]{:S(2)}) copy-start(bf16[4,8,128,128]{3,2,1,0:T(8,128)(2,1)} %tiles_ref.3) | copy-start | bytes 3145732
  0.0 8.8 %copy-start.2 = (s32[32,8]{0,1:T(8,128)S(1)}, s32[32,8]{0,1:T(8,128)}, u32[]{:S(2)}) copy-start(s32[32,8]{0,1:T(8,128)} %param.2) | copy-start | bytes 3076
  0.0 26.6 %collective-permute-start = (bf16[4,8,128,128]{3,2,1,0:T(8,128)(2,1)}, bf16[4,8,128,128]{3,2,1,0:T(8,128)(2,1)S(1)}, u32[]{:S(2)}, u32[]{:S(2)}) collective-permute-start(bf16[4,8,128,128]{3,2,1,0:T(8,128)(2,1)} %tiles_ref.3), channel_id=1, source_target_pairs={{0,2},{1,15},{2,4},{3,1},{4,6},{5,3},{6,8},{7,5},{8,10},{9,7},{10,... | collective-permute-start | bytes 3145736 | tf_op jit(solution)/shard_map/ppermute | solution.py:319
  3.6 6.4 %copy-start.1 = (s32[2]{0:T(128)S(1)}, s32[2]{0:T(128)}, u32[]{:S(2)}) copy-start(s32[2]{0:T(128)} %pad_add_fusion.info_ref) | copy-start | bytes 28
  7.2 26.2 %collective-permute-start.3 = (bf16[26,128,128]{2,1,0:T(8,128)(2,1)}, bf16[26,128,128]{2,1,0:T(8,128)(2,1)S(1)}, u32[]{:S(2)}, u32[]{:S(2)}) collective-permute-start(bf16[26,128,128]{2,1,0:T(8,128)(2,1)} %pack.1), channel_id=1, source_target_pairs={{0,4},{1,13},{2,6},{3,15},{4,8},{5,1},{6,10},{7,3},{8,12},{9,5},{1... | collective-permute-start | bytes 2555912 | tf_op jit(solution)/shard_map/ppermute | solution.py:319
  26.7 2.9 %collective-permute-start.2 = (bf16[2,8,128,128]{3,2,1,0:T(8,128)(2,1)S(1)}, bf16[2,8,128,128]{3,2,1,0:T(8,128)(2,1)S(1)}, u32[]{:S(2)}, u32[]{:S(2)}) collective-permute-start(bf16[2,8,128,128]{3,2,1,0:T(8,128)(2,1)S(1)} %get-tuple-element.32), channel_id=1, source_target_pairs={{0,1},{1,0},{2,3},{3,2},{4,5},{5,4},{6,7},{7,6},{8,9},{9,8},{10,11... | collective-permute-start | bytes 1572872 | tf_op jit(solution)/shard_map/ppermute | solution.py:322
  26.8 2.8 %collective-permute-start.1 = (bf16[2,8,128,128]{3,2,1,0:T(8,128)(2,1)S(1)}, bf16[2,8,128,128]{3,2,1,0:T(8,128)(2,1)S(1)}, u32[]{:S(2)}, u32[]{:S(2)}) collective-permute-start(bf16[2,8,128,128]{3,2,1,0:T(8,128)(2,1)S(1)} %get-tuple-element.33), channel_id=1, source_target_pairs={{0,1},{1,0},{2,3},{3,2},{4,5},{5,4},{6,7},{7,6},{8,9},{9,8},{10,11... | collective-permute-start | bytes 1572872 | tf_op jit(solution)/shard_map/ppermute | solution.py:322
  35.1 4.7 %collective-permute-start.4 = (bf16[26,128,128]{2,1,0:T(8,128)(2,1)S(1)}, bf16[26,128,128]{2,1,0:T(8,128)(2,1)S(1)}, u32[]{:S(2)}, u32[]{:S(2)}) collective-permute-start(bf16[26,128,128]{2,1,0:T(8,128)(2,1)S(1)} %low_second.1.sent_ref), channel_id=1, source_target_pairs={{0,1},{1,0},{2,3},{3,2},{4,5},{5,4},{6,7},{7,6},{8,9},{9,8},{10,11... | collective-permute-start | bytes 2555912 | tf_op jit(solution)/shard_map/ppermute | solution.py:322

commit v5 on v4

--- a/solution.py
+++ b/solution.py
@@ -242,8 +242,8 @@
     LAST.first(own, {2: low, 3: low, 4: own, 5: own}, Dense(square_ref, 8, 4), mask_ref, square_part, cube_part)
 
 
-def last_second_kernel(info_ref, place_ref, mask_ref, own_ref, other_ref, ready_ref, square_part, cube_part,
-                       out_ref, high_ref, square_ref, dense_ref, rows_ref, sems):
+def last_second_kernel(info_ref, place_ref, slot_ref, mask_ref, own_ref, other_ref, ready_ref, square_part, cube_part,
+                       out_ref, high_ref, square_ref, dense_ref, empty_ref, sem):
     for row in range(ROWS):
         for column in range(8):
             if column < row + 5:
@@ -252,28 +252,31 @@
                 high_ref[block(3 - row), block(7 - column)] = jnp.zeros((BS, BS), jnp.bfloat16)
     own, high = Dense(own_ref, 8, 4), Dense(high_ref, 12, 8)
     result = Dense(dense_ref, 8, 4)
-    empty = dense_ref.shape[1] // BS - 1
-    dense_ref[:, block(empty)] = jnp.zeros((ROWS * BS, BS), jnp.bfloat16)
+    empty_ref[...] = jnp.zeros_like(empty_ref)
+    for row in range(ROWS):
+        for slot in range(SLOTS):
+            copy = pltpu.make_async_copy(empty_ref, out_ref.at[local_row(info_ref, row), slot], sem)
+            pl.when(place_ref[(8 + row) * SLOTS + slot] >= WINDOW)(copy.start)
 
     def write(p, c, value):
         result[p, c] = value
-
-    copies = []
-
-    def finish(p):
-        for row in (2 * p - 8, 2 * p - 7):
-            for slot in range(SLOTS):
-                where = place_ref[(8 + row) * SLOTS + slot] - 4
-                rows_ref[row, slot] = dense_ref[block(row), lanes(jnp.minimum(where, empty))]
-            copies.append(pltpu.make_async_copy(rows_ref.at[row], out_ref.at[local_row(info_ref, row)], sems.at[row]))
-            copies[-1].start()
+        for down in range(2):
+            for right in range(2):
+                row, column = 2 * p + down, 2 * c + right
+                if abs(row - column) > HALF:
+                    continue
+                slot = slot_ref[(row - 8) * WINDOW + column]
+                copy = pltpu.make_async_copy(
+                    dense_ref.at[block(row, 8), block(column, 4)],
+                    out_ref.at[local_row(info_ref, row - 8), jnp.minimum(slot, SLOTS - 1)], sem,
+                )
+                pl.when(slot < SLOTS)(copy.start)
 
     LAST.second(
         own, {4: own, 5: own, 6: high, 7: high}, Dense(square_ref, 8, 4), Dense(ready_ref, 8, 4), mask_ref,
-        square_part, cube_part, write, finish,
-    )
-    for copy in copies:
-        copy.wait()
+        square_part, cube_part, write,
+    )
+    pltpu.make_async_copy(out_ref, out_ref, sem).wait()
 
 
 def call(kernel, scalars, operands, outs, scratch, name, space=pltpu.VMEM, limit=12, out_space=pltpu.VMEM):
@@ -333,6 +336,8 @@
     where = (sign * (window - base) + FAR + 2 * total) % total
     where = jnp.where((window < total) & (where < WINDOW), where, WINDOW)
     place = where.reshape(-1)
+    match = where[FAR:FAR + ROWS, :, None] == jnp.arange(WINDOW, dtype=jnp.int32)
+    slot = jnp.min(jnp.where(match, jnp.arange(SLOTS, dtype=jnp.int32)[None, :, None], SLOTS), axis=1).reshape(-1)
     pattern = jnp.any(where[:, :, None] == jnp.arange(WINDOW, dtype=jnp.int32), axis=1)
     mask = pattern.astype(jnp.int32).reshape(-1)
 
@@ -355,9 +360,8 @@
         last_first_kernel, (mask,), (sent, current), [dense(4), *partial_sums(LAST)], [scratch(8)], "last_first"
     )
     (out,) = call(
-        last_second_kernel, (info, place, mask), (current, current_other, ready, *parts),
-        [jax.ShapeDtypeStruct(tiles.shape, tiles.dtype)], [scratch(8), scratch(12), scratch(13),
-         pltpu.VMEM(tiles.shape, tiles.dtype), pltpu.SemaphoreType.DMA((ROWS,))],
+        last_second_kernel, (info, place, slot, mask), (current, current_other, ready, *parts),
+        [jax.ShapeDtypeStruct(tiles.shape, tiles.dtype)], [scratch(8), scratch(12), scratch(12), pltpu.VMEM((BS, BS), jnp.bfloat16), pltpu.SemaphoreType.DMA],
         "last_second", out_space=pltpu.HBM,
     )
     return out

time: 43.4 us -> 43.2 us (level)
  transfers between devices with their start and end apart: 5 -> 5, of which waited for: 1 -> 1; matrix products, arithmetic and copies ran while one was open for 4% -> 5% of each run, Pallas kernels for 29% -> 29%
where the time goes in v5:
time: 43.2 us; the launch traced here: 42.9 us
  Pallas kernels  17.3 us (40%)
  waiting for transfers between devices  15.7 us (36%)
  starting transfers between devices  7.63 us (18%)
  local copies, waits for them, and re-layouts  1.1 us (3%)
  other arithmetic  1 us (2%)
    pallas_call x7, Pallas kernels, call(): pl.pallas_call(kernel, out_shape=outs, in_specs=[smem] * len(scalars) + [...  17.3 us
    ppermute x2, waiting for transfers between devices, shifted(): return lax.ppermute(value, axes, pairs)  15.7 us
    ppermute x2, starting transfers between devices, shifted(): return lax.ppermute(value, axes, pairs)  4.6 us
    ppermute x3, starting transfers between devices, swapped(): return lax.ppermute(value, 'layer', [(0, 1), (1, 0)])  3.03 us
  transfers between devices with their start and end apart: 5, of which 1 were waited for; matrix products, arithmetic and copies ran while one was open for 5% of the time, Pallas kernels for 29%

profile of v5, /device:TPU:0, one launch (start us, length us, event | category | flops | bytes accessed | tf_op | source)
XLA Modules:
  0.0 42.9 jit_solution(2340358892824847403)
XLA Ops:
  0.0 0.0 copy-start
  0.0 0.0 copy-start.2
  0.0 2.9 %collective-permute-start = (bf16[4,8,128,128]{3,2,1,0:T(8,128)(2,1)}, bf16[4,8,128,128]{3,2,1,0:T(8,128)(2,1)S(1)}, u32[]{:S(2)}, u32[]{:S(2)}) collective-permute-start(bf16[4,8,128,128]{3,2,1,0:T(8,128)(2,1)} %tiles_ref.3), channel_id=1, source_target_pairs={{0,2},{1,15},{2,4},{3,1},{4,6},{5,3},{6,8},{7,5},{8,10},{9,7},{10,... | collective-permute-start | bytes 3145736 | tf_op jit(solution)/shard_map/ppermute | solution.py:322
  2.9 0.7 %pad_add_fusion.info_ref = s32[2]{0:T(128)} fusion(s32[1]{0:T(128)} %bitcast.1, s32[1]{0:T(128)} %bitcast), kind=kLoop, calls=%fused_computation.30 | loop fusion | flops 2 | bytes 16 | tf_op jit(solution)/shard_map/stack | solution.py:314
  3.6 0.0 copy-start.1
  3.6 3.5 %pack.1 = bf16[26,128,128]{2,1,0:T(8,128)(2,1)} custom-call(s32[2]{0:T(128)} %pad_add_fusion.info_ref, s32[8,32]{1,0:T(8,128)} %bitcast.5, bf16[4,8,128,128]{3,2,1,0:T(8,128)(2,1)} %tiles_ref.3), custom_call_target="tpu_custom_call" | custom-call | tf_op jit(solution)/shard_map/pack/pallas_call | solution.py:284
  7.1 1.7 %collective-permute-start.3 = (bf16[26,128,128]{2,1,0:T(8,128)(2,1)}, bf16[26,128,128]{2,1,0:T(8,128)(2,1)S(1)}, u32[]{:S(2)}, u32[]{:S(2)}) collective-permute-start(bf16[26,128,128]{2,1,0:T(8,128)(2,1)} %pack.1), channel_id=1, source_target_pairs={{0,4},{1,13},{2,6},{3,15},{4,8},{5,1},{6,10},{7,3},{8,12},{9,5},{1... | collective-permute-start | bytes 2555912 | tf_op jit(solution)/shard_map/ppermute | solution.py:322
  8.8 0.0 copy-done.2
  8.8 0.1 copy.5
  8.9 0.6 %gather_fusion = s32[16,8]{1,0:T(8,128)S(1)} fusion(s32[32,8]{1,0:T(8,128)S(1)} %copy.5, s32[1024]{0:T(1024)S(1)} %pad_clamp_fusion), kind=kCustom, calls=%fused_computation | custom fusion | bytes 1088 | tf_op jit(solution)/shard_map/jit(_take)/gather | solution.py:335
  9.5 0.1 and_select_fusion
  9.6 0.1 add.122
  9.7 0.1 lt.68
  9.8 0.1 fusion
  9.9 0.1 reshape.119.mask_ref
  10.0 0.0 copy-done
  10.0 0.0 copy-done.1
  10.0 0.9 %own_rows.1.own_ref = bf16[512,1664]{1,0:T(8,128)(2,1)S(1)} custom-call(s32[2]{0:T(128)S(1)} %copy-done.1, s32[128]{0:T(128)S(1)} %and_select_fusion.1.place_ref, bf16[4,8,128,128]{3,2,1,0:T(8,128)(2,1)S(1)} %copy-done), custom_call_target="tpu_custom_call" | custom-call | tf_op jit(solution)/shard_map/own_rows/pallas_call | solution.py:284
  10.8 15.7 %collective-permute-done.near_ref = bf16[4,8,128,128]{3,2,1,0:T(8,128)(2,1)S(1)} collective-permute-done((bf16[4,8,128,128]{3,2,1,0:T(8,128)(2,1)}, bf16[4,8,128,128]{3,2,1,0:T(8,128)(2,1)S(1)}, u32[]{:S(2)}, u32[]{:S(2)}) %collective-permute-start) | collective-permute-done | bytes 1048608 | tf_op jit(solution)/shard_map/ppermute | solution.py:322
  26.6 0.1 fusion.6
  26.7 0.1 collective-permute-start.2
  26.8 0.5 %collective-permute-start.1 = (bf16[2,8,128,128]{3,2,1,0:T(8,128)(2,1)S(1)}, bf16[2,8,128,128]{3,2,1,0:T(8,128)(2,1)S(1)}, u32[]{:S(2)}, u32[]{:S(2)}) collective-permute-start(bf16[2,8,128,128]{3,2,1,0:T(8,128)(2,1)S(1)} %get-tuple-element.33), channel_id=1, source_target_pairs={{0,1},{1,0},{2,3},{3,2},{4,5},{5,4},{6,7},{7,6},{8,9},{9,8},{10,11... | collective-permute-start | bytes 1572872 | tf_op jit(solution)/shard_map/ppermute | solution.py:325
  27.3 2.3 %low_first.1 = (bf16[512,1664]{1,0:T(8,128)(2,1)S(1)}, bf16[512,512]{1,0:T(8,128)(2,1)S(1)}, f32[7,256,256]{2,1,0:T(8,128)S(1)}, f32[7,256,256]{2,1,0:T(8,128)S(1)}) custom-call(s32[2]{0:T(128)S(1)} %copy-done.1, s32[128]{0:T(128)S(1)} %and_select_fusion.1.place_ref, s32[256]{0:T(256)S(1)} %reshape.119.mask_ref, ...), custom_call_target="tpu_custom_call" | custom-call | tf_op jit(solution)/shard_map/low_first/pallas_call | solution.py:284
  29.6 0.0 collective-permute-done.2.other1_ref
  29.6 0.0 collective-permute-done.1.other0_ref
  29.6 3.8 %own.1.own_ref = bf16[512,1536]{1,0:T(8,128)(2,1)S(1)} custom-call(s32[2]{0:T(128)S(1)} %copy-done.1, s32[128]{0:T(128)S(1)} %and_select_fusion.1.place_ref, s32[256]{0:T(256)S(1)} %reshape.119.mask_ref, bf16[512,1664]{1,0:T(8,128)(2,1)S(1)} %get-tuple-element.22.low_ref, bf16[512,1664]{1,0:T(8,128)(2,1)S(1)} %own_rows.1.own_ref, ...), custom_call_target="tpu_custom_call" | custom-call | tf_op jit(solution)/shard_map/own/pallas_call | solution.py:284
  33.4 0.0 collective-permute-done.3.far_ref
  33.5 1.9 %low_second.1.sent_ref = bf16[26,128,128]{2,1,0:T(8,128)(2,1)S(1)} custom-call(s32[256]{0:T(256)S(1)} %reshape.119.mask_ref, bf16[26,128,128]{2,1,0:T(8,128)(2,1)S(1)} %collective-permute-done.3.far_ref, bf16[512,1664]{1,0:T(8,128)(2,1)S(1)} %get-tuple-element.22.low_ref, bf16[512,512]{1,0:T(8,128)(2,1)S(1)} %get-tuple-element.23.ready_ref, ...), custom_call_target="tpu_custom_call" | custom-call | tf_op jit(solution)/shard_map/low_second/pallas_call | solution.py:284
  35.3 2.5 %collective-permute-start.4 = (bf16[26,128,128]{2,1,0:T(8,128)(2,1)S(1)}, bf16[26,128,128]{2,1,0:T(8,128)(2,1)S(1)}, u32[]{:S(2)}, u32[]{:S(2)}) collective-permute-start(bf16[26,128,128]{2,1,0:T(8,128)(2,1)S(1)} %low_second.1.sent_ref), channel_id=1, source_target_pairs={{0,1},{1,0},{2,3},{3,2},{4,5},{5,4},{6,7},{7,6},{8,9},{9,8},{10,11... | collective-permute-start | bytes 2555912 | tf_op jit(solution)/shard_map/ppermute | solution.py:325
  37.8 0.1 select_reduce_fusion
  37.9 0.1 reshape.118.slot_ref
  38.0 2.0 %last_first.1 = (bf16[512,512]{1,0:T(8,128)(2,1)S(1)}, f32[7,256,256]{2,1,0:T(8,128)S(1)}, f32[7,256,256]{2,1,0:T(8,128)S(1)}) custom-call(s32[256]{0:T(256)S(1)} %reshape.119.mask_ref, bf16[26,128,128]{2,1,0:T(8,128)(2,1)S(1)} %low_second.1.sent_ref, bf16[512,1536]{1,0:T(8,128)(2,1)S(1)} %own.1.own_ref), custom_call_target="tpu_custom_call" | custom-call | tf_op jit(solution)/shard_map/last_first/pallas_call | solution.py:284
  40.0 0.0 collective-permute-done.4.other_ref
  40.0 2.9 %last_second.1 = bf16[4,8,128,128]{3,2,1,0:T(8,128)(2,1)} custom-call(s32[2]{0:T(128)S(1)} %copy-done.1, s32[128]{0:T(128)S(1)} %and_select_fusion.1.place_ref, s32[64]{0:T(128)S(1)} %reshape.118.slot_ref, s32[256]{0:T(256)S(1)} %reshape.119.mask_ref, bf16[512,1536]{1,0:T(8,128)(2,1)S(1)} %own.1.own_ref, ...), custom_call_target="tpu_custom_call" | custom-call | tf_op jit(solution)/shard_map/last_second/pallas_call | solution.py:284
  (6 shorter events, 0.1 us)
Async XLA Ops:
  0.0 10.0 %copy-start = (bf16[4,8,128,128]{3,2,1,0:T(8,128)(2,1)S(1)}, bf16[4,8,128,128]{3,2,1,0:T(8,128)(2,1)}, u32[]{:S(2)}) copy-start(bf16[4,8,128,128]{3,2,1,0:T(8,128)(2,1)} %tiles_ref.3) | copy-start | bytes 3145732
  0.0 8.8 %copy-start.2 = (s32[32,8]{0,1:T(8,128)S(1)}, s32[32,8]{0,1:T(8,128)}, u32[]{:S(2)}) copy-start(s32[32,8]{0,1:T(8,128)} %param.2) | copy-start | bytes 3076
  0.0 26.6 %collective-permute-start = (bf16[4,8,128,128]{3,2,1,0:T(8,128)(2,1)}, bf16[4,8,128,128]{3,2,1,0:T(8,128)(2,1)S(1)}, u32[]{:S(2)}, u32[]{:S(2)}) collective-permute-start(bf16[4,8,128,128]{3,2,1,0:T(8,128)(2,1)} %tiles_ref.3), channel_id=1, source_target_pairs={{0,2},{1,15},{2,4},{3,1},{4,6},{5,3},{6,8},{7,5},{8,10},{9,7},{10,... | collective-permute-start | bytes 3145736 | tf_op jit(solution)/shard_map/ppermute | solution.py:322
  3.6 6.4 %copy-start.1 = (s32[2]{0:T(128)S(1)}, s32[2]{0:T(128)}, u32[]{:S(2)}) copy-start(s32[2]{0:T(128)} %pad_add_fusion.info_ref) | copy-start | bytes 28
  7.1 26.3 %collective-permute-start.3 = (bf16[26,128,128]{2,1,0:T(8,128)(2,1)}, bf16[26,128,128]{2,1,0:T(8,128)(2,1)S(1)}, u32[]{:S(2)}, u32[]{:S(2)}) collective-permute-start(bf16[26,128,128]{2,1,0:T(8,128)(2,1)} %pack.1), channel_id=1, source_target_pairs={{0,4},{1,13},{2,6},{3,15},{4,8},{5,1},{6,10},{7,3},{8,12},{9,5},{1... | collective-permute-start | bytes 2555912 | tf_op jit(solution)/shard_map/ppermute | solution.py:322
  26.7 2.9 %collective-permute-start.2 = (bf16[2,8,128,128]{3,2,1,0:T(8,128)(2,1)S(1)}, bf16[2,8,128,128]{3,2,1,0:T(8,128)(2,1)S(1)}, u32[]{:S(2)}, u32[]{:S(2)}) collective-permute-start(bf16[2,8,128,128]{3,2,1,0:T(8,128)(2,1)S(1)} %get-tuple-element.32), channel_id=1, source_target_pairs={{0,1},{1,0},{2,3},{3,2},{4,5},{5,4},{6,7},{7,6},{8,9},{9,8},{10,11... | collective-permute-start | bytes 1572872 | tf_op jit(solution)/shard_map/ppermute | solution.py:325
  26.8 2.8 %collective-permute-start.1 = (bf16[2,8,128,128]{3,2,1,0:T(8,128)(2,1)S(1)}, bf16[2,8,128,128]{3,2,1,0:T(8,128)(2,1)S(1)}, u32[]{:S(2)}, u32[]{:S(2)}) collective-permute-start(bf16[2,8,128,128]{3,2,1,0:T(8,128)(2,1)S(1)} %get-tuple-element.33), channel_id=1, source_target_pairs={{0,1},{1,0},{2,3},{3,2},{4,5},{5,4},{6,7},{7,6},{8,9},{9,8},{10,11... | collective-permute-start | bytes 1572872 | tf_op jit(solution)/shard_map/ppermute | solution.py:325
  35.3 4.7 %collective-permute-start.4 = (bf16[26,128,128]{2,1,0:T(8,128)(2,1)S(1)}, bf16[26,128,128]{2,1,0:T(8,128)(2,1)S(1)}, u32[]{:S(2)}, u32[]{:S(2)}) collective-permute-start(bf16[26,128,128]{2,1,0:T(8,128)(2,1)S(1)} %low_second.1.sent_ref), channel_id=1, source_target_pairs={{0,1},{1,0},{2,3},{3,2},{4,5},{5,4},{6,7},{7,6},{8,9},{9,8},{10,11... | collective-permute-start | bytes 2555912 | tf_op jit(solution)/shard_map/ppermute | solution.py:325

commit v6 on v5

--- a/solution.py
+++ b/solution.py
@@ -72,6 +72,19 @@
             for i in range(1, len(sources)):
                 value = jnp.where(held >= i * count, sources[i][held % count, slot], value)
             target_ref[block(row), lanes(where)] = value
+
+
+class Part:
+    def __init__(self, ref, first):
+        self.ref, self.first = ref, first
+
+    def __getitem__(self, at):
+        return self.ref[self.first + at]
+
+
+def tables(ref):
+    firsts = (0, 2, 2 + WINDOW * SLOTS, 2 + WINDOW * SLOTS + ROWS * WINDOW)
+    return [Part(ref, first) for first in firsts]
 
 
 def kept(value, mask_ref, row_pair, column_pair):
@@ -183,19 +196,22 @@
 LAST = Step((4, 5), 2, 7, (2, 3, 4, 5), (6, 7), lambda p: range(p - 2, p + 3))
 
 
-def own_rows_kernel(info_ref, place_ref, tiles_ref, own_ref):
+def own_rows_kernel(table_ref, tiles_ref, own_ref):
+    info_ref, place_ref, _, _ = tables(table_ref)
     own_ref[...] = jnp.zeros_like(own_ref)
     spread(info_ref, place_ref, (tiles_ref,), 8, own_ref, 4)
 
 
-def low_first_kernel(info_ref, place_ref, mask_ref, near_ref, own_ref, low_ref, square_ref, square_part, cube_part):
+def low_first_kernel(table_ref, near_ref, own_ref, low_ref, square_ref, square_part, cube_part):
+    info_ref, place_ref, _, mask_ref = tables(table_ref)
     low_ref[...] = jnp.zeros_like(low_ref)
     spread(info_ref, place_ref, (near_ref,), 4, low_ref, 0)
     low, own = Dense(low_ref, 4, 0), Dense(own_ref, 8, 4)
     LOW.first(low, {2: low, 3: low, 4: own, 5: own}, Dense(square_ref, 4, 8), mask_ref, square_part, cube_part)
 
 
-def own_kernel(info_ref, place_ref, mask_ref, low_ref, own_ref, other0_ref, other1_ref, next_ref, high_ref, square_ref):
+def own_kernel(table_ref, low_ref, own_ref, other0_ref, other1_ref, next_ref, high_ref, square_ref):
+    info_ref, place_ref, _, mask_ref = tables(table_ref)
     high_ref[...] = jnp.zeros_like(high_ref)
     spread(info_ref, place_ref, (other0_ref, other1_ref), 12, high_ref, 8)
     low, own, high = Dense(low_ref, 4, 0), Dense(own_ref, 8, 4), Dense(high_ref, 12, 8)
@@ -209,7 +225,8 @@
     OWN.all(own, {2: low, 3: low, 4: own, 5: own, 6: high, 7: high}, Dense(square_ref, 8, 4), mask_ref, write)
 
 
-def low_second_kernel(mask_ref, far_ref, low_ref, ready_ref, square_part, cube_part, sent_ref, far_dense_ref, square_ref):
+def low_second_kernel(table_ref, far_ref, low_ref, ready_ref, square_part, cube_part, sent_ref, far_dense_ref, square_ref):
+    _, _, _, mask_ref = tables(table_ref)
     for row in range(ROWS):
         for column in range(8):
             if column < row + 5:
@@ -231,7 +248,8 @@
     )
 
 
-def last_first_kernel(mask_ref, sent_ref, own_ref, square_ref, square_part, cube_part, low_ref):
+def last_first_kernel(table_ref, sent_ref, own_ref, square_ref, square_part, cube_part, low_ref):
+    _, _, _, mask_ref = tables(table_ref)
     for row in range(ROWS):
         for column in range(8):
             if column < row + 5:
@@ -242,8 +260,9 @@
     LAST.first(own, {2: low, 3: low, 4: own, 5: own}, Dense(square_ref, 8, 4), mask_ref, square_part, cube_part)
 
 
-def last_second_kernel(info_ref, place_ref, slot_ref, mask_ref, own_ref, other_ref, ready_ref, square_part, cube_part,
+def last_second_kernel(table_ref, own_ref, other_ref, ready_ref, square_part, cube_part,
                        out_ref, high_ref, square_ref, dense_ref, empty_ref, sem):
+    info_ref, place_ref, slot_ref, mask_ref = tables(table_ref)
     for row in range(ROWS):
         for column in range(8):
             if column < row + 5:
@@ -340,27 +359,28 @@
     slot = jnp.min(jnp.where(match, jnp.arange(SLOTS, dtype=jnp.int32)[None, :, None], SLOTS), axis=1).reshape(-1)
     pattern = jnp.any(where[:, :, None] == jnp.arange(WINDOW, dtype=jnp.int32), axis=1)
     mask = pattern.astype(jnp.int32).reshape(-1)
-
-    (own,) = call(own_rows_kernel, (info, place), (tiles,), [dense(13)], [], "own_rows")
-
-    near, packed_rows, own, mask = lax.optimization_barrier((near, packed_rows, own, mask))
+    table = jnp.concatenate([info, place, slot, mask])
+
+    (own,) = call(own_rows_kernel, (table,), (tiles,), [dense(13)], [], "own_rows")
+
+    near, packed_rows, own = lax.optimization_barrier((near, packed_rows, own))
     other = [swapped(near[:2]), swapped(near[2:])]
     low, ready, *parts = call(
-        low_first_kernel, (info, place, mask), (near, own), [dense(13), dense(4), *partial_sums(LOW)], [], "low_first"
+        low_first_kernel, (table,), (near, own), [dense(13), dense(4), *partial_sums(LOW)], [], "low_first"
     )
     (current,) = call(
-        own_kernel, (info, place, mask), (low, own, *other), [dense(12)], [scratch(9), scratch(12)], "own"
+        own_kernel, (table,), (low, own, *other), [dense(12)], [scratch(9), scratch(12)], "own"
     )
     low, current = lax.optimization_barrier((low, current))
     (sent,) = call(
-        low_second_kernel, (mask,), (far, low, ready, *parts), [packed], [scratch(8), scratch(12)], "low_second"
+        low_second_kernel, (table,), (far, low, ready, *parts), [packed], [scratch(8), scratch(12)], "low_second"
     )
     current_other = swapped(sent)
     ready, *parts = call(
-        last_first_kernel, (mask,), (sent, current), [dense(4), *partial_sums(LAST)], [scratch(8)], "last_first"
+        last_first_kernel, (table,), (sent, current), [dense(4), *partial_sums(LAST)], [scratch(8)], "last_first"
     )
     (out,) = call(
-        last_second_kernel, (info, place, slot, mask), (current, current_other, ready, *parts),
+        last_second_kernel, (table,), (current, current_other, ready, *parts),
         [jax.ShapeDtypeStruct(tiles.shape, tiles.dtype)], [scratch(8), scratch(12), scratch(12), pltpu.VMEM((BS, BS), jnp.bfloat16), pltpu.SemaphoreType.DMA],
         "last_second", out_space=pltpu.HBM,
     )

time: 43.2 us -> 42.8 us (level)
  no operation moved by 1% of the time
where the time goes in v6:
time: 42.8 us; the launch traced here: 42.6 us
  Pallas kernels  16.9 us (39%)
  waiting for transfers between devices  15.9 us (37%)
  starting transfers between devices  7.57 us (18%)
  local copies, waits for them, and re-layouts  1.17 us (3%)
  other arithmetic  0.92 us (2%)
    pallas_call x7, Pallas kernels, call(): pl.pallas_call(kernel, out_shape=outs, in_specs=[smem] * len(scalars) + [...  16.9 us
    ppermute x2, waiting for transfers between devices, shifted(): return lax.ppermute(value, axes, pairs)  15.9 us
    ppermute x2, starting transfers between devices, shifted(): return lax.ppermute(value, axes, pairs)  4.62 us
    ppermute x3, starting transfers between devices, swapped(): return lax.ppermute(value, 'layer', [(0, 1), (1, 0)])  2.95 us
  transfers between devices with their start and end apart: 5, of which 1 were waited for; matrix products, arithmetic and copies ran while one was open for 5% of the time, Pallas kernels for 29%

profile of v6, /device:TPU:0, one launch (start us, length us, event | category | flops | bytes accessed | tf_op | source)
XLA Modules:
  0.0 42.6 jit_solution(17236384192664250072)
XLA Ops:
  0.0 0.0 copy-start
  0.0 0.0 copy-start.1
  0.0 2.9 %collective-permute-start = (bf16[4,8,128,128]{3,2,1,0:T(8,128)(2,1)}, bf16[4,8,128,128]{3,2,1,0:T(8,128)(2,1)S(1)}, u32[]{:S(2)}, u32[]{:S(2)}) collective-permute-start(bf16[4,8,128,128]{3,2,1,0:T(8,128)(2,1)} %tiles_ref.3), channel_id=1, source_target_pairs={{0,2},{1,15},{2,4},{3,1},{4,6},{5,3},{6,8},{7,5},{8,10},{9,7},{10,... | collective-permute-start | bytes 3145736 | tf_op jit(solution)/shard_map/ppermute | solution.py:341
  2.9 0.6 %pad_add_fusion.info_ref = s32[2]{0:T(128)} fusion(s32[1]{0:T(128)} %bitcast.1, s32[1]{0:T(128)} %bitcast), kind=kLoop, calls=%fused_computation.30 | loop fusion | flops 2 | bytes 16 | tf_op jit(solution)/shard_map/stack | solution.py:333
  3.5 3.4 %pack.1 = bf16[26,128,128]{2,1,0:T(8,128)(2,1)} custom-call(s32[2]{0:T(128)} %pad_add_fusion.info_ref, s32[8,32]{1,0:T(8,128)} %bitcast.5, bf16[4,8,128,128]{3,2,1,0:T(8,128)(2,1)} %tiles_ref.3), custom_call_target="tpu_custom_call" | custom-call | tf_op jit(solution)/shard_map/pack/pallas_call | solution.py:303
  6.9 1.7 %collective-permute-start.3 = (bf16[26,128,128]{2,1,0:T(8,128)(2,1)}, bf16[26,128,128]{2,1,0:T(8,128)(2,1)S(1)}, u32[]{:S(2)}, u32[]{:S(2)}) collective-permute-start(bf16[26,128,128]{2,1,0:T(8,128)(2,1)} %pack.1), channel_id=1, source_target_pairs={{0,4},{1,13},{2,6},{3,15},{4,8},{5,1},{6,10},{7,3},{8,12},{9,5},{1... | collective-permute-start | bytes 2555912 | tf_op jit(solution)/shard_map/ppermute | solution.py:341
  8.6 0.0 copy-done.1
  8.6 0.1 copy.5
  8.7 0.6 %gather_fusion = s32[16,8]{1,0:T(8,128)S(1)} fusion(s32[32,8]{1,0:T(8,128)S(1)} %copy.5, s32[1024]{0:T(1024)S(1)} %pad_clamp_fusion), kind=kCustom, calls=%fused_computation | custom fusion | bytes 1088 | tf_op jit(solution)/shard_map/jit(_take)/gather | solution.py:354
  9.3 0.1 and_select_fusion
  9.4 0.1 add.122
  9.4 0.1 lt.68
  9.6 0.1 select_reduce_fusion
  9.6 0.1 reshape.118
  9.7 0.1 fusion
  9.9 0.1 reshape.119
  9.9 0.1 concatenate.4.table_ref
  10.0 0.0 copy-done
  10.0 0.9 %own_rows.1.own_ref = bf16[512,1664]{1,0:T(8,128)(2,1)S(1)} custom-call(s32[450]{0:T(512)S(1)} %concatenate.4.table_ref, bf16[4,8,128,128]{3,2,1,0:T(8,128)(2,1)S(1)} %copy-done), custom_call_target="tpu_custom_call" | custom-call | tf_op jit(solution)/shard_map/own_rows/pallas_call | solution.py:303
  10.9 15.9 %collective-permute-done.near_ref = bf16[4,8,128,128]{3,2,1,0:T(8,128)(2,1)S(1)} collective-permute-done((bf16[4,8,128,128]{3,2,1,0:T(8,128)(2,1)}, bf16[4,8,128,128]{3,2,1,0:T(8,128)(2,1)S(1)}, u32[]{:S(2)}, u32[]{:S(2)}) %collective-permute-start) | collective-permute-done | bytes 1048608 | tf_op jit(solution)/shard_map/ppermute | solution.py:341
  26.8 0.1 fusion.6
  26.9 0.1 collective-permute-start.2
  27.0 0.5 %collective-permute-start.1 = (bf16[2,8,128,128]{3,2,1,0:T(8,128)(2,1)S(1)}, bf16[2,8,128,128]{3,2,1,0:T(8,128)(2,1)S(1)}, u32[]{:S(2)}, u32[]{:S(2)}) collective-permute-start(bf16[2,8,128,128]{3,2,1,0:T(8,128)(2,1)S(1)} %get-tuple-element.31), channel_id=1, source_target_pairs={{0,1},{1,0},{2,3},{3,2},{4,5},{5,4},{6,7},{7,6},{8,9},{9,8},{10,11... | collective-permute-start | bytes 1572872 | tf_op jit(solution)/shard_map/ppermute | solution.py:344
  27.5 2.3 %low_first.1 = (bf16[512,1664]{1,0:T(8,128)(2,1)S(1)}, bf16[512,512]{1,0:T(8,128)(2,1)S(1)}, f32[7,256,256]{2,1,0:T(8,128)S(1)}, f32[7,256,256]{2,1,0:T(8,128)S(1)}) custom-call(s32[450]{0:T(512)S(1)} %concatenate.4.table_ref, bf16[4,8,128,128]{3,2,1,0:T(8,128)(2,1)S(1)} %collective-permute-done.near_ref, bf16[512,1664]{1,0:T(8,128)(2,1)S(1)} %own_rows.1.own_ref), custom_call_target="tpu_custom_call" | custom-call | tf_op jit(solution)/shard_map/low_first/pallas_call | solution.py:303
  29.8 0.0 collective-permute-done.2.other1_ref
  29.8 0.0 collective-permute-done.1.other0_ref
  29.8 3.7 %own.1.own_ref = bf16[512,1536]{1,0:T(8,128)(2,1)S(1)} custom-call(s32[450]{0:T(512)S(1)} %concatenate.4.table_ref, bf16[512,1664]{1,0:T(8,128)(2,1)S(1)} %get-tuple-element.20.low_ref, bf16[512,1664]{1,0:T(8,128)(2,1)S(1)} %own_rows.1.own_ref, bf16[2,8,128,128]{3,2,1,0:T(8,128)(2,1)S(1)} %collective-permute-done.1.other0_ref, ...), custom_call_target="tpu_custom_call" | custom-call | tf_op jit(solution)/shard_map/own/pallas_call | solution.py:303
  33.5 0.0 collective-permute-done.3.far_ref
  33.5 1.8 %low_second.1.sent_ref = bf16[26,128,128]{2,1,0:T(8,128)(2,1)S(1)} custom-call(s32[450]{0:T(512)S(1)} %concatenate.4.table_ref, bf16[26,128,128]{2,1,0:T(8,128)(2,1)S(1)} %collective-permute-done.3.far_ref, bf16[512,1664]{1,0:T(8,128)(2,1)S(1)} %get-tuple-element.20.low_ref, bf16[512,512]{1,0:T(8,128)(2,1)S(1)} %get-tuple-element.21.ready_ref, ...), custom_call_target="tpu_custom_call" | custom-call | tf_op jit(solution)/shard_map/low_second/pallas_call | solution.py:303
  35.3 2.4 %collective-permute-start.4 = (bf16[26,128,128]{2,1,0:T(8,128)(2,1)S(1)}, bf16[26,128,128]{2,1,0:T(8,128)(2,1)S(1)}, u32[]{:S(2)}, u32[]{:S(2)}) collective-permute-start(bf16[26,128,128]{2,1,0:T(8,128)(2,1)S(1)} %low_second.1.sent_ref), channel_id=1, source_target_pairs={{0,1},{1,0},{2,3},{3,2},{4,5},{5,4},{6,7},{7,6},{8,9},{9,8},{10,11... | collective-permute-start | bytes 2555912 | tf_op jit(solution)/shard_map/ppermute | solution.py:344
  37.7 2.1 %last_first.1 = (bf16[512,512]{1,0:T(8,128)(2,1)S(1)}, f32[7,256,256]{2,1,0:T(8,128)S(1)}, f32[7,256,256]{2,1,0:T(8,128)S(1)}) custom-call(s32[450]{0:T(512)S(1)} %concatenate.4.table_ref, bf16[26,128,128]{2,1,0:T(8,128)(2,1)S(1)} %low_second.1.sent_ref, bf16[512,1536]{1,0:T(8,128)(2,1)S(1)} %own.1.own_ref), custom_call_target="tpu_custom_call" | custom-call | tf_op jit(solution)/shard_map/last_first/pallas_call | solution.py:303
  39.8 0.0 collective-permute-done.4.other_ref
  39.8 2.8 %last_second.1 = bf16[4,8,128,128]{3,2,1,0:T(8,128)(2,1)} custom-call(s32[450]{0:T(512)S(1)} %concatenate.4.table_ref, bf16[512,1536]{1,0:T(8,128)(2,1)S(1)} %own.1.own_ref, bf16[26,128,128]{2,1,0:T(8,128)(2,1)S(1)} %collective-permute-done.4.other_ref, bf16[512,512]{1,0:T(8,128)(2,1)S(1)} %get-tuple-element.24.ready_ref, ...), custom_call_target="tpu_custom_call" | custom-call | tf_op jit(solution)/shard_map/last_second/pallas_call | solution.py:303
  (6 shorter events, 0.1 us)
Async XLA Ops:
  0.0 10.0 %copy-start = (bf16[4,8,128,128]{3,2,1,0:T(8,128)(2,1)S(1)}, bf16[4,8,128,128]{3,2,1,0:T(8,128)(2,1)}, u32[]{:S(2)}) copy-start(bf16[4,8,128,128]{3,2,1,0:T(8,128)(2,1)} %tiles_ref.3) | copy-start | bytes 3145732
  0.0 8.6 %copy-start.1 = (s32[32,8]{0,1:T(8,128)S(1)}, s32[32,8]{0,1:T(8,128)}, u32[]{:S(2)}) copy-start(s32[32,8]{0,1:T(8,128)} %param.2) | copy-start | bytes 3076
  0.0 26.8 %collective-permute-start = (bf16[4,8,128,128]{3,2,1,0:T(8,128)(2,1)}, bf16[4,8,128,128]{3,2,1,0:T(8,128)(2,1)S(1)}, u32[]{:S(2)}, u32[]{:S(2)}) collective-permute-start(bf16[4,8,128,128]{3,2,1,0:T(8,128)(2,1)} %tiles_ref.3), channel_id=1, source_target_pairs={{0,2},{1,15},{2,4},{3,1},{4,6},{5,3},{6,8},{7,5},{8,10},{9,7},{10,... | collective-permute-start | bytes 3145736 | tf_op jit(solution)/shard_map/ppermute | solution.py:341
  6.9 26.6 %collective-permute-start.3 = (bf16[26,128,128]{2,1,0:T(8,128)(2,1)}, bf16[26,128,128]{2,1,0:T(8,128)(2,1)S(1)}, u32[]{:S(2)}, u32[]{:S(2)}) collective-permute-start(bf16[26,128,128]{2,1,0:T(8,128)(2,1)} %pack.1), channel_id=1, source_target_pairs={{0,4},{1,13},{2,6},{3,15},{4,8},{5,1},{6,10},{7,3},{8,12},{9,5},{1... | collective-permute-start | bytes 2555912 | tf_op jit(solution)/shard_map/ppermute | solution.py:341
  26.9 2.9 %collective-permute-start.2 = (bf16[2,8,128,128]{3,2,1,0:T(8,128)(2,1)S(1)}, bf16[2,8,128,128]{3,2,1,0:T(8,128)(2,1)S(1)}, u32[]{:S(2)}, u32[]{:S(2)}) collective-permute-start(bf16[2,8,128,128]{3,2,1,0:T(8,128)(2,1)S(1)} %get-tuple-element.30), channel_id=1, source_target_pairs={{0,1},{1,0},{2,3},{3,2},{4,5},{5,4},{6,7},{7,6},{8,9},{9,8},{10,11... | collective-permute-start | bytes 1572872 | tf_op jit(solution)/shard_map/ppermute | solution.py:344
  27.0 2.8 %collective-permute-start.1 = (bf16[2,8,128,128]{3,2,1,0:T(8,128)(2,1)S(1)}, bf16[2,8,128,128]{3,2,1,0:T(8,128)(2,1)S(1)}, u32[]{:S(2)}, u32[]{:S(2)}) collective-permute-start(bf16[2,8,128,128]{3,2,1,0:T(8,128)(2,1)S(1)} %get-tuple-element.31), channel_id=1, source_target_pairs={{0,1},{1,0},{2,3},{3,2},{4,5},{5,4},{6,7},{7,6},{8,9},{9,8},{10,11... | collective-permute-start | bytes 1572872 | tf_op jit(solution)/shard_map/ppermute | solution.py:344
  35.3 4.5 %collective-permute-start.4 = (bf16[26,128,128]{2,1,0:T(8,128)(2,1)S(1)}, bf16[26,128,128]{2,1,0:T(8,128)(2,1)S(1)}, u32[]{:S(2)}, u32[]{:S(2)}) collective-permute-start(bf16[26,128,128]{2,1,0:T(8,128)(2,1)S(1)} %low_second.1.sent_ref), channel_id=1, source_target_pairs={{0,1},{1,0},{2,3},{3,2},{4,5},{5,4},{6,7},{7,6},{8,9},{9,8},{10,11... | collective-permute-start | bytes 2555912 | tf_op jit(solution)/shard_map/ppermute | solution.py:344

commit v7 on v6

--- a/solution.py
+++ b/solution.py
@@ -116,6 +116,20 @@
         self.ref[self.rows(at[0]), self.columns(at[1])] = value
 
 
+class Packed:
+    def __init__(self, ref, first_row, first_column):
+        self.ref, self.first_row, self.first_column = ref, first_row, first_column
+
+    def __getitem__(self, at):
+        parts = []
+        for row in (2 * at[0] - self.first_row, 2 * at[0] + 1 - self.first_row):
+            columns = [2 * at[1] + right - self.first_column for right in range(2)]
+            parts.append(jnp.concatenate(
+                [self.ref[start_of(row) + c] if c < row + 5 else jnp.zeros((BS, BS), jnp.bfloat16) for c in columns], axis=1
+            ))
+        return jnp.concatenate(parts, axis=0)
+
+
 def product(left, right, row_pair, column_pair, ks):
     ks = [k for k in sorted(ks) if abs(k - row_pair) <= 2 and abs(k - column_pair) <= 2]
     total = None
@@ -126,7 +140,8 @@
             count += 1
         part = jnp.dot(
             left.ref[left.rows(row_pair), left.columns(ks[0], count)],
-            source.ref[source.rows(ks[0], count), source.columns(column_pair)],
+            jnp.concatenate([source[k, column_pair] for k in ks[:count]], axis=0) if isinstance(source, Packed)
+            else source.ref[source.rows(ks[0], count), source.columns(column_pair)],
             preferred_element_type=jnp.float32,
         )
         total = part if total is None else total + part
@@ -144,40 +159,51 @@
     def whole(self, row_pair, column_pair):
         return not any(abs(k - row_pair) <= 2 and abs(k - column_pair) <= 2 for k in self.late)
 
+    def places(self):
+        return [(p, c) for p in self.pairs for c in self.columns(p)]
+
+    def reached(self, row_pair, column_pair):
+        return any(abs(k - row_pair) <= 2 and abs(k - column_pair) <= 2 for k in self.early)
+
     def open(self):
-        squares = [(p, c) for p in self.pairs for c in self.columns(p) if not self.whole(p, c)]
+        squares = [(p, c) for p, c in self.places() if not self.whole(p, c) and self.reached(p, c)]
         cubes = [(p, c) for p in self.pairs for c in self.wanted(p) if self.done(p, c)]
         return {at: i for i, at in enumerate(squares)}, {at: i for i, at in enumerate(cubes)}
 
     def done(self, row_pair, column_pair):
         return [k for k in self.columns(row_pair) if self.whole(row_pair, k) and abs(k - column_pair) <= 2]
 
-    def first(self, left, right, square, mask_ref, square_part, cube_part):
+    def first(self, left, right, square, mask_ref, square_part, cube_part, begun=None):
         squares, cubes = self.open()
-        for p in self.pairs:
-            for c in self.columns(p):
-                value = product(left, right, p, c, self.early)
-                if (p, c) in squares:
-                    square_part[squares[p, c]] = value
-                else:
-                    square[p, c] = kept(value, mask_ref, p, c).astype(jnp.bfloat16)
+        for i, (p, c) in enumerate(self.places()):
+            if not self.reached(p, c):
+                continue
+            value = product(left, right, p, c, self.early)
+            if begun is not None:
+                value = begun[i] + value
+            if (p, c) in squares:
+                square_part[squares[p, c]] = value
+            else:
+                square[p, c] = kept(value, mask_ref, p, c).astype(jnp.bfloat16)
         for (p, c), i in cubes.items():
             cube_part[i] = product(square, right, p, c, self.done(p, c))
 
-    def second(self, left, right, square, ready, mask_ref, square_part, cube_part, write, finish=lambda p: None):
+    def second(self, left, right, square, ready, mask_ref, square_part, cube_part, write, begun=None):
         squares, cubes = self.open()
-        for (p, c), i in squares.items():
-            value = square_part[i] + product(left, right, p, c, self.late)
-            square[p, c] = kept(value, mask_ref, p, c).astype(jnp.bfloat16)
+        late = [(p, c) for p, c in self.places() if not self.whole(p, c)]
+        for i, (p, c) in enumerate(self.places()):
+            if (p, c) in late:
+                part = square_part[squares[p, c]] if (p, c) in squares else begun[i]
+                value = part + product(left, right, p, c, self.late)
+                square[p, c] = kept(value, mask_ref, p, c).astype(jnp.bfloat16)
         for p in self.pairs:
             for c in self.wanted(p):
                 rest = [k for k in self.columns(p) if not self.whole(p, k)]
                 cube = product(square, right, p, c, rest)
                 if (p, c) in cubes:
                     cube = cube_part[cubes[p, c]] if cube is None else cube_part[cubes[p, c]] + cube
-                own = (square if (p, c) in squares else ready)[p, c].astype(jnp.float32)
+                own = (square if (p, c) in late else ready)[p, c].astype(jnp.float32)
                 write(p, c, (3.0 * own - 2.0 * kept(cube, mask_ref, p, c)).astype(jnp.bfloat16))
-            finish(p)
 
     def all(self, left, right, square, mask_ref, write):
         for p in self.pairs:
@@ -193,7 +219,7 @@
 
 OWN = Step((4, 5), 2, 7, (2, 3, 4, 5, 6, 7), (), lambda p: range(p - 2, p + 3))
 LOW = Step((2, 3), 0, 5, (2, 3, 4, 5), (0, 1), lambda p: range(2, p + 3))
-LAST = Step((4, 5), 2, 7, (2, 3, 4, 5), (6, 7), lambda p: range(p - 2, p + 3))
+LAST = Step((4, 5), 2, 7, (2, 3), (6, 7), lambda p: range(p - 2, p + 3))
 
 
 def own_rows_kernel(table_ref, tiles_ref, own_ref):
@@ -210,7 +236,7 @@
     LOW.first(low, {2: low, 3: low, 4: own, 5: own}, Dense(square_ref, 4, 8), mask_ref, square_part, cube_part)
 
 
-def own_kernel(table_ref, low_ref, own_ref, other0_ref, other1_ref, next_ref, high_ref, square_ref):
+def own_kernel(table_ref, low_ref, own_ref, other0_ref, other1_ref, next_ref, begun_ref, high_ref, square_ref):
     info_ref, place_ref, _, mask_ref = tables(table_ref)
     high_ref[...] = jnp.zeros_like(high_ref)
     spread(info_ref, place_ref, (other0_ref, other1_ref), 12, high_ref, 8)
@@ -223,17 +249,13 @@
         result[p, c] = value
 
     OWN.all(own, {2: low, 3: low, 4: own, 5: own, 6: high, 7: high}, Dense(square_ref, 8, 4), mask_ref, write)
-
-
-def low_second_kernel(table_ref, far_ref, low_ref, ready_ref, square_part, cube_part, sent_ref, far_dense_ref, square_ref):
-    _, _, _, mask_ref = tables(table_ref)
-    for row in range(ROWS):
-        for column in range(8):
-            if column < row + 5:
-                far_dense_ref[block(row), block(column)] = far_ref[start_of(row) + column]
-            else:
-                far_dense_ref[block(row), block(column)] = jnp.zeros((BS, BS), jnp.bfloat16)
-    low, far = Dense(low_ref, 4, 0), Dense(far_dense_ref, 0, 0)
+    for i, (p, c) in enumerate(LAST.places()):
+        begun_ref[i] = product(result, {4: result, 5: result}, p, c, (4, 5))
+
+
+def low_second_kernel(table_ref, far_ref, low_ref, ready_ref, square_part, cube_part, sent_ref, square_ref):
+    mask_ref = tables(table_ref)[3]
+    low, far = Dense(low_ref, 4, 0), Packed(far_ref, 0, 0)
 
     def write(p, c, value):
         for down in range(2):
@@ -248,7 +270,7 @@
     )
 
 
-def last_first_kernel(table_ref, sent_ref, own_ref, square_ref, square_part, cube_part, low_ref):
+def last_first_kernel(table_ref, sent_ref, own_ref, begun_ref, square_ref, square_part, cube_part, low_ref):
     _, _, _, mask_ref = tables(table_ref)
     for row in range(ROWS):
         for column in range(8):
@@ -257,10 +279,10 @@
             else:
                 low_ref[block(row), block(column)] = jnp.zeros((BS, BS), jnp.bfloat16)
     low, own = Dense(low_ref, 4, 4), Dense(own_ref, 8, 4)
-    LAST.first(own, {2: low, 3: low, 4: own, 5: own}, Dense(square_ref, 8, 4), mask_ref, square_part, cube_part)
-
-
-def last_second_kernel(table_ref, own_ref, other_ref, ready_ref, square_part, cube_part,
+    LAST.first(own, {2: low, 3: low, 4: own, 5: own}, Dense(square_ref, 8, 4), mask_ref, square_part, cube_part, begun_ref)
+
+
+def last_second_kernel(table_ref, own_ref, begun_ref, other_ref, ready_ref, square_part, cube_part,
                        out_ref, high_ref, square_ref, dense_ref, empty_ref, sem):
     info_ref, place_ref, slot_ref, mask_ref = tables(table_ref)
     for row in range(ROWS):
@@ -293,7 +315,7 @@
 
     LAST.second(
         own, {4: own, 5: own, 6: high, 7: high}, Dense(square_ref, 8, 4), Dense(ready_ref, 8, 4), mask_ref,
-        square_part, cube_part, write,
+        square_part, cube_part, write, begun_ref,
     )
     pltpu.make_async_copy(out_ref, out_ref, sem).wait()
 
@@ -368,19 +390,20 @@
     low, ready, *parts = call(
         low_first_kernel, (table,), (near, own), [dense(13), dense(4), *partial_sums(LOW)], [], "low_first"
     )
-    (current,) = call(
-        own_kernel, (table,), (low, own, *other), [dense(12)], [scratch(9), scratch(12)], "own"
+    begun = jax.ShapeDtypeStruct((len(LAST.places()), TILE, TILE), jnp.float32)
+    current, begun = call(
+        own_kernel, (table,), (low, own, *other), [dense(12), begun], [scratch(9), scratch(12)], "own"
     )
     low, current = lax.optimization_barrier((low, current))
     (sent,) = call(
-        low_second_kernel, (table,), (far, low, ready, *parts), [packed], [scratch(8), scratch(12)], "low_second"
+        low_second_kernel, (table,), (far, low, ready, *parts), [packed], [scratch(12)], "low_second"
     )
     current_other = swapped(sent)
     ready, *parts = call(
-        last_first_kernel, (table,), (sent, current), [dense(4), *partial_sums(LAST)], [scratch(8)], "last_first"
+        last_first_kernel, (table,), (sent, current, begun), [dense(4), *partial_sums(LAST)], [scratch(8)], "last_first"
     )
     (out,) = call(
-        last_second_kernel, (table,), (current, current_other, ready, *parts),
+        last_second_kernel, (table,), (current, begun, current_other, ready, *parts),
         [jax.ShapeDtypeStruct(tiles.shape, tiles.dtype)], [scratch(8), scratch(12), scratch(12), pltpu.VMEM((BS, BS), jnp.bfloat16), pltpu.SemaphoreType.DMA],
         "last_second", out_space=pltpu.HBM,
     )

time: 42.8 us -> 42.6 us (level)
  starting transfers between devices: 7.57 us -> 7 us
    ppermute x3, starting transfers between devices: 2.95 us -> 2.44 us  [swapped(): return lax.ppermute(value, 'layer', [(0, 1), (1, 0)])]
    ppermute x3, waiting for transfers between devices: 0.01 us -> 0.52 us  [swapped(): return lax.ppermute(value, 'layer', [(0, 1), (1, 0)])]
  transfers between devices with their start and end apart: 5 -> 5, of which waited for: 1 -> 2; matrix products, arithmetic and copies ran while one was open for 5% -> 5% of each run, Pallas kernels for 29% -> 29%
where the time goes in v7:
time: 42.6 us; the launch traced here: 42.4 us
  Pallas kernels  16.9 us (40%)
  waiting for transfers between devices  16.3 us (38%)
  starting transfers between devices  7 us (16%)
  local copies, waits for them, and re-layouts  1.16 us (3%)
  other arithmetic  0.99 us (2%)
    pallas_call x7, Pallas kernels, call(): pl.pallas_call(kernel, out_shape=outs, in_specs=[smem] * len(scalars) + [...  16.9 us
    ppermute x2, waiting for transfers between devices, shifted(): return lax.ppermute(value, axes, pairs)  15.7 us
    ppermute x2, starting transfers between devices, shifted(): return lax.ppermute(value, axes, pairs)  4.57 us
    ppermute x3, starting transfers between devices, swapped(): return lax.ppermute(value, 'layer', [(0, 1), (1, 0)])  2.44 us
  transfers between devices with their start and end apart: 5, of which 2 were waited for; matrix products, arithmetic and copies ran while one was open for 5% of the time, Pallas kernels for 29%

profile of v7, /device:TPU:0, one launch (start us, length us, event | category | flops | bytes accessed | tf_op | source)
XLA Modules:
  0.0 42.4 jit_solution(11540645872025197458)
XLA Ops:
  0.0 0.0 copy-start
  0.0 0.0 copy-start.1
  0.0 2.9 %collective-permute-start = (bf16[4,8,128,128]{3,2,1,0:T(8,128)(2,1)}, bf16[4,8,128,128]{3,2,1,0:T(8,128)(2,1)S(1)}, u32[]{:S(2)}, u32[]{:S(2)}) collective-permute-start(bf16[4,8,128,128]{3,2,1,0:T(8,128)(2,1)} %tiles_ref.3), channel_id=1, source_target_pairs={{0,2},{1,15},{2,4},{3,1},{4,6},{5,3},{6,8},{7,5},{8,10},{9,7},{10,... | collective-permute-start | bytes 3145736 | tf_op jit(solution)/shard_map/ppermute | solution.py:363
  2.9 0.7 %pad_add_fusion.info_ref = s32[2]{0:T(128)} fusion(s32[1]{0:T(128)} %bitcast.1, s32[1]{0:T(128)} %bitcast), kind=kLoop, calls=%fused_computation.30 | loop fusion | flops 2 | bytes 16 | tf_op jit(solution)/shard_map/stack | solution.py:355
  3.6 3.4 %pack.1 = bf16[26,128,128]{2,1,0:T(8,128)(2,1)} custom-call(s32[2]{0:T(128)} %pad_add_fusion.info_ref, s32[8,32]{1,0:T(8,128)} %bitcast.5, bf16[4,8,128,128]{3,2,1,0:T(8,128)(2,1)} %tiles_ref.3), custom_call_target="tpu_custom_call" | custom-call | tf_op jit(solution)/shard_map/pack/pallas_call | solution.py:325
  7.0 1.6 %collective-permute-start.3 = (bf16[26,128,128]{2,1,0:T(8,128)(2,1)}, bf16[26,128,128]{2,1,0:T(8,128)(2,1)S(1)}, u32[]{:S(2)}, u32[]{:S(2)}) collective-permute-start(bf16[26,128,128]{2,1,0:T(8,128)(2,1)} %pack.1), channel_id=1, source_target_pairs={{0,4},{1,13},{2,6},{3,15},{4,8},{5,1},{6,10},{7,3},{8,12},{9,5},{1... | collective-permute-start | bytes 2555912 | tf_op jit(solution)/shard_map/ppermute | solution.py:363
  8.6 0.0 copy-done.1
  8.6 0.1 copy.5
  8.7 0.6 %gather_fusion = s32[16,8]{1,0:T(8,128)S(1)} fusion(s32[32,8]{1,0:T(8,128)S(1)} %copy.5, s32[1024]{0:T(1024)S(1)} %pad_clamp_fusion), kind=kCustom, calls=%fused_computation | custom fusion | bytes 1088 | tf_op jit(solution)/shard_map/jit(_take)/gather | solution.py:376
  9.3 0.1 and_select_fusion
  9.4 0.1 add.122
  9.5 0.1 lt.68
  9.6 0.1 select_reduce_fusion
  9.7 0.1 reshape.118
  9.8 0.1 fusion
  9.9 0.1 reshape.119
  10.0 0.1 concatenate.4.table_ref
  10.1 0.0 copy-done
  10.1 0.9 %own_rows.1.own_ref = bf16[512,1664]{1,0:T(8,128)(2,1)S(1)} custom-call(s32[450]{0:T(512)S(1)} %concatenate.4.table_ref, bf16[4,8,128,128]{3,2,1,0:T(8,128)(2,1)S(1)} %copy-done), custom_call_target="tpu_custom_call" | custom-call | tf_op jit(solution)/shard_map/own_rows/pallas_call | solution.py:325
  11.0 15.7 %collective-permute-done.near_ref = bf16[4,8,128,128]{3,2,1,0:T(8,128)(2,1)S(1)} collective-permute-done((bf16[4,8,128,128]{3,2,1,0:T(8,128)(2,1)}, bf16[4,8,128,128]{3,2,1,0:T(8,128)(2,1)S(1)}, u32[]{:S(2)}, u32[]{:S(2)}) %collective-permute-start) | collective-permute-done | bytes 1048608 | tf_op jit(solution)/shard_map/ppermute | solution.py:363
  26.7 0.1 fusion.6
  26.8 0.1 collective-permute-start.2
  26.9 0.5 %collective-permute-start.1 = (bf16[2,8,128,128]{3,2,1,0:T(8,128)(2,1)S(1)}, bf16[2,8,128,128]{3,2,1,0:T(8,128)(2,1)S(1)}, u32[]{:S(2)}, u32[]{:S(2)}) collective-permute-start(bf16[2,8,128,128]{3,2,1,0:T(8,128)(2,1)S(1)} %get-tuple-element.35), channel_id=1, source_target_pairs={{0,1},{1,0},{2,3},{3,2},{4,5},{5,4},{6,7},{7,6},{8,9},{9,8},{10,11... | collective-permute-start | bytes 1572872 | tf_op jit(solution)/shard_map/ppermute | solution.py:366
  27.4 2.3 %low_first.1 = (bf16[512,1664]{1,0:T(8,128)(2,1)S(1)}, bf16[512,512]{1,0:T(8,128)(2,1)S(1)}, f32[7,256,256]{2,1,0:T(8,128)S(1)}, f32[7,256,256]{2,1,0:T(8,128)S(1)}) custom-call(s32[450]{0:T(512)S(1)} %concatenate.4.table_ref, bf16[4,8,128,128]{3,2,1,0:T(8,128)(2,1)S(1)} %collective-permute-done.near_ref, bf16[512,1664]{1,0:T(8,128)(2,1)S(1)} %own_rows.1.own_ref), custom_call_target="tpu_custom_call" | custom-call | tf_op jit(solution)/shard_map/low_first/pallas_call | solution.py:325
  29.7 0.0 collective-permute-done.2.other1_ref
  29.7 0.0 collective-permute-done.1.other0_ref
  29.7 4.3 %own.1 = (bf16[512,1536]{1,0:T(8,128)(2,1)S(1)}, f32[10,256,256]{2,1,0:T(8,128)S(1)}) custom-call(s32[450]{0:T(512)S(1)} %concatenate.4.table_ref, bf16[512,1664]{1,0:T(8,128)(2,1)S(1)} %get-tuple-element.24.low_ref, bf16[512,1664]{1,0:T(8,128)(2,1)S(1)} %own_rows.1.own_ref, bf16[2,8,128,128]{3,2,1,0:T(8,128)(2,1)S(1)} %collective-permute-done.1.other0_ref, ...), custom_call_target="tpu_custom_call" | custom-call | tf_op jit(solution)/shard_map/own/pallas_call | solution.py:325
  34.0 0.0 collective-permute-done.3.far_ref
  34.0 1.7 %low_second.1.sent_ref = bf16[26,128,128]{2,1,0:T(8,128)(2,1)S(1)} custom-call(s32[450]{0:T(512)S(1)} %concatenate.4.table_ref, bf16[26,128,128]{2,1,0:T(8,128)(2,1)S(1)} %collective-permute-done.3.far_ref, bf16[512,1664]{1,0:T(8,128)(2,1)S(1)} %get-tuple-element.24.low_ref, bf16[512,512]{1,0:T(8,128)(2,1)S(1)} %get-tuple-element.25.ready_ref, ...), custom_call_target="tpu_custom_call" | custom-call | tf_op jit(solution)/shard_map/low_second/pallas_call | solution.py:325
  35.8 1.9 %collective-permute-start.4 = (bf16[26,128,128]{2,1,0:T(8,128)(2,1)S(1)}, bf16[26,128,128]{2,1,0:T(8,128)(2,1)S(1)}, u32[]{:S(2)}, u32[]{:S(2)}) collective-permute-start(bf16[26,128,128]{2,1,0:T(8,128)(2,1)S(1)} %low_second.1.sent_ref), channel_id=1, source_target_pairs={{0,1},{1,0},{2,3},{3,2},{4,5},{5,4},{6,7},{7,6},{8,9},{9,8},{10,11... | collective-permute-start | bytes 2555912 | tf_op jit(solution)/shard_map/ppermute | solution.py:366
  37.6 1.5 %last_first.1 = (bf16[512,512]{1,0:T(8,128)(2,1)S(1)}, f32[4,256,256]{2,1,0:T(8,128)S(1)}, f32[7,256,256]{2,1,0:T(8,128)S(1)}) custom-call(s32[450]{0:T(512)S(1)} %concatenate.4.table_ref, bf16[26,128,128]{2,1,0:T(8,128)(2,1)S(1)} %low_second.1.sent_ref, bf16[512,1536]{1,0:T(8,128)(2,1)S(1)} %get-tuple-element.22.own_ref, ...), custom_call_target="tpu_custom_call" | custom-call | tf_op jit(solution)/shard_map/last_first/pallas_call | solution.py:325
  39.1 0.5 %collective-permute-done.4.other_ref = bf16[26,128,128]{2,1,0:T(8,128)(2,1)S(1)} collective-permute-done((bf16[26,128,128]{2,1,0:T(8,128)(2,1)S(1)}, bf16[26,128,128]{2,1,0:T(8,128)(2,1)S(1)}, u32[]{:S(2)}, u32[]{:S(2)}) %collective-permute-start.4) | collective-permute-done | bytes 852000 | tf_op jit(solution)/shard_map/ppermute | solution.py:366
  39.6 2.8 %last_second.1 = bf16[4,8,128,128]{3,2,1,0:T(8,128)(2,1)} custom-call(s32[450]{0:T(512)S(1)} %concatenate.4.table_ref, bf16[512,1536]{1,0:T(8,128)(2,1)S(1)} %get-tuple-element.22.own_ref, f32[10,256,256]{2,1,0:T(8,128)S(1)} %get-tuple-element.23.begun_ref, bf16[26,128,128]{2,1,0:T(8,128)(2,1)S(1)} %collective-permute-done.4.other_ref, ...), custom_call_target="tpu_custom_call" | custom-call | tf_op jit(solution)/shard_map/last_second/pallas_call | solution.py:325
  (6 shorter events, 0.1 us)
Async XLA Ops:
  0.0 10.1 %copy-start = (bf16[4,8,128,128]{3,2,1,0:T(8,128)(2,1)S(1)}, bf16[4,8,128,128]{3,2,1,0:T(8,128)(2,1)}, u32[]{:S(2)}) copy-start(bf16[4,8,128,128]{3,2,1,0:T(8,128)(2,1)} %tiles_ref.3) | copy-start | bytes 3145732
  0.0 8.6 %copy-start.1 = (s32[32,8]{0,1:T(8,128)S(1)}, s32[32,8]{0,1:T(8,128)}, u32[]{:S(2)}) copy-start(s32[32,8]{0,1:T(8,128)} %param.2) | copy-start | bytes 3076
  0.0 26.7 %collective-permute-start = (bf16[4,8,128,128]{3,2,1,0:T(8,128)(2,1)}, bf16[4,8,128,128]{3,2,1,0:T(8,128)(2,1)S(1)}, u32[]{:S(2)}, u32[]{:S(2)}) collective-permute-start(bf16[4,8,128,128]{3,2,1,0:T(8,128)(2,1)} %tiles_ref.3), channel_id=1, source_target_pairs={{0,2},{1,15},{2,4},{3,1},{4,6},{5,3},{6,8},{7,5},{8,10},{9,7},{10,... | collective-permute-start | bytes 3145736 | tf_op jit(solution)/shard_map/ppermute | solution.py:363
  7.0 27.0 %collective-permute-start.3 = (bf16[26,128,128]{2,1,0:T(8,128)(2,1)}, bf16[26,128,128]{2,1,0:T(8,128)(2,1)S(1)}, u32[]{:S(2)}, u32[]{:S(2)}) collective-permute-start(bf16[26,128,128]{2,1,0:T(8,128)(2,1)} %pack.1), channel_id=1, source_target_pairs={{0,4},{1,13},{2,6},{3,15},{4,8},{5,1},{6,10},{7,3},{8,12},{9,5},{1... | collective-permute-start | bytes 2555912 | tf_op jit(solution)/shard_map/ppermute | solution.py:363
  26.8 2.9 %collective-permute-start.2 = (bf16[2,8,128,128]{3,2,1,0:T(8,128)(2,1)S(1)}, bf16[2,8,128,128]{3,2,1,0:T(8,128)(2,1)S(1)}, u32[]{:S(2)}, u32[]{:S(2)}) collective-permute-start(bf16[2,8,128,128]{3,2,1,0:T(8,128)(2,1)S(1)} %get-tuple-element.34), channel_id=1, source_target_pairs={{0,1},{1,0},{2,3},{3,2},{4,5},{5,4},{6,7},{7,6},{8,9},{9,8},{10,11... | collective-permute-start | bytes 1572872 | tf_op jit(solution)/shard_map/ppermute | solution.py:366
  26.9 2.8 %collective-permute-start.1 = (bf16[2,8,128,128]{3,2,1,0:T(8,128)(2,1)S(1)}, bf16[2,8,128,128]{3,2,1,0:T(8,128)(2,1)S(1)}, u32[]{:S(2)}, u32[]{:S(2)}) collective-permute-start(bf16[2,8,128,128]{3,2,1,0:T(8,128)(2,1)S(1)} %get-tuple-element.35), channel_id=1, source_target_pairs={{0,1},{1,0},{2,3},{3,2},{4,5},{5,4},{6,7},{7,6},{8,9},{9,8},{10,11... | collective-permute-start | bytes 1572872 | tf_op jit(solution)/shard_map/ppermute | solution.py:366
  35.8 3.9 %collective-permute-start.4 = (bf16[26,128,128]{2,1,0:T(8,128)(2,1)S(1)}, bf16[26,128,128]{2,1,0:T(8,128)(2,1)S(1)}, u32[]{:S(2)}, u32[]{:S(2)}) collective-permute-start(bf16[26,128,128]{2,1,0:T(8,128)(2,1)S(1)} %low_second.1.sent_ref), channel_id=1, source_target_pairs={{0,1},{1,0},{2,3},{3,2},{4,5},{5,4},{6,7},{7,6},{8,9},{9,8},{10,11... | collective-permute-start | bytes 2555912 | tf_op jit(solution)/shard_map/ppermute | solution.py:366

commit v8 on v7

--- a/solution.py
+++ b/solution.py
@@ -188,7 +188,7 @@
         for (p, c), i in cubes.items():
             cube_part[i] = product(square, right, p, c, self.done(p, c))
 
-    def second(self, left, right, square, ready, mask_ref, square_part, cube_part, write, begun=None):
+    def second(self, left, right, square, ready, mask_ref, square_part, cube_part, write, begun=None, masked=True):
         squares, cubes = self.open()
         late = [(p, c) for p, c in self.places() if not self.whole(p, c)]
         for i, (p, c) in enumerate(self.places()):
@@ -203,7 +203,7 @@
                 if (p, c) in cubes:
                     cube = cube_part[cubes[p, c]] if cube is None else cube_part[cubes[p, c]] + cube
                 own = (square if (p, c) in late else ready)[p, c].astype(jnp.float32)
-                write(p, c, (3.0 * own - 2.0 * kept(cube, mask_ref, p, c)).astype(jnp.bfloat16))
+                write(p, c, (3.0 * own - 2.0 * (kept(cube, mask_ref, p, c) if masked else cube)).astype(jnp.bfloat16))
 
     def all(self, left, right, square, mask_ref, write):
         for p in self.pairs:
@@ -315,7 +315,7 @@
 
     LAST.second(
         own, {4: own, 5: own, 6: high, 7: high}, Dense(square_ref, 8, 4), Dense(ready_ref, 8, 4), mask_ref,
-        square_part, cube_part, write, begun_ref,
+        square_part, cube_part, write, begun_ref, masked=False,
     )
     pltpu.make_async_copy(out_ref, out_ref, sem).wait()
 

time: 42.6 us -> 42.7 us (level)
  no operation moved by 1% of the time
where the time goes in v8:
time: 42.7 us; the launch traced here: 42.4 us
  Pallas kernels  16.9 us (40%)
  waiting for transfers between devices  16.2 us (38%)
  starting transfers between devices  7.03 us (16%)
  local copies, waits for them, and re-layouts  1.16 us (3%)
  other arithmetic  0.99 us (2%)
    pallas_call x7, Pallas kernels, call(): pl.pallas_call(kernel, out_shape=outs, in_specs=[smem] * len(scalars) + [...  16.9 us
    ppermute x2, waiting for transfers between devices, shifted(): return lax.ppermute(value, axes, pairs)  15.7 us
    ppermute x2, starting transfers between devices, shifted(): return lax.ppermute(value, axes, pairs)  4.58 us
    ppermute x3, starting transfers between devices, swapped(): return lax.ppermute(value, 'layer', [(0, 1), (1, 0)])  2.45 us
  transfers between devices with their start and end apart: 5, of which 2 were waited for; matrix products, arithmetic and copies ran while one was open for 5% of the time, Pallas kernels for 29%

profile of v8, /device:TPU:0, one launch (start us, length us, event | category | flops | bytes accessed | tf_op | source)
XLA Modules:
  0.0 42.4 jit_solution(2152431283725668732)
XLA Ops:
  0.0 0.0 copy-start
  0.0 0.0 copy-start.1
  0.0 2.9 %collective-permute-start = (bf16[4,8,128,128]{3,2,1,0:T(8,128)(2,1)}, bf16[4,8,128,128]{3,2,1,0:T(8,128)(2,1)S(1)}, u32[]{:S(2)}, u32[]{:S(2)}) collective-permute-start(bf16[4,8,128,128]{3,2,1,0:T(8,128)(2,1)} %tiles_ref.3), channel_id=1, source_target_pairs={{0,2},{1,15},{2,4},{3,1},{4,6},{5,3},{6,8},{7,5},{8,10},{9,7},{10,... | collective-permute-start | bytes 3145736 | tf_op jit(solution)/shard_map/ppermute | solution.py:363
  2.9 0.7 %pad_add_fusion.info_ref = s32[2]{0:T(128)} fusion(s32[1]{0:T(128)} %bitcast.1, s32[1]{0:T(128)} %bitcast), kind=kLoop, calls=%fused_computation.30 | loop fusion | flops 2 | bytes 16 | tf_op jit(solution)/shard_map/stack | solution.py:355
  3.6 3.4 %pack.1 = bf16[26,128,128]{2,1,0:T(8,128)(2,1)} custom-call(s32[2]{0:T(128)} %pad_add_fusion.info_ref, s32[8,32]{1,0:T(8,128)} %bitcast.5, bf16[4,8,128,128]{3,2,1,0:T(8,128)(2,1)} %tiles_ref.3), custom_call_target="tpu_custom_call" | custom-call | tf_op jit(solution)/shard_map/pack/pallas_call | solution.py:325
  7.0 1.6 %collective-permute-start.3 = (bf16[26,128,128]{2,1,0:T(8,128)(2,1)}, bf16[26,128,128]{2,1,0:T(8,128)(2,1)S(1)}, u32[]{:S(2)}, u32[]{:S(2)}) collective-permute-start(bf16[26,128,128]{2,1,0:T(8,128)(2,1)} %pack.1), channel_id=1, source_target_pairs={{0,4},{1,13},{2,6},{3,15},{4,8},{5,1},{6,10},{7,3},{8,12},{9,5},{1... | collective-permute-start | bytes 2555912 | tf_op jit(solution)/shard_map/ppermute | solution.py:363
  8.6 0.0 copy-done.1
  8.6 0.1 copy.5
  8.7 0.6 %gather_fusion = s32[16,8]{1,0:T(8,128)S(1)} fusion(s32[32,8]{1,0:T(8,128)S(1)} %copy.5, s32[1024]{0:T(1024)S(1)} %pad_clamp_fusion), kind=kCustom, calls=%fused_computation | custom fusion | bytes 1088 | tf_op jit(solution)/shard_map/jit(_take)/gather | solution.py:376
  9.3 0.1 and_select_fusion
  9.4 0.1 add.122
  9.5 0.1 lt.68
  9.6 0.1 select_reduce_fusion
  9.7 0.1 reshape.118
  9.8 0.1 fusion
  9.9 0.1 reshape.119
  10.0 0.1 concatenate.4.table_ref
  10.1 0.0 copy-done
  10.1 0.9 %own_rows.1.own_ref = bf16[512,1664]{1,0:T(8,128)(2,1)S(1)} custom-call(s32[450]{0:T(512)S(1)} %concatenate.4.table_ref, bf16[4,8,128,128]{3,2,1,0:T(8,128)(2,1)S(1)} %copy-done), custom_call_target="tpu_custom_call" | custom-call | tf_op jit(solution)/shard_map/own_rows/pallas_call | solution.py:325
  11.0 15.7 %collective-permute-done.near_ref = bf16[4,8,128,128]{3,2,1,0:T(8,128)(2,1)S(1)} collective-permute-done((bf16[4,8,128,128]{3,2,1,0:T(8,128)(2,1)}, bf16[4,8,128,128]{3,2,1,0:T(8,128)(2,1)S(1)}, u32[]{:S(2)}, u32[]{:S(2)}) %collective-permute-start) | collective-permute-done | bytes 1048608 | tf_op jit(solution)/shard_map/ppermute | solution.py:363
  26.7 0.1 fusion.6
  26.8 0.1 collective-permute-start.2
  26.9 0.5 %collective-permute-start.1 = (bf16[2,8,128,128]{3,2,1,0:T(8,128)(2,1)S(1)}, bf16[2,8,128,128]{3,2,1,0:T(8,128)(2,1)S(1)}, u32[]{:S(2)}, u32[]{:S(2)}) collective-permute-start(bf16[2,8,128,128]{3,2,1,0:T(8,128)(2,1)S(1)} %get-tuple-element.35), channel_id=1, source_target_pairs={{0,1},{1,0},{2,3},{3,2},{4,5},{5,4},{6,7},{7,6},{8,9},{9,8},{10,11... | collective-permute-start | bytes 1572872 | tf_op jit(solution)/shard_map/ppermute | solution.py:366
  27.4 2.3 %low_first.1 = (bf16[512,1664]{1,0:T(8,128)(2,1)S(1)}, bf16[512,512]{1,0:T(8,128)(2,1)S(1)}, f32[7,256,256]{2,1,0:T(8,128)S(1)}, f32[7,256,256]{2,1,0:T(8,128)S(1)}) custom-call(s32[450]{0:T(512)S(1)} %concatenate.4.table_ref, bf16[4,8,128,128]{3,2,1,0:T(8,128)(2,1)S(1)} %collective-permute-done.near_ref, bf16[512,1664]{1,0:T(8,128)(2,1)S(1)} %own_rows.1.own_ref), custom_call_target="tpu_custom_call" | custom-call | tf_op jit(solution)/shard_map/low_first/pallas_call | solution.py:325
  29.7 0.0 collective-permute-done.2.other1_ref
  29.7 0.0 collective-permute-done.1.other0_ref
  29.7 4.3 %own.1 = (bf16[512,1536]{1,0:T(8,128)(2,1)S(1)}, f32[10,256,256]{2,1,0:T(8,128)S(1)}) custom-call(s32[450]{0:T(512)S(1)} %concatenate.4.table_ref, bf16[512,1664]{1,0:T(8,128)(2,1)S(1)} %get-tuple-element.24.low_ref, bf16[512,1664]{1,0:T(8,128)(2,1)S(1)} %own_rows.1.own_ref, bf16[2,8,128,128]{3,2,1,0:T(8,128)(2,1)S(1)} %collective-permute-done.1.other0_ref, ...), custom_call_target="tpu_custom_call" | custom-call | tf_op jit(solution)/shard_map/own/pallas_call | solution.py:325
  34.0 0.0 collective-permute-done.3.far_ref
  34.0 1.7 %low_second.1.sent_ref = bf16[26,128,128]{2,1,0:T(8,128)(2,1)S(1)} custom-call(s32[450]{0:T(512)S(1)} %concatenate.4.table_ref, bf16[26,128,128]{2,1,0:T(8,128)(2,1)S(1)} %collective-permute-done.3.far_ref, bf16[512,1664]{1,0:T(8,128)(2,1)S(1)} %get-tuple-element.24.low_ref, bf16[512,512]{1,0:T(8,128)(2,1)S(1)} %get-tuple-element.25.ready_ref, ...), custom_call_target="tpu_custom_call" | custom-call | tf_op jit(solution)/shard_map/low_second/pallas_call | solution.py:325
  35.7 1.9 %collective-permute-start.4 = (bf16[26,128,128]{2,1,0:T(8,128)(2,1)S(1)}, bf16[26,128,128]{2,1,0:T(8,128)(2,1)S(1)}, u32[]{:S(2)}, u32[]{:S(2)}) collective-permute-start(bf16[26,128,128]{2,1,0:T(8,128)(2,1)S(1)} %low_second.1.sent_ref), channel_id=1, source_target_pairs={{0,1},{1,0},{2,3},{3,2},{4,5},{5,4},{6,7},{7,6},{8,9},{9,8},{10,11... | collective-permute-start | bytes 2555912 | tf_op jit(solution)/shard_map/ppermute | solution.py:366
  37.6 1.5 %last_first.1 = (bf16[512,512]{1,0:T(8,128)(2,1)S(1)}, f32[4,256,256]{2,1,0:T(8,128)S(1)}, f32[7,256,256]{2,1,0:T(8,128)S(1)}) custom-call(s32[450]{0:T(512)S(1)} %concatenate.4.table_ref, bf16[26,128,128]{2,1,0:T(8,128)(2,1)S(1)} %low_second.1.sent_ref, bf16[512,1536]{1,0:T(8,128)(2,1)S(1)} %get-tuple-element.22.own_ref, ...), custom_call_target="tpu_custom_call" | custom-call | tf_op jit(solution)/shard_map/last_first/pallas_call | solution.py:325
  39.1 0.5 %collective-permute-done.4.other_ref = bf16[26,128,128]{2,1,0:T(8,128)(2,1)S(1)} collective-permute-done((bf16[26,128,128]{2,1,0:T(8,128)(2,1)S(1)}, bf16[26,128,128]{2,1,0:T(8,128)(2,1)S(1)}, u32[]{:S(2)}, u32[]{:S(2)}) %collective-permute-start.4) | collective-permute-done | bytes 852000 | tf_op jit(solution)/shard_map/ppermute | solution.py:366
  39.6 2.8 %last_second.1 = bf16[4,8,128,128]{3,2,1,0:T(8,128)(2,1)} custom-call(s32[450]{0:T(512)S(1)} %concatenate.4.table_ref, bf16[512,1536]{1,0:T(8,128)(2,1)S(1)} %get-tuple-element.22.own_ref, f32[10,256,256]{2,1,0:T(8,128)S(1)} %get-tuple-element.23.begun_ref, bf16[26,128,128]{2,1,0:T(8,128)(2,1)S(1)} %collective-permute-done.4.other_ref, ...), custom_call_target="tpu_custom_call" | custom-call | tf_op jit(solution)/shard_map/last_second/pallas_call | solution.py:325
  (6 shorter events, 0.1 us)
Async XLA Ops:
  0.0 10.1 %copy-start = (bf16[4,8,128,128]{3,2,1,0:T(8,128)(2,1)S(1)}, bf16[4,8,128,128]{3,2,1,0:T(8,128)(2,1)}, u32[]{:S(2)}) copy-start(bf16[4,8,128,128]{3,2,1,0:T(8,128)(2,1)} %tiles_ref.3) | copy-start | bytes 3145732
  0.0 8.6 %copy-start.1 = (s32[32,8]{0,1:T(8,128)S(1)}, s32[32,8]{0,1:T(8,128)}, u32[]{:S(2)}) copy-start(s32[32,8]{0,1:T(8,128)} %param.2) | copy-start | bytes 3076
  0.0 26.7 %collective-permute-start = (bf16[4,8,128,128]{3,2,1,0:T(8,128)(2,1)}, bf16[4,8,128,128]{3,2,1,0:T(8,128)(2,1)S(1)}, u32[]{:S(2)}, u32[]{:S(2)}) collective-permute-start(bf16[4,8,128,128]{3,2,1,0:T(8,128)(2,1)} %tiles_ref.3), channel_id=1, source_target_pairs={{0,2},{1,15},{2,4},{3,1},{4,6},{5,3},{6,8},{7,5},{8,10},{9,7},{10,... | collective-permute-start | bytes 3145736 | tf_op jit(solution)/shard_map/ppermute | solution.py:363
  7.0 27.0 %collective-permute-start.3 = (bf16[26,128,128]{2,1,0:T(8,128)(2,1)}, bf16[26,128,128]{2,1,0:T(8,128)(2,1)S(1)}, u32[]{:S(2)}, u32[]{:S(2)}) collective-permute-start(bf16[26,128,128]{2,1,0:T(8,128)(2,1)} %pack.1), channel_id=1, source_target_pairs={{0,4},{1,13},{2,6},{3,15},{4,8},{5,1},{6,10},{7,3},{8,12},{9,5},{1... | collective-permute-start | bytes 2555912 | tf_op jit(solution)/shard_map/ppermute | solution.py:363
  26.8 2.9 %collective-permute-start.2 = (bf16[2,8,128,128]{3,2,1,0:T(8,128)(2,1)S(1)}, bf16[2,8,128,128]{3,2,1,0:T(8,128)(2,1)S(1)}, u32[]{:S(2)}, u32[]{:S(2)}) collective-permute-start(bf16[2,8,128,128]{3,2,1,0:T(8,128)(2,1)S(1)} %get-tuple-element.34), channel_id=1, source_target_pairs={{0,1},{1,0},{2,3},{3,2},{4,5},{5,4},{6,7},{7,6},{8,9},{9,8},{10,11... | collective-permute-start | bytes 1572872 | tf_op jit(solution)/shard_map/ppermute | solution.py:366
  26.9 2.8 %collective-permute-start.1 = (bf16[2,8,128,128]{3,2,1,0:T(8,128)(2,1)S(1)}, bf16[2,8,128,128]{3,2,1,0:T(8,128)(2,1)S(1)}, u32[]{:S(2)}, u32[]{:S(2)}) collective-permute-start(bf16[2,8,128,128]{3,2,1,0:T(8,128)(2,1)S(1)} %get-tuple-element.35), channel_id=1, source_target_pairs={{0,1},{1,0},{2,3},{3,2},{4,5},{5,4},{6,7},{7,6},{8,9},{9,8},{10,11... | collective-permute-start | bytes 1572872 | tf_op jit(solution)/shard_map/ppermute | solution.py:366
  35.7 3.9 %collective-permute-start.4 = (bf16[26,128,128]{2,1,0:T(8,128)(2,1)S(1)}, bf16[26,128,128]{2,1,0:T(8,128)(2,1)S(1)}, u32[]{:S(2)}, u32[]{:S(2)}) collective-permute-start(bf16[26,128,128]{2,1,0:T(8,128)(2,1)S(1)} %low_second.1.sent_ref), channel_id=1, source_target_pairs={{0,1},{1,0},{2,3},{3,2},{4,5},{5,4},{6,7},{7,6},{8,9},{9,8},{10,11... | collective-permute-start | bytes 2555912 | tf_op jit(solution)/shard_map/ppermute | solution.py:366
